TPU v7x, 32 devices: a whole 2x2x4 slice. The times are simulated.
32 devices in a mesh: clip: 4 (over y, core), seq: 8 (over z, x).
Axes of the slice: x: 2, y: 2, z: 4, core: 2. Of those that a mesh axis runs over, the one named last changes fastest.
Arguments:
- tokens: bfloat16 [4, 1024, 1536], P('clip', 'seq'), may hold values from -6 to 6
- caption: bfloat16 [4, 128, 4096], P('clip', 'seq'), may hold values from -6 to 6
- condition: bfloat16 [4, 1024], P('clip'), may hold values from -6 to 6
- caption_len: int32 [4], P('clip'), may hold values from 32 to 128, as said below
- frame_shape: int32 [4, 3], P('clip'), may hold values from 2 to 32, as said below
- rope_shift: int32 [4, 3], P('clip'), may hold values from 0 to 64
- w_modulation: bfloat16 [1024, 6144], P(('clip', 'seq')), may hold values from -0.1875 to 0.1875
- mod_bias: bfloat16 [6144], P(('clip', 'seq')), may hold values from -3 to 3
- w_attention: bfloat16 [1536, 4608], P(('clip', 'seq')), may hold values from -0.15625 to 0.15625
- w_output: bfloat16 [1536, 1536], P(('clip', 'seq')), may hold values from -0.15625 to 0.15625
- w_caption: bfloat16 [4096, 3072], P(('clip', 'seq')), may hold values from -0.09375 to 0.09375
- norm_gains: bfloat16 [7, 1536], P(None, ('clip', 'seq')), may hold values from 0.099609375 to 1.8984375
- head_gate: bfloat16 [24], replicated, may hold values from -1.5 to 1.5
- w_gateup: bfloat16 [1536, 8192], P(('clip', 'seq')), may hold values from -0.15625 to 0.15625
- w_down: bfloat16 [4096, 1536], P(('clip', 'seq')), may hold values from -0.09375 to 0.09375
- cotangent: bfloat16 [4, 1024, 1536], P('clip', 'seq'), may hold values from -6 to 6
Outputs:
- block_out: float32 [4, 1024, 1536], P('clip', 'seq')
- grad_tokens: float32 [4, 1024, 1536], P('clip', 'seq')
- grad_caption: float32 [4, 128, 4096], P('clip', 'seq')
- grad_condition: float32 [4, 1024], P('clip')
- grad_w_modulation: float32 [1024, 6144], P(('clip', 'seq'))
- grad_mod_bias: float32 [6144], P(('clip', 'seq'))
- grad_w_attention: float32 [1536, 4608], P(('clip', 'seq'))
- grad_w_output: float32 [1536, 1536], P(('clip', 'seq'))
- grad_w_caption: float32 [4096, 3072], P(('clip', 'seq'))
- grad_norm_gains: float32 [7, 1536], P(None, ('clip', 'seq'))
- grad_head_gate: float32 [24], replicated
- grad_w_gateup: float32 [1536, 8192], P(('clip', 'seq'))
- grad_w_down: float32 [4096, 1536], P(('clip', 'seq'))
Inputs may be any that keep to these rules, and one draw needn't show every extreme that they name: `caption_len`: one clip, which one drawn from the seed, uses all 128 caption tokens; every other clip uses fewer. `frame_shape`: per clip (frames, height, width): width + 1 is 8, 16 or 32, height is 4 to 16, and frames is the least number with frames * height * (width + 1) >= 1024; the first clip has width 7 and height 4, the second width 31 and height 16.
All inputs are finite; a program needn't handle non-finite values.
Results may differ from a plain program's by a relative error of at most 0.023.
Values may be sent and summed in bfloat16 or wider, within the bound.
No kernel may reach another device: no remote copies, remote signals or barrier semaphores. Data moves between devices by JAX's collectives and lax.ppermute only.
A program may use at most 448 MiB of HBM per device.

v0:
```python
import math

import jax
import jax.numpy as jnp
from jax import lax
from jax.sharding import PartitionSpec as P

epsilon = 1e-06
theta_base = 10000.0
highest = lax.Precision.HIGHEST


def rms_norm(value):
    return value * lax.rsqrt(jnp.mean(value * value, axis=-1, keepdims=True) + epsilon)


def rms_back(value, upstream):
    return jax.vjp(rms_norm, value)[1](upstream)[0]


def rope_angles(shape_row, shift_row, position, half_dim):
    across = shape_row[2] + 1
    column_place = position % across + shift_row[2]
    row_place = position // across % shape_row[1] + shift_row[1]
    frame_place = position // (across * shape_row[1]) + shift_row[0]
    frame_count = half_dim // 4
    row_count = 3 * half_dim // 8
    column_count = half_dim - frame_count - row_count
    pieces = []
    for place_index, group_size in (
        (frame_place, frame_count),
        (row_place, row_count),
        (column_place, column_count),
    ):
        frequency = theta_base ** (-jnp.arange(group_size, dtype=jnp.float32) / group_size)
        pieces.append(place_index.astype(jnp.float32)[:, None] * frequency[None, :])
    return jnp.concatenate(pieces, axis=1)


def rotate(value, cosine, sine_table):
    half_dim = value.shape[-1] // 2
    front_half = value[..., :half_dim]
    back_half = value[..., half_dim:]
    return jnp.concatenate(
        [
            front_half * cosine - back_half * sine_table,
            back_half * cosine + front_half * sine_table,
        ],
        axis=-1,
    )


def soft_weights(scores):
    shifted = jnp.exp(scores - jnp.max(scores, axis=-1, keepdims=True))
    return shifted / jnp.sum(shifted, axis=-1, keepdims=True)


def local(
    tokens,
    caption,
    condition,
    caption_len,
    frame_shape,
    rope_shift,
    w_modulation,
    mod_bias,
    w_attention,
    w_output,
    w_caption,
    norm_gains,
    head_gate,
    w_gateup,
    w_down,
    cotangent,
):
    clip_count, local_len, model_width = tokens.shape
    head_count = head_gate.shape[0]
    head_dim = model_width // head_count
    score_scale = head_dim ** (-0.5)
    row_total = clip_count * local_len
    text_local = caption.shape[1]
    text_total = text_local * lax.axis_size("seq")
    gathered = (
        lax.all_gather(w_modulation, ("clip", "seq"), axis=0, tiled=True),
        lax.all_gather(mod_bias, ("clip", "seq"), axis=0, tiled=True),
        lax.all_gather(w_attention, ("clip", "seq"), axis=0, tiled=True),
        lax.all_gather(w_output, ("clip", "seq"), axis=0, tiled=True),
        lax.all_gather(w_caption, ("clip", "seq"), axis=0, tiled=True),
        lax.all_gather(norm_gains, ("clip", "seq"), axis=1, tiled=True),
    )
    full_mod, full_bias, full_attn, full_out, full_caption, full_gains = gathered
    gain_rows = full_gains.astype(jnp.float32)
    tanh_gate = jnp.tanh(head_gate.astype(jnp.float32))
    cond_float = condition.astype(jnp.float32)
    cond_act = jax.nn.silu(cond_float).astype(jnp.bfloat16)
    modulation = jnp.dot(cond_act, full_mod, preferred_element_type=jnp.float32) + full_bias.astype(
        jnp.float32
    )
    scale_attn = modulation[:, None, :model_width]
    gate_attn = jnp.tanh(modulation[:, None, model_width : 2 * model_width])
    scale_ffn = modulation[:, None, 2 * model_width : 3 * model_width]
    gate_ffn = jnp.tanh(modulation[:, None, 3 * model_width :])
    token_float = tokens.astype(jnp.float32)
    token_normed = rms_norm(token_float)
    normed_flat = (
        (token_normed * gain_rows[0] * (1.0 + scale_attn))
        .astype(jnp.bfloat16)
        .reshape(row_total, model_width)
    )
    projected = jnp.dot(normed_flat, full_attn, preferred_element_type=jnp.float32).reshape(
        clip_count, local_len, 3 * model_width
    )
    query_pre = projected[..., :model_width]
    key_pre = projected[..., model_width : 2 * model_width]
    query_normed = rms_norm(query_pre)
    key_normed = rms_norm(key_pre)
    position = lax.axis_index("seq") * local_len + jnp.arange(local_len, dtype=jnp.int32)
    angles = jax.vmap(
        lambda shape_row, shift_row: rope_angles(shape_row, shift_row, position, head_dim // 2)
    )(frame_shape, rope_shift)
    cosine = jnp.cos(angles)[:, :, None, :]
    sine_table = jnp.sin(angles)[:, :, None, :]
    split_shape = (clip_count, local_len, head_count, head_dim)
    queries = rotate((query_normed * gain_rows[4]).reshape(split_shape), cosine, sine_table).astype(
        jnp.bfloat16
    )
    key_rows = rotate((key_normed * gain_rows[5]).reshape(split_shape), cosine, sine_table).astype(
        jnp.bfloat16
    )
    value_rows = projected[..., 2 * model_width :].reshape(split_shape).astype(jnp.bfloat16)
    caption_flat = caption.reshape(clip_count * text_local, caption.shape[2])
    text_proj = jnp.dot(caption_flat, full_caption, preferred_element_type=jnp.float32).reshape(
        clip_count, text_local, 2 * model_width
    )
    text_key_pre = text_proj[..., :model_width]
    text_key_normed = rms_norm(text_key_pre)
    text_shape = (clip_count, text_local, head_count, head_dim)
    text_keys = (text_key_normed * gain_rows[6]).astype(jnp.bfloat16).reshape(text_shape)
    text_values = text_proj[..., model_width:].astype(jnp.bfloat16).reshape(text_shape)
    all_text_keys, all_text_values = (
        lax.all_gather(text_keys, "seq", axis=1, tiled=True),
        lax.all_gather(text_values, "seq", axis=1, tiled=True),
    )
    stat_shape = (clip_count, head_count, local_len)
    start_stats = (jnp.full(stat_shape, -1e30, jnp.float32), jnp.zeros(stat_shape, jnp.float32))
    piece_keys = lax.all_gather(key_rows, "seq", axis=1, tiled=True)
    key_count = piece_keys.shape[1]
    block_len = math.gcd(key_count, 512)

    def stat_one_block(block_index, inner_state):
        row_max, row_sum = inner_state
        block_keys = lax.dynamic_slice_in_dim(piece_keys, block_index * block_len, block_len, 1)
        scores = (
            jnp.einsum("cqhd,ckhd->chqk", queries, block_keys, preferred_element_type=jnp.float32)
            * score_scale
        )
        new_max = jnp.maximum(row_max, jnp.max(scores, axis=-1))
        row_sum = row_sum * jnp.exp(row_max - new_max) + jnp.sum(
            jnp.exp(scores - new_max[..., None]), axis=-1
        )
        return (new_max, row_sum)

    row_max, row_sum = lax.fori_loop(0, key_count // block_len, stat_one_block, start_stats)
    log_sum = row_max + jnp.log(row_sum)
    attend_piece_keys = lax.all_gather(key_rows, "seq", axis=1, tiled=True)
    piece_values = lax.all_gather(value_rows, "seq", axis=1, tiled=True)
    key_count = attend_piece_keys.shape[1]
    attend_block_len = math.gcd(key_count, 512)

    def attend_one_block(block_index, weighted):
        block_keys = lax.dynamic_slice_in_dim(
            attend_piece_keys, block_index * attend_block_len, attend_block_len, 1
        )
        block_values = lax.dynamic_slice_in_dim(
            piece_values, block_index * attend_block_len, attend_block_len, 1
        )
        scores = (
            jnp.einsum("cqhd,ckhd->chqk", queries, block_keys, preferred_element_type=jnp.float32)
            * score_scale
        )
        probs = jnp.exp(scores - log_sum[..., None]).astype(jnp.bfloat16)
        return weighted + jnp.einsum(
            "chqk,ckhd->chqd", probs, block_values, preferred_element_type=jnp.float32
        )

    weighted = lax.fori_loop(
        0,
        key_count // attend_block_len,
        attend_one_block,
        jnp.zeros(stat_shape + (head_dim,), jnp.float32),
    )
    self_out = jnp.transpose(weighted, (0, 2, 1, 3))
    usable = jnp.arange(text_total, dtype=jnp.int32)[None, :] < caption_len[:, None]
    text_scores = (
        jnp.einsum("cqhd,ckhd->chqk", queries, all_text_keys, preferred_element_type=jnp.float32)
        * score_scale
    )
    text_scores = jnp.where(usable[:, None, None, :], text_scores, -1e30)
    text_weights = soft_weights(text_scores)
    text_low = text_weights.astype(jnp.bfloat16)
    cross_out = jnp.einsum(
        "chqk,ckhd->cqhd", text_low, all_text_values, preferred_element_type=jnp.float32
    )
    mixed_heads = self_out + tanh_gate[None, None, :, None] * cross_out
    mixed_flat = mixed_heads.reshape(row_total, model_width).astype(jnp.bfloat16)
    attn_proj = jnp.dot(mixed_flat, full_out, preferred_element_type=jnp.float32).reshape(
        clip_count, local_len, model_width
    )
    attn_normed = rms_norm(attn_proj)
    residual = token_float + gate_attn * attn_normed * gain_rows[1]
    full_gateup, full_down = (
        lax.all_gather(w_gateup, ("clip", "seq"), axis=0, tiled=True),
        lax.all_gather(w_down, ("clip", "seq"), axis=0, tiled=True),
    )
    hidden_units = full_down.shape[0]
    residual_normed = rms_norm(residual)
    normed_ffn = (
        (residual_normed * gain_rows[2] * (1.0 + scale_ffn))
        .astype(jnp.bfloat16)
        .reshape(row_total, model_width)
    )
    gate_up = jnp.dot(normed_ffn, full_gateup, preferred_element_type=jnp.float32)
    gate_part = gate_up[:, :hidden_units]
    up_part = gate_up[:, hidden_units:]
    gate_sigmoid = jax.nn.sigmoid(gate_part)
    activated = (gate_part * gate_sigmoid * up_part).astype(jnp.bfloat16)
    down_proj = jnp.dot(activated, full_down, preferred_element_type=jnp.float32).reshape(
        clip_count, local_len, model_width
    )
    down_normed = rms_norm(down_proj)
    block_out = residual + gate_ffn * down_normed * gain_rows[3]
    upstream = cotangent.astype(jnp.float32)
    gain_three = jnp.sum(upstream * gate_ffn * down_normed, axis=(0, 1))
    grad_gate_ffn = jnp.sum(upstream * down_normed * gain_rows[3], axis=1) * (
        1.0 - gate_ffn[:, 0] * gate_ffn[:, 0]
    )
    grad_down = (
        rms_back(down_proj, upstream * gate_ffn * gain_rows[3])
        .astype(jnp.bfloat16)
        .reshape(row_total, model_width)
    )
    full_gateup, full_down = (
        lax.all_gather(w_gateup, ("clip", "seq"), axis=0, tiled=True),
        lax.all_gather(w_down, ("clip", "seq"), axis=0, tiled=True),
    )
    wgrad_down = jnp.dot(activated.T, grad_down, preferred_element_type=jnp.float32)
    grad_act = jnp.dot(grad_down, full_down.T, preferred_element_type=jnp.float32)
    grad_gate_part = grad_act * up_part * gate_sigmoid * (1.0 + gate_part * (1.0 - gate_sigmoid))
    grad_up_part = grad_act * gate_part * gate_sigmoid
    grad_gate_up = jnp.concatenate([grad_gate_part, grad_up_part], axis=1).astype(jnp.bfloat16)
    wgrad_gateup = jnp.dot(normed_ffn.T, grad_gate_up, preferred_element_type=jnp.float32)
    grad_normed_ffn = jnp.dot(
        grad_gate_up, full_gateup.T, preferred_element_type=jnp.float32
    ).reshape(clip_count, local_len, model_width)
    gain_two = jnp.sum(grad_normed_ffn * residual_normed * (1.0 + scale_ffn), axis=(0, 1))
    grad_scale_ffn = jnp.sum(grad_normed_ffn * residual_normed * gain_rows[2], axis=1)
    grad_residual = upstream + rms_back(
        residual, grad_normed_ffn * gain_rows[2] * (1.0 + scale_ffn)
    )
    gain_one = jnp.sum(grad_residual * gate_attn * attn_normed, axis=(0, 1))
    grad_gate_attn = jnp.sum(grad_residual * attn_normed * gain_rows[1], axis=1) * (
        1.0 - gate_attn[:, 0] * gate_attn[:, 0]
    )
    grad_attn = (
        rms_back(attn_proj, grad_residual * gate_attn * gain_rows[1])
        .astype(jnp.bfloat16)
        .reshape(row_total, model_width)
    )
    full_mod, full_attn, full_out, full_caption = (
        lax.all_gather(w_modulation, ("clip", "seq"), axis=0, tiled=True),
        lax.all_gather(w_attention, ("clip", "seq"), axis=0, tiled=True),
        lax.all_gather(w_output, ("clip", "seq"), axis=0, tiled=True),
        lax.all_gather(w_caption, ("clip", "seq"), axis=0, tiled=True),
    )
    wgrad_output = jnp.dot(mixed_flat.T, grad_attn, preferred_element_type=jnp.float32)
    grad_mixed = (
        jnp.dot(grad_attn, full_out.T, preferred_element_type=jnp.float32)
        .reshape(split_shape)
        .astype(jnp.bfloat16)
    )
    grad_float = grad_mixed.astype(jnp.float32)
    grad_head_gate = jnp.sum(grad_float * cross_out, axis=(0, 1, 3)) * (1.0 - tanh_gate * tanh_gate)
    delta_rows = jnp.sum(grad_float * self_out, axis=-1)
    delta_heads = jnp.transpose(delta_rows, (0, 2, 1))
    lse_rows = jnp.transpose(log_sum, (0, 2, 1))
    text_grad = (
        jnp.einsum(
            "cqhd,ckhd->chqk", grad_mixed, all_text_values, preferred_element_type=jnp.float32
        )
        * tanh_gate[None, :, None, None]
    )
    text_center = jnp.sum(text_weights * text_grad, axis=-1, keepdims=True)
    grad_text_scores = (text_weights * (text_grad - text_center)).astype(jnp.bfloat16)
    grad_queries = (
        jnp.einsum(
            "chqk,ckhd->cqhd", grad_text_scores, all_text_keys, preferred_element_type=jnp.float32
        )
        * score_scale
    )
    grad_text_keys = (
        jnp.einsum("chqk,cqhd->ckhd", grad_text_scores, queries, preferred_element_type=jnp.float32)
        * score_scale
    )
    grad_text_values = (
        jnp.einsum("chqk,cqhd->ckhd", text_low, grad_mixed, preferred_element_type=jnp.float32)
        * tanh_gate[None, None, :, None]
    )
    text_back_keys, text_back_values = (
        lax.psum_scatter(
            grad_text_keys.astype(jnp.bfloat16), "seq", scatter_dimension=1, tiled=True
        ).astype(jnp.float32),
        lax.psum_scatter(
            grad_text_values.astype(jnp.bfloat16), "seq", scatter_dimension=1, tiled=True
        ).astype(jnp.float32),
    )
    query_piece_keys = lax.all_gather(key_rows, "seq", axis=1, tiled=True)
    query_piece_values = lax.all_gather(value_rows, "seq", axis=1, tiled=True)
    key_count = query_piece_keys.shape[1]
    query_block_len = math.gcd(key_count, 512)

    def query_one_block(block_index, inner_state):
        block_keys = lax.dynamic_slice_in_dim(
            query_piece_keys, block_index * query_block_len, query_block_len, 1
        )
        block_values = lax.dynamic_slice_in_dim(
            query_piece_values, block_index * query_block_len, query_block_len, 1
        )
        scores = (
            jnp.einsum("cqhd,ckhd->chqk", queries, block_keys, preferred_element_type=jnp.float32)
            * score_scale
        )
        probs = jnp.exp(scores - log_sum[..., None])
        grad_probs = jnp.einsum(
            "cqhd,ckhd->chqk", grad_mixed, block_values, preferred_element_type=jnp.float32
        )
        grad_scores = (probs * (grad_probs - delta_heads[..., None])).astype(jnp.bfloat16)
        return (
            inner_state
            + jnp.einsum(
                "chqk,ckhd->cqhd", grad_scores, block_keys, preferred_element_type=jnp.float32
            )
            * score_scale
        )

    grad_self_queries = lax.fori_loop(
        0, key_count // query_block_len, query_one_block, jnp.zeros(split_shape, jnp.float32)
    )
    grad_queries = grad_queries + grad_self_queries
    zero_grads = (jnp.zeros(split_shape, jnp.float32), jnp.zeros(split_shape, jnp.float32))
    piece_queries = lax.all_gather(queries.astype(jnp.float32), "seq", axis=1, tiled=True).astype(
        jnp.bfloat16
    )
    piece_grads = lax.all_gather(grad_float, "seq", axis=1, tiled=True).astype(jnp.bfloat16)
    piece_lse = lax.all_gather(lse_rows, "seq", axis=1, tiled=True)
    piece_delta = lax.all_gather(delta_rows, "seq", axis=1, tiled=True)
    query_count = piece_queries.shape[1]
    key_block_len = math.gcd(query_count, 512)

    def key_one_block(block_index, inner_state):
        grad_key_acc, grad_value_acc = inner_state
        block_queries = lax.dynamic_slice_in_dim(
            piece_queries, block_index * key_block_len, key_block_len, 1
        )
        block_grads = lax.dynamic_slice_in_dim(
            piece_grads, block_index * key_block_len, key_block_len, 1
        )
        block_lse = jnp.transpose(
            lax.dynamic_slice_in_dim(piece_lse, block_index * key_block_len, key_block_len, 1),
            (0, 2, 1),
        )
        block_delta = jnp.transpose(
            lax.dynamic_slice_in_dim(piece_delta, block_index * key_block_len, key_block_len, 1),
            (0, 2, 1),
        )
        scores = (
            jnp.einsum(
                "cqhd,ckhd->chqk", block_queries, key_rows, preferred_element_type=jnp.float32
            )
            * score_scale
        )
        probs = jnp.exp(scores - block_lse[..., None])
        grad_value_acc = grad_value_acc + jnp.einsum(
            "chqk,cqhd->ckhd",
            probs.astype(jnp.bfloat16),
            block_grads,
            preferred_element_type=jnp.float32,
        )
        grad_probs = jnp.einsum(
            "cqhd,ckhd->chqk", block_grads, value_rows, preferred_element_type=jnp.float32
        )
        grad_scores = (probs * (grad_probs - block_delta[..., None])).astype(jnp.bfloat16)
        grad_key_acc = (
            grad_key_acc
            + jnp.einsum(
                "chqk,cqhd->ckhd", grad_scores, block_queries, preferred_element_type=jnp.float32
            )
            * score_scale
        )
        return (grad_key_acc, grad_value_acc)

    grad_keys, grad_values = lax.fori_loop(
        0, query_count // key_block_len, key_one_block, zero_grads
    )
    flat_shape = (clip_count, local_len, model_width)
    grad_query_rot = rotate(grad_queries, cosine, -sine_table).reshape(flat_shape)
    grad_key_rot = rotate(grad_keys, cosine, -sine_table).reshape(flat_shape)
    gain_four = jnp.sum(grad_query_rot * query_normed, axis=(0, 1))
    gain_five = jnp.sum(grad_key_rot * key_normed, axis=(0, 1))
    grad_query_pre = rms_back(query_pre, grad_query_rot * gain_rows[4])
    grad_key_pre = rms_back(key_pre, grad_key_rot * gain_rows[5])
    grad_projected = (
        jnp.concatenate([grad_query_pre, grad_key_pre, grad_values.reshape(flat_shape)], axis=-1)
        .astype(jnp.bfloat16)
        .reshape(row_total, 3 * model_width)
    )
    wgrad_attention = jnp.dot(normed_flat.T, grad_projected, preferred_element_type=jnp.float32)
    grad_normed = jnp.dot(grad_projected, full_attn.T, preferred_element_type=jnp.float32).reshape(
        flat_shape
    )
    gain_zero = jnp.sum(grad_normed * token_normed * (1.0 + scale_attn), axis=(0, 1))
    grad_scale_attn = jnp.sum(grad_normed * token_normed * gain_rows[0], axis=1)
    grad_tokens = grad_residual + rms_back(
        token_float, grad_normed * gain_rows[0] * (1.0 + scale_attn)
    )
    grad_text_key_rows = text_back_keys.reshape(clip_count, text_local, model_width)
    gain_six = jnp.sum(grad_text_key_rows * text_key_normed, axis=(0, 1))
    grad_text_pre = rms_back(text_key_pre, grad_text_key_rows * gain_rows[6])
    grad_text_proj = (
        jnp.concatenate(
            [grad_text_pre, text_back_values.reshape(clip_count, text_local, model_width)], axis=-1
        )
        .astype(jnp.bfloat16)
        .reshape(clip_count * text_local, 2 * model_width)
    )
    wgrad_caption = jnp.dot(caption_flat.T, grad_text_proj, preferred_element_type=jnp.float32)
    grad_caption = jnp.dot(
        grad_text_proj, full_caption.T, preferred_element_type=jnp.float32
    ).reshape(clip_count, text_local, caption.shape[2])
    grad_mod_row = jnp.concatenate(
        [grad_scale_attn, grad_gate_attn, grad_scale_ffn, grad_gate_ffn], axis=1
    )
    bias_grad = jnp.sum(grad_mod_row, axis=0)
    wgrad_modulation = jnp.dot(cond_act.astype(jnp.float32).T, grad_mod_row, precision=highest)
    cond_sigmoid = jax.nn.sigmoid(cond_float)
    grad_cond_act = jnp.dot(grad_mod_row, full_mod.astype(jnp.float32).T, precision=highest)
    grad_cond_part = grad_cond_act * cond_sigmoid * (1.0 + cond_float * (1.0 - cond_sigmoid))
    gain_grads = jnp.stack(
        [gain_zero, gain_one, gain_two, gain_three, gain_four, gain_five, gain_six]
    )
    partial_owned = (
        lax.psum_scatter(
            wgrad_modulation.astype(jnp.bfloat16), "clip", scatter_dimension=0, tiled=True
        ).astype(jnp.float32),
        lax.psum_scatter(
            bias_grad.astype(jnp.bfloat16), "clip", scatter_dimension=0, tiled=True
        ).astype(jnp.float32),
        lax.psum_scatter(
            wgrad_attention.astype(jnp.bfloat16), "clip", scatter_dimension=0, tiled=True
        ).astype(jnp.float32),
        lax.psum_scatter(
            wgrad_output.astype(jnp.bfloat16), "clip", scatter_dimension=0, tiled=True
        ).astype(jnp.float32),
        lax.psum_scatter(
            wgrad_caption.astype(jnp.bfloat16), "clip", scatter_dimension=0, tiled=True
        ).astype(jnp.float32),
        lax.psum_scatter(
            gain_grads.astype(jnp.bfloat16), "clip", scatter_dimension=1, tiled=True
        ).astype(jnp.float32),
        lax.psum_scatter(
            wgrad_gateup.astype(jnp.bfloat16), "clip", scatter_dimension=0, tiled=True
        ).astype(jnp.float32),
        lax.psum_scatter(
            wgrad_down.astype(jnp.bfloat16), "clip", scatter_dimension=0, tiled=True
        ).astype(jnp.float32),
    )
    owned = (
        lax.psum_scatter(
            partial_owned[0].astype(jnp.bfloat16), "seq", scatter_dimension=0, tiled=True
        ).astype(jnp.float32),
        lax.psum_scatter(
            partial_owned[1].astype(jnp.bfloat16), "seq", scatter_dimension=0, tiled=True
        ).astype(jnp.float32),
        lax.psum_scatter(
            partial_owned[2].astype(jnp.bfloat16), "seq", scatter_dimension=0, tiled=True
        ).astype(jnp.float32),
        lax.psum_scatter(
            partial_owned[3].astype(jnp.bfloat16), "seq", scatter_dimension=0, tiled=True
        ).astype(jnp.float32),
        lax.psum_scatter(
            partial_owned[4].astype(jnp.bfloat16), "seq", scatter_dimension=0, tiled=True
        ).astype(jnp.float32),
        lax.psum_scatter(
            partial_owned[5].astype(jnp.bfloat16), "seq", scatter_dimension=1, tiled=True
        ).astype(jnp.float32),
        lax.psum_scatter(
            partial_owned[6].astype(jnp.bfloat16), "seq", scatter_dimension=0, tiled=True
        ).astype(jnp.float32),
        lax.psum_scatter(
            partial_owned[7].astype(jnp.bfloat16), "seq", scatter_dimension=0, tiled=True
        ).astype(jnp.float32),
    )
    grad_gate_total = lax.psum(grad_head_gate, ("clip", "seq"))
    grad_condition = lax.psum(grad_cond_part, "seq")
    return (
        block_out,
        grad_tokens,
        grad_caption,
        grad_condition,
        owned[0],
        owned[1],
        owned[2],
        owned[3],
        owned[4],
        owned[5],
        grad_gate_total,
        owned[6],
        owned[7],
    )


def solution(mesh):
    placed = (
        P("clip", "seq", None),
        P("clip", "seq", None),
        P("clip", None),
        P("clip"),
        P("clip", None),
        P("clip", None),
        P(("clip", "seq"), None),
        P(("clip", "seq")),
        P(("clip", "seq"), None),
        P(("clip", "seq"), None),
        P(("clip", "seq"), None),
        P(None, ("clip", "seq")),
        P(),
        P(("clip", "seq"), None),
        P(("clip", "seq"), None),
        P("clip", "seq", None),
    )
    return jax.shard_map(
        local,
        mesh=mesh,
        in_specs=placed,
        out_specs=(
            P("clip", "seq", None),
            P("clip", "seq", None),
            P("clip", "seq", None),
            P("clip", None),
            P(("clip", "seq"), None),
            P(("clip", "seq")),
            P(("clip", "seq"), None),
            P(("clip", "seq"), None),
            P(("clip", "seq"), None),
            P(None, ("clip", "seq")),
            P(),
            P(("clip", "seq"), None),
            P(("clip", "seq"), None),
        ),
        check_vma=False,
    )
```

profile of v0, /device:TPU:1, one launch (start us, length us, event | category | flops | bytes accessed | tf_op | source)
XLA Modules:
  0.0 2514.2 jit_solution(16652940430061687403)
XLA Ops:
  12.0 63.7 %all-gather.1 = bf16[32,48,7]{1,2,0:T(8,128)(2,1)S(1)} all-gather(bf16[1,48,7]{1,2,0:T(8,128)(2,1)} %bitcast.475), channel_id=1, replica_groups=mesh['clip'=4,'seq'=8] {'clip','seq'}, dimensions={0}, use_global_device_ids=true | all-gather | bytes 22176 | tf_op jit(solution)/shard_map/all_gather | solution.py:89
  77.4 44.3 %all-reduce = bf16[6144]{0:T(1024)(128)(2,1)S(1)} all-reduce(bf16[6144]{0:T(1024)(128)(2,1)S(1)} %dynamic-update-slice), channel_id=1, replica_groups=mesh['clip'=4,'seq'=8] {'clip','seq'}, use_global_device_ids=true, to_apply=%add | all-reduce | flops 6144 | bytes 24576
  134.2 81.7 %all-gather.15.cloned.1.call-done = bf16[1536,4608]{1,0:T(8,128)(2,1)} async-done(((bf16[48,4608]{1,0:T(8,128)(2,1)}), bf16[1536,4608]{1,0:T(8,128)(2,1)}) %all-gather.15.cloned.1.call-update) | async-done | bytes 14155792 | tf_op jit(solution)/shard_map/all_gather | solution.py:86
  238.6 54.0 %all-gather.17.cloned.1.call-done = bf16[1,1024,24,64]{1,3,2,0:T(8,128)(2,1)} async-done(((bf16[1,128,24,64]{1,3,2,0:T(8,128)(2,1)}), bf16[1,1024,24,64]{1,3,2,0:T(8,128)(2,1)}) %all-gather.17.cloned.1.call-update) | async-done | bytes 3145744 | tf_op jit(solution)/shard_map/all_gather | solution.py:165
  292.6 18.3 while.60
  310.9 44.9 %all-gather.19.cloned.1.call-done = bf16[1,1024,24,64]{1,3,2,0:T(8,128)(2,1)} async-done(((bf16[1,128,24,64]{1,3,2,0:T(8,128)(2,1)}), bf16[1,1024,24,64]{1,3,2,0:T(8,128)(2,1)}) %all-gather.19.cloned.1.call-update) | async-done | bytes 3145744 | tf_op jit(solution)/shard_map/all_gather | solution.py:166
  364.0 148.4 %all-gather.21.cloned.1.call-done = bf16[4096,3072]{1,0:T(8,128)(2,1)} async-done(((bf16[128,3072]{1,0:T(8,128)(2,1)}), bf16[4096,3072]{1,0:T(8,128)(2,1)}) %all-gather.21.cloned.1.call-update) | async-done | bytes 25165840 | tf_op jit(solution)/shard_map/all_gather | solution.py:88
  522.6 27.0 %all_gather.65 = bf16[1,128,24,64]{3,2,0,1:T(8,128)(2,1)S(1)} all-gather(bf16[1,16,24,64]{3,2,0,1:T(8,128)(2,1)S(1)} %bitcast.461), channel_id=1, replica_groups=mesh['clip'=4,'seq'=8] {'seq'}, dimensions={1}, use_global_device_ids=true | all-gather | bytes 442368 | tf_op jit(solution)/shard_map/all_gather | solution.py:141
  550.2 28.1 %all_gather.64 = bf16[1,128,24,64]{3,2,0,1:T(8,128)(2,1)S(1)} all-gather(bf16[1,16,24,64]{3,2,0,1:T(8,128)(2,1)S(1)} %bitcast.462), channel_id=1, replica_groups=mesh['clip'=4,'seq'=8] {'seq'}, dimensions={1}, use_global_device_ids=true | all-gather | bytes 442368 | tf_op jit(solution)/shard_map/all_gather | solution.py:142
  592.4 153.7 %all-gather.25.cloned.1.call-done = bf16[1536,8192]{1,0:T(8,128)(2,1)} async-done(((bf16[48,8192]{1,0:T(8,128)(2,1)}), bf16[1536,8192]{1,0:T(8,128)(2,1)}) %all-gather.25.cloned.1.call-update) | async-done | bytes 25165840 | tf_op jit(solution)/shard_map/all_gather | solution.py:212
  759.2 84.2 %all-gather.27.cloned.1.call-done = bf16[4096,1536]{1,0:T(8,128)(2,1)} async-done(((bf16[128,1536]{1,0:T(8,128)(2,1)}), bf16[4096,1536]{1,0:T(8,128)(2,1)}) %all-gather.27.cloned.1.call-update) | async-done | bytes 12582928 | tf_op jit(solution)/shard_map/all_gather | solution.py:213
  862.6 15.7 multiply_reduce_fusion.4
  891.1 26.5 %all_gather.70 = f32[1,1024,24]{1,2,0:T(8,128)} all-gather(f32[1,128,24]{1,2,0:T(8,128)S(1)} %bitcast.470), channel_id=1, replica_groups=mesh['clip'=4,'seq'=8] {'seq'}, dimensions={1}, use_global_device_ids=true | all-gather | bytes 110592 | tf_op jit(solution)/shard_map/all_gather | solution.py:354
  925.4 26.3 %all-gather = f32[1024,24]{0,1:T(8,128)} all-gather(f32[128,24]{0,1:T(8,128)S(1)} %get-tuple-element.724), channel_id=2, replica_groups=mesh['clip'=4,'seq'=8] {'seq'}, dimensions={0}, use_global_device_ids=true | all-gather | bytes 110592 | tf_op jit(solution)/shard_map/all_gather | solution.py:355
  951.6 23.3 while.62
  979.3 34.5 %all-gather.29.cloned.1.call-done = bf16[1,1024,24,64]{1,3,2,0:T(8,128)(2,1)} async-done(((bf16[1,128,24,64]{1,3,2,0:T(8,128)(2,1)}), bf16[1,1024,24,64]{1,3,2,0:T(8,128)(2,1)}) %all-gather.29.cloned.1.call-update) | async-done | bytes 3145744 | tf_op jit(solution)/shard_map/all_gather | solution.py:350
  1013.8 63.5 %all-gather.31.cloned.1.call-done = bf16[1,1024,24,64]{1,3,2,0:T(8,128)(2,1)} async-done(((bf16[1,128,24,64]{1,3,2,0:T(8,128)(2,1)}), bf16[1,1024,24,64]{1,3,2,0:T(8,128)(2,1)}) %all-gather.31.cloned.1.call-update) | async-done | bytes 3145744 | tf_op jit(solution)/shard_map/all_gather | solution.py:353
  1077.4 35.2 %while.63 = (s32[]{:T(128)}, f32[1,128,24,64]{1,3,2,0:T(8,128)}, f32[1,128,24,64]{1,3,2,0:T(8,128)S(1)}, bf16[1,1024,24,64]{1,3,2,0:T(8,128)(2,1)}, bf16[1,128,2...) while((s32[]{:T(128)}, f32[1,128,24,64]{1,3,2,0:T(8,128)}, ...), condition=%wide.region_24.26_spmd.clone, body=%wide.region_23.25_spmd.clone.sunk | while | flops 818872320 | bytes 29443784 | solution.py:401
  1165.4 15.1 convolution_convert_fusion
  1194.7 20.3 reduce-scatter.35.cloned.1.call-done
  1215.3 101.4 %reduce-scatter.45.cloned.1.call-done = bf16[1024,1536]{1,0:T(8,128)(2,1)} async-done(((bf16[4096,1536]{1,0:T(8,128)(2,1)}), bf16[1024,1536]{1,0:T(8,128)(2,1)}) %reduce-scatter.45.cloned.1.call-update) | async-done | bytes 3145744 | tf_op jit(solution)/shard_map/reduce_scatter | solution.py:472
  1316.8 101.7 %reduce-scatter.27.cloned.1.call-done = bf16[256,6144]{1,0:T(8,128)(2,1)} async-done(((bf16[1024,6144]{1,0:T(8,128)(2,1)}), bf16[256,6144]{1,0:T(8,128)(2,1)}) %reduce-scatter.27.cloned.1.call-update) | async-done | bytes 3145744 | tf_op jit(solution)/shard_map/reduce_scatter | solution.py:451
  1418.5 112.0 %reduce-scatter.31.cloned.1.call-done = bf16[384,4608]{1,0:T(8,128)(2,1)} async-done(((bf16[1536,4608]{1,0:T(8,128)(2,1)}), bf16[384,4608]{1,0:T(8,128)(2,1)}) %reduce-scatter.31.cloned.1.call-update) | async-done | bytes 3538960 | tf_op jit(solution)/shard_map/reduce_scatter | solution.py:457
  1530.5 183.0 %reduce-scatter.41.cloned.1.call-done = bf16[384,8192]{1,0:T(8,128)(2,1)} async-done(((bf16[1536,8192]{1,0:T(8,128)(2,1)}), bf16[384,8192]{1,0:T(8,128)(2,1)}) %reduce-scatter.41.cloned.1.call-update) | async-done | bytes 6291472 | tf_op jit(solution)/shard_map/reduce_scatter | solution.py:469
  1713.6 183.0 %reduce-scatter.39.cloned.1.call-done = bf16[1024,3072]{0,1:T(8,128)(2,1)} async-done(((bf16[4096,3072]{0,1:T(8,128)(2,1)}), bf16[1024,3072]{0,1:T(8,128)(2,1)}) %reduce-scatter.39.cloned.1.call-update) | async-done | bytes 6291472 | tf_op jit(solution)/shard_map/reduce_scatter | solution.py:463
  1908.5 38.7 %psum.15 = f32[24]{0:T(128)} all-reduce(f32[24]{0:T(128)S(1)} %subtract_multiply_fusion.2), channel_id=1, replica_groups=mesh['clip'=4,'seq'=8] {'clip','seq'}, use_global_device_ids=true, to_apply=%region_55.57 | all-reduce | flops 24 | bytes 192 | tf_op jit(solution)/shard_map/psum | solution.py:502
  1970.8 16.6 all-reduce.2
  2024.9 76.9 %reduce-scatter.47.cloned.1.call-done = bf16[128,1536]{1,0:T(8,128)(2,1)} async-done(((bf16[1024,1536]{1,0:T(8,128)(2,1)}), bf16[128,1536]{1,0:T(8,128)(2,1)}) %reduce-scatter.47.cloned.1.call-update) | async-done | bytes 393232 | tf_op jit(solution)/shard_map/reduce_scatter | solution.py:498
  2103.8 75.8 %reduce-scatter.29.cloned.1.call-done = bf16[32,6144]{1,0:T(8,128)(2,1)} async-done(((bf16[256,6144]{1,0:T(8,128)(2,1)}), bf16[32,6144]{1,0:T(8,128)(2,1)}) %reduce-scatter.29.cloned.1.call-update) | async-done | bytes 393232 | tf_op jit(solution)/shard_map/reduce_scatter | solution.py:477
  2181.5 80.8 %reduce-scatter.33.cloned.1.call-done = bf16[48,4608]{1,0:T(8,128)(2,1)} async-done(((bf16[384,4608]{1,0:T(8,128)(2,1)}), bf16[48,4608]{1,0:T(8,128)(2,1)}) %reduce-scatter.33.cloned.1.call-update) | async-done | bytes 442384 | tf_op jit(solution)/shard_map/reduce_scatter | solution.py:483
  2264.3 119.0 %reduce-scatter.43.cloned.1.call-done = bf16[48,8192]{1,0:T(8,128)(2,1)} async-done(((bf16[384,8192]{1,0:T(8,128)(2,1)}), bf16[48,8192]{1,0:T(8,128)(2,1)}) %reduce-scatter.43.cloned.1.call-update) | async-done | bytes 786448 | tf_op jit(solution)/shard_map/reduce_scatter | solution.py:495
  2385.7 118.6 %reduce-scatter.49.cloned.1.call-done = bf16[128,3072]{1,0:T(8,128)(2,1)} async-done(((bf16[1024,3072]{1,0:T(8,128)(2,1)}), bf16[128,3072]{1,0:T(8,128)(2,1)}) %reduce-scatter.49.cloned.1.call-update) | async-done | bytes 786448
  (416 shorter events, 362.1 us)
Async XLA Ops:
  7.2 505.2 %copy-start = (bf16[1,16,4096]{2,1,0:T(8,128)(2,1)S(1)}, bf16[1,16,4096]{2,1,0:T(8,128)(2,1)}, u32[]{:S(2)}) copy-start(bf16[1,16,4096]{2,1,0:T(8,128)(2,1)} %param.27) | copy-start | bytes 393220
  7.2 120.5 %all-gather.13.cloned.1.call-start = ((), (), s32[]{:S(2)}) async-start(), calls=%async_computation.16 | async-start | bytes 12976128 | tf_op jit(solution)/shard_map/all_gather | solution.py:84
  7.9 208.0 %all-gather.15.cloned.1.call-start = ((), (), s32[]{:S(2)}) async-start(), calls=%async_computation.17 | async-start | bytes 14598144 | tf_op jit(solution)/shard_map/all_gather | solution.py:86
  8.7 283.9 %all-gather.17.cloned.1.call-start = ((), (), s32[]{:S(2)}) async-start(), calls=%async_computation.18 | async-start | bytes 3538944 | tf_op jit(solution)/shard_map/all_gather | solution.py:165
  231.2 348.4 %copy-start.25 = (bf16[1,128,24,32]{1,3,2,0:T(8,128)(2,1)}, bf16[1,128,24,32]{1,3,2,0:T(8,128)(2,1)S(1)}, u32[]{:S(2)}) copy-start(bf16[1,128,24,32]{1,3,2,0:T(8,128)(2,1)S(1)} %get-tuple-element.813) | copy-start | bytes 589828
  232.1 123.7 %all-gather.19.cloned.1.call-start = ((), (), s32[]{:S(2)}) async-start(), calls=%async_computation.19 | async-start | bytes 3538944 | tf_op jit(solution)/shard_map/all_gather | solution.py:166
  234.9 277.4 %all-gather.21.cloned.1.call-start = ((), (), s32[]{:S(2)}) async-start(), calls=%async_computation.20 | async-start | bytes 25952256 | tf_op jit(solution)/shard_map/all_gather | solution.py:88
  235.5 353.3 %all-gather.23.cloned.1.call-start = ((), (), s32[]{:S(2)}) async-start(), calls=%async_computation.21 | async-start | bytes 4866048 | tf_op jit(solution)/shard_map/all_gather | solution.py:87
  236.1 510.1 %all-gather.25.cloned.1.call-start = ((), (), s32[]{:S(2)}) async-start(), calls=%async_computation.22 | async-start | bytes 25952256 | tf_op jit(solution)/shard_map/all_gather | solution.py:212
  236.8 606.5 %all-gather.27.cloned.1.call-start = ((), (), s32[]{:S(2)}) async-start(), calls=%async_computation.23 | async-start | bytes 12976128 | tf_op jit(solution)/shard_map/all_gather | solution.py:213
  237.6 739.5 %reduce-scatter.23.cloned.1.call-start = ((), (), s32[]{:S(2)}) async-start(), calls=%async_computation.26 | async-start | bytes 884736 | tf_op jit(solution)/shard_map/reduce_scatter | solution.py:309
  238.5 343.0 %copy-start.97 = (f32[24]{0:T(128)}, f32[24]{0:T(128)S(1)}, u32[]{:S(2)}) copy-start(f32[24]{0:T(128)S(1)} %convert_tanh_fusion) | copy-start | bytes 292
  363.9 158.3 %copy-start.2 = (bf16[1,128,24,64]{1,3,2,0:T(8,128)(2,1)}, bf16[1,128,24,64]{1,3,2,0:T(8,128)(2,1)S(1)}, u32[]{:S(2)}) copy-start(bf16[1,128,24,64]{1,3,2,0:T(8,128)(2,1)S(1)} %get-tuple-element.1202) | copy-start | bytes 1179652
  364.0 217.5 %copy-start.30 = (f32[1,24,128,64]{2,3,1,0:T(8,128)}, f32[1,24,128,64]{2,3,1,0:T(8,128)S(1)}, u32[]{:S(2)}) copy-start(f32[1,24,128,64]{2,3,1,0:T(8,128)S(1)} %get-tuple-element.514) | copy-start | bytes 2359300
  592.4 285.9 %copy-start.6 = (f32[1,128,1536]{2,1,0:T(8,128)}, f32[1,128,1536]{2,1,0:T(8,128)S(1)}, u32[]{:S(2)}) copy-start(f32[1,128,1536]{2,1,0:T(8,128)S(1)} %get-tuple-element.798) | copy-start | bytes 2359300
  889.7 124.1 %all-gather.29.cloned.1.call-start = ((), (), s32[]{:S(2)}) async-start(), calls=%async_computation.24 | async-start | bytes 3538944 | tf_op jit(solution)/shard_map/all_gather | solution.py:350
  890.2 187.1 %all-gather.31.cloned.1.call-start = ((), (), s32[]{:S(2)}) async-start(), calls=%async_computation.25 | async-start | bytes 3538944 | tf_op jit(solution)/shard_map/all_gather | solution.py:353
  891.0 289.6 %reduce-scatter.25.cloned.1.call-start = ((), (), s32[]{:S(2)}) async-start(), calls=%async_computation.27 | async-start | bytes 884736 | tf_op jit(solution)/shard_map/reduce_scatter | solution.py:312
  977.0 217.1 %reduce-scatter.51.cloned.1.call-start = ((), (), s32[]{:S(2)}) async-start(), calls=%async_computation.40 | async-start | bytes 491520
  1135.6 79.4 %reduce-scatter.35.cloned.1.call-start = ((), (), s32[]{:S(2)}) async-start(), calls=%async_computation.32 | async-start | bytes 5898240 | tf_op jit(solution)/shard_map/reduce_scatter | solution.py:460
  1139.3 177.4 %reduce-scatter.45.cloned.1.call-start = ((), (), s32[]{:S(2)}) async-start(), calls=%async_computation.37 | async-start | bytes 15728640 | tf_op jit(solution)/shard_map/reduce_scatter | solution.py:472
  1147.0 271.5 %reduce-scatter.27.cloned.1.call-start = ((), (), s32[]{:S(2)}) async-start(), calls=%async_computation.28 | async-start | bytes 15728640 | tf_op jit(solution)/shard_map/reduce_scatter | solution.py:451
  1155.4 375.1 %reduce-scatter.31.cloned.1.call-start = ((), (), s32[]{:S(2)}) async-start(), calls=%async_computation.30 | async-start | bytes 17694720 | tf_op jit(solution)/shard_map/reduce_scatter | solution.py:457
  1164.0 549.6 %reduce-scatter.41.cloned.1.call-start = ((), (), s32[]{:S(2)}) async-start(), calls=%async_computation.35 | async-start | bytes 31457280 | tf_op jit(solution)/shard_map/reduce_scatter | solution.py:469
  1180.5 716.1 %reduce-scatter.39.cloned.1.call-start = ((), (), s32[]{:S(2)}) async-start(), calls=%async_computation.34 | async-start | bytes 31457280 | tf_op jit(solution)/shard_map/reduce_scatter | solution.py:463
  1194.0 822.3 %reduce-scatter.53.cloned.1.call-start = ((), (), s32[]{:S(2)}) async-start(), calls=%async_computation.41 | async-start | bytes 110592
  1194.6 828.6 %reduce-scatter.37.cloned.1.call-start = ((), (), s32[]{:S(2)}) async-start(), calls=%async_computation.33 | async-start | bytes 1327104 | tf_op jit(solution)/shard_map/reduce_scatter | solution.py:486
  1215.0 886.8 %reduce-scatter.47.cloned.1.call-start = ((), (), s32[]{:S(2)}) async-start(), calls=%async_computation.38 | async-start | bytes 3538944 | tf_op jit(solution)/shard_map/reduce_scatter | solution.py:498
  1316.7 862.8 %reduce-scatter.29.cloned.1.call-start = ((), (), s32[]{:S(2)}) async-start(), calls=%async_computation.29 | async-start | bytes 3538944 | tf_op jit(solution)/shard_map/reduce_scatter | solution.py:477
  1418.5 843.9 %reduce-scatter.33.cloned.1.call-start = ((), (), s32[]{:S(2)}) async-start(), calls=%async_computation.31 | async-start | bytes 3981312 | tf_op jit(solution)/shard_map/reduce_scatter | solution.py:483
  1530.5 852.8 %reduce-scatter.43.cloned.1.call-start = ((), (), s32[]{:S(2)}) async-start(), calls=%async_computation.36 | async-start | bytes 7077888 | tf_op jit(solution)/shard_map/reduce_scatter | solution.py:495
  1713.6 790.7 %reduce-scatter.49.cloned.1.call-start = ((), (), s32[]{:S(2)}) async-start(), calls=%async_computation.39 | async-start | bytes 7077888
  (93 other events, 2277.6 us)
Sparse Core Ops, SparseCore 0:
  11.0 100.1 all-gather.12
  114.2 101.6 all-gather.14
  232.2 60.3 all-gather.16
  294.5 61.2 all-gather.18
  358.6 153.6 all-gather.20
  515.2 73.5 all-gather.22
  591.8 154.3 all-gather.24
  749.1 94.1 all-gather.26
  889.8 58.9 reduce-scatter.22
  950.8 62.9 all-gather.28
  1016.0 61.2 all-gather.30
  1081.4 59.2 reduce-scatter.24
  1143.2 21.4 reduce-scatter.50
  1167.1 47.8 reduce-scatter.34
  1217.6 99.0 reduce-scatter.44
  1319.3 99.0 reduce-scatter.26
  1421.0 109.3 reduce-scatter.30
  1533.1 180.4 reduce-scatter.40
  1716.2 180.4 reduce-scatter.38
  1900.1 55.8 reduce-scatter.52
  1959.7 63.5 reduce-scatter.36
  2027.3 74.5 reduce-scatter.46
  2105.8 73.6 reduce-scatter.28
  2183.5 78.7 reduce-scatter.32
  2266.3 116.9 reduce-scatter.42
  2387.2 117.0 reduce-scatter.48
where the time goes:
time: 2520 us; the launch traced here: 2510 us
  waiting for transfers between devices  1850 us (73%)
  blocking collectives  297 us (12%)
  matrix products  242 us (10%)
  other arithmetic  51.3 us (2%)
  local copies, waits for them, and re-layouts  47.9 us (2%)
    reduce_scatter x1, waiting for transfers between devices, local(): lax.psum_scatter(wgrad_gateup.astype(jnp.bfloat16), 'clip', scatter_dimen...  183 us
    reduce_scatter x1, waiting for transfers between devices, local(): lax.psum_scatter(wgrad_caption.astype(jnp.bfloat16), 'clip', scatter_dime...  183 us
    all_gather x1, waiting for transfers between devices, local(): lax.all_gather(w_gateup, ('clip', 'seq'), axis=0, tiled=True)  154 us
    all_gather x1, waiting for transfers between devices, local(): lax.all_gather(w_caption, ('clip', 'seq'), axis=0, tiled=True)  148 us
    unnamed x29, waiting for transfers between devices  124 us
    reduce_scatter x1, waiting for transfers between devices, local(): lax.psum_scatter(partial_owned[6].astype(jnp.bfloat16), 'seq', scatter_di...  119 us
    reduce_scatter x1, waiting for transfers between devices, local(): lax.psum_scatter(wgrad_attention.astype(jnp.bfloat16), 'clip', scatter_di...  112 us
    reduce_scatter x1, waiting for transfers between devices, local(): lax.psum_scatter(wgrad_modulation.astype(jnp.bfloat16), 'clip', scatter_d...  102 us
  transfers between devices with their start and end apart: 26, of which 21 were waited for; matrix products, arithmetic and copies ran while one was open for 11% of the time, Pallas kernels for 0%

commit v1 on v0

--- a/solution.py
+++ b/solution.py
@@ -3,11 +3,14 @@
 import jax
 import jax.numpy as jnp
 from jax import lax
+from jax.sharding import Mesh
 from jax.sharding import PartitionSpec as P
 
 epsilon = 1e-06
 theta_base = 10000.0
 highest = lax.Precision.HIGHEST
+bf16 = jnp.bfloat16
+f32 = jnp.float32
 
 
 def rms_norm(value):
@@ -518,43 +521,553 @@
     )
 
 
+def flip(value, axis):
+    return lax.ppermute(value, axis, [(0, 1), (1, 0)])
+
+
+def from_ahead(value, axis, step):
+    count = lax.axis_size(axis)
+    return lax.ppermute(value, axis, [((i + step) % count, i) for i in range(count)])
+
+
+def swap_z(value, bit):
+    return lax.ppermute(value, "z", [(i, i ^ bit) for i in range(4)])
+
+
+def sum_seq(value):
+    value = value + flip(value, "x")
+    value = value + swap_z(value, 1)
+    return value + swap_z(value, 2)
+
+
+def to_relative(value):
+    value = jnp.where(lax.axis_index("x") == 0, value, value[:, ::-1])
+    return jnp.roll(value, -lax.axis_index("z"), axis=0)
+
+
+def to_absolute(value):
+    value = jnp.where(lax.axis_index("x") == 0, value, value[:, ::-1])
+    return jnp.roll(value, lax.axis_index("z"), axis=0)
+
+
+def clip_relative(value):
+    value = jnp.where(lax.axis_index("y") == 0, value, value[::-1])
+    return jnp.where(lax.axis_index("core") == 0, value, value[:, ::-1])
+
+
+def gather_plane(value):
+    rows = value.shape[0]
+    half = rows // 2
+    from_x = flip(value, "x")
+    from_y = flip(value, "y")
+    far_front = flip(from_y[:half], "x")
+    far_back = flip(from_x[half:], "y")
+    four = jnp.concatenate([value, from_x, from_y, far_front, far_back], axis=0)
+    return jnp.concatenate([four, flip(four, "core")], axis=0)
+
+
+def scatter_plane(value):
+    count = value.shape[0] // 2
+    rows = count // 4
+    half = rows // 2
+    four = value[:count] + flip(value[count:].astype(bf16), "core").astype(f32)
+    own, for_x, for_y, far = [four[i * rows : (i + 1) * rows] for i in range(4)]
+    by_x = flip(jnp.concatenate([for_x[:half], far[:half]]).astype(bf16), "x").astype(f32)
+    by_y = flip(jnp.concatenate([for_y[half:], far[half:]]).astype(bf16), "y").astype(f32)
+    own = own + jnp.concatenate([by_x[:half], by_y[:half]])
+    last_y = flip((for_y[:half] + by_x[half:]).astype(bf16), "y").astype(f32)
+    last_x = flip((for_x[half:] + by_y[half:]).astype(bf16), "x").astype(f32)
+    return own + jnp.concatenate([last_y, last_x])
+
+
+def gather_seq(value):
+    rows = value.shape[0]
+    early = rows // 4
+    rest = rows - early
+    ahead = [from_ahead(value[early:], "z", k) for k in (1, 2, 3)]
+    other = flip(value, "x")
+    both = jnp.concatenate([value[:early], other[:early]], axis=0)
+    early_ahead = [from_ahead(both, "z", k) for k in (1, 2, 3)]
+    other_ahead = flip(jnp.concatenate(ahead, axis=0), "x")
+    pieces = [value, other]
+    for k in range(3):
+        pieces += [
+            early_ahead[k][:early],
+            ahead[k],
+            early_ahead[k][early:],
+            other_ahead[k * rest : (k + 1) * rest],
+        ]
+    return jnp.concatenate(pieces, axis=0)
+
+
+def scatter_seq(value):
+    rows = value.shape[0] // 8
+    early = rows // 4
+    parts = value.reshape(4, 2, rows, value.shape[1])
+    low = parts.astype(bf16)
+    other = flip(low[1:, 1, early:], "x").astype(f32)
+    front = [from_ahead(low[(4 - k) % 4, :, :early], "z", k).astype(f32) for k in (1, 2, 3)]
+    front_sum = parts[0, :, :early] + front[0] + front[1] + front[2]
+    back_sum = (parts[1:, 0, early:] + other).astype(bf16)
+    back = [from_ahead(back_sum[3 - k], "z", k).astype(f32) for k in (1, 2, 3)]
+    last = flip(jnp.concatenate([front_sum[1].astype(bf16), low[0, 1, early:]]), "x").astype(f32)
+    out_front = front_sum[0] + last[:early]
+    out_back = parts[0, 0, early:] + last[early:] + back[0] + back[1] + back[2]
+    return jnp.concatenate([out_front, out_back])
+
+
+def scatter_clip(value):
+    pair = value[:2] + flip(value[2:], "y")
+    return pair[0] + flip(pair[1], "core")
+
+
+def gather_clip(value):
+    pair = jnp.stack([value, flip(value, "core")])
+    return jnp.concatenate([pair, flip(pair, "y")])
+
+
+def rms_scale(square_mean):
+    return lax.rsqrt(square_mean + epsilon)
+
+
+def local_fast(
+    tokens,
+    caption,
+    condition,
+    caption_len,
+    frame_shape,
+    rope_shift,
+    w_modulation,
+    mod_bias,
+    w_attention,
+    w_output,
+    w_caption,
+    norm_gains,
+    head_gate,
+    w_gateup,
+    w_down,
+    cotangent,
+):
+    seq_axes = ("z", "x")
+    clip_axes = ("y", "core")
+    all_axes = clip_axes + seq_axes
+    plane_axes = ("y", "core", "x")
+    rows, width = tokens.shape[1:]
+    total = rows * 8
+    heads = head_gate.shape[0]
+    head_dim = width // heads
+    own_heads = heads // 8
+    cols = own_heads * head_dim
+    score_scale = head_dim ** (-0.5)
+    text_rows = caption.shape[1]
+    text_total = text_rows * 8
+    z_at, x_at = lax.axis_index("z"), lax.axis_index("x")
+    seq_at = z_at * 2 + x_at
+    owner = (lax.axis_index("y") * 2 + lax.axis_index("core")) * 8 + seq_at
+
+    own_tokens = tokens[0]
+    token_all = gather_seq(own_tokens)
+
+    attn_piece = jnp.transpose(
+        w_attention.reshape(-1, 3, 8, cols), (2, 0, 1, 3)
+    ).reshape(8, -1, 3 * cols)
+    attn_piece = lax.all_to_all(attn_piece, seq_axes, 0, 0, tiled=True)
+    attn_piece = attn_piece.reshape(1, 1, -1, 3 * cols)
+    own_attn = gather_clip(attn_piece[0, 0]).reshape(2, 2, -1, 3 * cols)
+    own_attn = clip_relative(own_attn).reshape(width, 3 * cols)
+
+    cond_float = condition[0].astype(f32)
+    cond_act = jax.nn.silu(cond_float).astype(bf16)
+    cond_all = gather_clip(cond_act)
+    cond_rows = w_modulation.shape[0]
+    cond_own = lax.dynamic_slice_in_dim(cond_all, owner * cond_rows, cond_rows, 1)
+    mod_part = jnp.dot(cond_own, w_modulation, preferred_element_type=f32)
+    bias_len = mod_bias.shape[0]
+    bias_wide = lax.dynamic_update_slice(
+        jnp.zeros((4 * width,), f32), mod_bias.astype(f32), (owner * bias_len,)
+    )
+    mod_part = mod_part + bias_wide[None]
+    gain_cols = norm_gains.shape[1]
+    gain_wide = lax.dynamic_update_slice(
+        jnp.zeros((7, width), f32), norm_gains.astype(f32), (0, owner * gain_cols)
+    ).reshape(-1)
+    sent = flip(jnp.concatenate([mod_part[2:].reshape(-1), gain_wide]), "y")
+    mod_pair = mod_part[:2] + sent[: 8 * width].reshape(2, -1)
+    gain_wide = gain_wide + sent[8 * width :]
+    sent = flip(jnp.concatenate([mod_pair[1], gain_wide]), "core")
+    small = sum_seq(jnp.concatenate([mod_pair[0], gain_wide]) + sent)
+    modulation = small[: 4 * width].reshape(4, width)
+    gain_rows = small[4 * width :].reshape(7, width)
+    scale_attn = modulation[0]
+    gate_attn = jnp.tanh(modulation[1])
+    scale_ffn = modulation[2]
+    gate_ffn = jnp.tanh(modulation[3])
+    gain_query = lax.dynamic_slice_in_dim(gain_rows[4], seq_at * cols, cols)
+    gain_key = lax.dynamic_slice_in_dim(gain_rows[5], seq_at * cols, cols)
+    gain_text = lax.dynamic_slice_in_dim(gain_rows[6], seq_at * cols, cols)
+    head_low = lax.dynamic_slice_in_dim(head_gate, seq_at * own_heads, own_heads)
+    tanh_gate = jnp.tanh(head_low.astype(f32))
+
+    hidden_own = w_down.shape[0]
+    ffn_piece = jnp.transpose(
+        w_gateup.reshape(-1, 2, 2, 2, 4, 2, hidden_own), (2, 3, 5, 0, 1, 4, 6)
+    ).reshape(8, -1, 8 * hidden_own)
+    ffn_piece = lax.all_to_all(ffn_piece, plane_axes, 0, 0, tiled=True)
+    block = 2 * ffn_piece.shape[1]
+    full_out = lax.all_gather(w_output, all_axes, axis=0, tiled=True)
+    own_gateup = lax.all_gather(ffn_piece.reshape(4, block, -1), "z", axis=0)
+    own_gateup = jnp.transpose(own_gateup, (1, 0, 2, 3)).reshape(width, -1)
+    own_down = lax.all_gather(w_down, "z", axis=0, tiled=True)
+    hidden = 4 * hidden_own
+
+    cap_cols = w_caption.shape[0]
+    cap_piece = jnp.transpose(caption[0].reshape(text_rows, 32, cap_cols), (1, 0, 2))
+    cap_piece = lax.all_to_all(cap_piece, all_axes, 0, 0, tiled=True)
+    cap_all = clip_relative(cap_piece.reshape(2, 2, text_total, cap_cols)).reshape(
+        4 * text_total, cap_cols
+    )
+    cap_weight = to_relative(
+        jnp.transpose(w_caption.reshape(cap_cols, 2, 4, 2, cols), (2, 3, 0, 1, 4))
+    ).reshape(8, cap_cols, 2 * cols)
+    text_part = jnp.einsum("tk,skn->tsn", cap_all, cap_weight, preferred_element_type=f32)
+    text_part = text_part.reshape(4, text_total, 8, 2 * cols).astype(bf16)
+    text_pair = text_part[:2].astype(f32) + flip(text_part[2:], "y").astype(f32)
+    text_one = text_pair[0] + flip(text_pair[1].astype(bf16), "core").astype(f32)
+    text_proj = scatter_seq(jnp.transpose(text_one, (1, 0, 2)).reshape(8 * text_total, 2 * cols))
+    text_key_pre = text_proj[:, :cols]
+    text_square = jnp.sum(text_key_pre * text_key_pre, axis=1)
+
+    token_float = token_all.astype(f32)
+    normed_all = (rms_norm(token_float) * gain_rows[0] * (1.0 + scale_attn)).astype(bf16)
+    projected = jnp.dot(normed_all, own_attn, preferred_element_type=f32)
+    projected = to_absolute(projected.reshape(4, 2, rows, 3 * cols)).reshape(total, 3 * cols)
+    query_pre = projected[:, :cols]
+    key_pre = projected[:, cols : 2 * cols]
+    squares = jnp.concatenate(
+        [jnp.sum(query_pre * query_pre, axis=1), jnp.sum(key_pre * key_pre, axis=1), text_square]
+    )
+    squares = sum_seq(squares) / width
+    scales = rms_scale(squares)
+    query_scale = scales[:total, None]
+    key_scale = scales[total : 2 * total, None]
+    text_scale = scales[2 * total :, None]
+    query_normed = query_pre * query_scale
+    key_normed = key_pre * key_scale
+    text_key_normed = text_key_pre * text_scale
+    position = jnp.arange(total, dtype=jnp.int32)
+    angles = rope_angles(frame_shape[0], rope_shift[0], position, head_dim // 2)
+    cosine = jnp.cos(angles)[:, None, :]
+    sine_table = jnp.sin(angles)[:, None, :]
+    split = (total, own_heads, head_dim)
+    queries = rotate((query_normed * gain_query).reshape(split), cosine, sine_table).astype(bf16)
+    key_rows = rotate((key_normed * gain_key).reshape(split), cosine, sine_table).astype(bf16)
+    values = projected[:, 2 * cols :].reshape(split).astype(bf16)
+    text_split = (text_total, own_heads, head_dim)
+    text_keys = (text_key_normed * gain_text).astype(bf16).reshape(text_split)
+    text_values = text_proj[:, cols:].astype(bf16).reshape(text_split)
+
+    scores = jnp.einsum("qhd,khd->hqk", queries, key_rows, preferred_element_type=f32) * score_scale
+    row_max = jnp.max(scores, axis=-1)
+    log_sum = row_max + jnp.log(jnp.sum(jnp.exp(scores - row_max[..., None]), axis=-1))
+    probs = jnp.exp(scores - log_sum[..., None])
+    probs_low = probs.astype(bf16)
+    self_out = jnp.einsum("hqk,khd->qhd", probs_low, values, preferred_element_type=f32)
+    usable = jnp.arange(text_total, dtype=jnp.int32) < caption_len[0]
+    text_scores = (
+        jnp.einsum("qhd,khd->hqk", queries, text_keys, preferred_element_type=f32) * score_scale
+    )
+    text_weights = soft_weights(jnp.where(usable[None, None, :], text_scores, -1e30))
+    text_low = text_weights.astype(bf16)
+    cross_out = jnp.einsum("hqk,khd->qhd", text_low, text_values, preferred_element_type=f32)
+    mixed = (self_out + tanh_gate[None, :, None] * cross_out).astype(bf16).reshape(total, cols)
+
+    mixed_own = lax.all_to_all(mixed.reshape(8, rows, cols), seq_axes, 0, 0, tiled=True)
+    mixed_own = jnp.transpose(mixed_own, (1, 0, 2)).reshape(rows, width)
+    attn_proj = jnp.dot(mixed_own, full_out, preferred_element_type=f32)
+    attn_scale = rms_scale(jnp.mean(attn_proj * attn_proj, axis=-1, keepdims=True))
+    attn_normed = attn_proj * attn_scale
+    own_float = own_tokens.astype(f32)
+    token_scale = rms_scale(jnp.mean(own_float * own_float, axis=-1, keepdims=True))
+    token_normed = own_float * token_scale
+    residual = own_float + gate_attn * attn_normed * gain_rows[1]
+    residual_scale = rms_scale(jnp.mean(residual * residual, axis=-1, keepdims=True))
+    residual_normed = residual * residual_scale
+    normed_ffn = (residual_normed * gain_rows[2] * (1.0 + scale_ffn)).astype(bf16)
+
+    normed_ffn_all = gather_plane(normed_ffn)
+    gate_up = jnp.dot(normed_ffn_all, own_gateup, preferred_element_type=f32)
+    gate_part = gate_up[:, :hidden]
+    up_part = gate_up[:, hidden:]
+    gate_sigmoid = jax.nn.sigmoid(gate_part)
+    activated = (gate_part * gate_sigmoid * up_part).astype(bf16)
+    down_proj = scatter_plane(jnp.dot(activated, own_down, preferred_element_type=f32))
+    down_scale = rms_scale(jnp.mean(down_proj * down_proj, axis=-1, keepdims=True))
+    down_normed = down_proj * down_scale
+    block_out = residual + gate_ffn * down_normed * gain_rows[3]
+
+    upstream = cotangent[0].astype(f32)
+    sum_three = jnp.sum(upstream * down_normed, axis=0)
+    grad_in = upstream * gate_ffn * gain_rows[3]
+    grad_down = (
+        (grad_in - down_normed * jnp.mean(grad_in * down_normed, axis=-1, keepdims=True))
+        * down_scale
+    ).astype(bf16)
+    grad_down_all = gather_plane(grad_down)
+    wgrad_down = jnp.dot(activated.T, grad_down_all, preferred_element_type=f32)
+    grad_act = jnp.dot(grad_down_all, own_down.T, preferred_element_type=f32)
+    grad_gate_part = grad_act * up_part * gate_sigmoid * (1.0 + gate_part * (1.0 - gate_sigmoid))
+    grad_up_part = grad_act * gate_part * gate_sigmoid
+    grad_gate_up = jnp.concatenate([grad_gate_part, grad_up_part], axis=1).astype(bf16)
+    grad_normed_ffn = scatter_plane(
+        jnp.dot(grad_gate_up, own_gateup.T, preferred_element_type=f32)
+    )
+    wgrad_gateup = jnp.dot(normed_ffn_all.T, grad_gate_up, preferred_element_type=f32)
+    wgrad_down = lax.psum_scatter(
+        wgrad_down.astype(bf16), "z", scatter_dimension=0, tiled=True
+    ).astype(f32)
+    wgrad_gateup = jnp.transpose(
+        wgrad_gateup.astype(bf16).reshape(4, 4, block, -1), (1, 0, 2, 3)
+    )
+    wgrad_gateup = lax.psum_scatter(wgrad_gateup, "z", scatter_dimension=0, tiled=False)
+    wgrad_gateup = lax.all_to_all(
+        wgrad_gateup.reshape(8, block // 2, -1), plane_axes, 0, 0, tiled=True
+    )
+    wgrad_gateup = (
+        jnp.transpose(
+            wgrad_gateup.reshape(2, 2, 2, block // 2, 2, 4, hidden_own), (3, 4, 0, 1, 5, 2, 6)
+        )
+        .reshape(block // 2, -1)
+        .astype(f32)
+    )
+
+    sum_two = jnp.sum(grad_normed_ffn * residual_normed, axis=0)
+    grad_in = grad_normed_ffn * gain_rows[2] * (1.0 + scale_ffn)
+    grad_residual = (
+        upstream
+        + (grad_in - residual_normed * jnp.mean(grad_in * residual_normed, axis=-1, keepdims=True))
+        * residual_scale
+    )
+    sum_one = jnp.sum(grad_residual * attn_normed, axis=0)
+    grad_in = grad_residual * gate_attn * gain_rows[1]
+    grad_attn = (
+        (grad_in - attn_normed * jnp.mean(grad_in * attn_normed, axis=-1, keepdims=True))
+        * attn_scale
+    ).astype(bf16)
+    grad_mixed_own = jnp.dot(grad_attn, full_out.T, preferred_element_type=f32).astype(bf16)
+    grad_mixed = lax.all_to_all(
+        jnp.transpose(grad_mixed_own.reshape(rows, 8, cols), (1, 0, 2)), seq_axes, 0, 0, tiled=True
+    ).reshape(split)
+    grad_attn_all = lax.all_gather(grad_attn, seq_axes, axis=0, tiled=True)
+    wgrad_output = jnp.dot(mixed.T, grad_attn_all, preferred_element_type=f32)
+    wgrad_output = wgrad_output.reshape(4, -1, width).astype(bf16)
+    wgrad_output = scatter_clip_low(clip_relative(wgrad_output.reshape(2, 2, -1, width)))
+    wgrad_output = lax.ppermute(
+        wgrad_output,
+        all_axes,
+        [(c * 8 + s, 4 * s + c) for c in range(4) for s in range(8)],
+    ).astype(f32)
+
+    grad_float = grad_mixed.astype(f32)
+    gate_sum = jnp.sum(grad_float * cross_out, axis=(0, 2)) * (1.0 - tanh_gate * tanh_gate)
+    text_grad = (
+        jnp.einsum("qhd,khd->hqk", grad_mixed, text_values, preferred_element_type=f32)
+        * tanh_gate[:, None, None]
+    )
+    text_center = jnp.sum(text_weights * text_grad, axis=-1, keepdims=True)
+    grad_text_scores = (text_weights * (text_grad - text_center)).astype(bf16)
+    grad_text_keys = (
+        jnp.einsum("hqk,qhd->khd", grad_text_scores, queries, preferred_element_type=f32)
+        * score_scale
+    ).reshape(text_total, cols)
+    grad_text_values = (
+        jnp.einsum("hqk,qhd->khd", text_low, grad_mixed, preferred_element_type=f32)
+        * tanh_gate[None, :, None]
+    ).reshape(text_total, cols)
+    grad_queries = jnp.einsum(
+        "hqk,khd->qhd", grad_text_scores, text_keys, preferred_element_type=f32
+    )
+    sum_six = jnp.sum(grad_text_keys * text_key_normed, axis=0)
+    grad_in = grad_text_keys * gain_text
+    text_mean = sum_seq(jnp.sum(grad_in * text_key_normed, axis=1)) / width
+    grad_text_pre = (grad_in - text_key_normed * text_mean[:, None]) * text_scale
+    grad_text_proj = jnp.concatenate([grad_text_pre, grad_text_values], axis=1).astype(bf16)
+    text_seq = gather_seq(grad_text_proj).reshape(8, text_total, 2 * cols)
+    text_all = jnp.concatenate([text_seq, flip(text_seq, "core")], axis=1)
+    text_all = jnp.concatenate([text_all, flip(text_all, "y")], axis=1)
+    wgrad_caption = jnp.einsum("tk,stn->skn", cap_all, text_all, preferred_element_type=f32)
+    wgrad_caption = jnp.transpose(
+        to_absolute(wgrad_caption.reshape(4, 2, cap_cols, 2, cols)), (2, 3, 0, 1, 4)
+    ).reshape(cap_cols, 2 * width)
+    grad_caption = jnp.einsum("stn,skn->tk", text_all, cap_weight, preferred_element_type=f32)
+    grad_caption = clip_relative(grad_caption.reshape(2, 2, text_total, cap_cols))
+    grad_caption = lax.all_to_all(
+        grad_caption.reshape(32, text_rows, cap_cols), all_axes, 0, 0, tiled=True
+    )
+    grad_caption = jnp.transpose(grad_caption, (1, 0, 2)).reshape(1, text_rows, 32 * cap_cols)
+
+    delta = jnp.sum(grad_float * self_out, axis=-1).T
+    grad_values = jnp.einsum("hqk,qhd->khd", probs_low, grad_mixed, preferred_element_type=f32)
+    grad_probs = jnp.einsum("qhd,khd->hqk", grad_mixed, values, preferred_element_type=f32)
+    grad_scores = (probs * (grad_probs - delta[..., None])).astype(bf16)
+    grad_keys = (
+        jnp.einsum("hqk,qhd->khd", grad_scores, queries, preferred_element_type=f32) * score_scale
+    )
+    grad_queries = (
+        grad_queries
+        + jnp.einsum("hqk,khd->qhd", grad_scores, key_rows, preferred_element_type=f32)
+    ) * score_scale
+    grad_query_rot = rotate(grad_queries, cosine, -sine_table).reshape(total, cols)
+    grad_key_rot = rotate(grad_keys, cosine, -sine_table).reshape(total, cols)
+    sum_four = jnp.sum(grad_query_rot * query_normed, axis=0)
+    sum_five = jnp.sum(grad_key_rot * key_normed, axis=0)
+    query_in = grad_query_rot * gain_query
+    key_in = grad_key_rot * gain_key
+    means = sum_seq(
+        jnp.concatenate(
+            [jnp.sum(query_in * query_normed, axis=1), jnp.sum(key_in * key_normed, axis=1)]
+        )
+    ) / width
+    grad_query_pre = (query_in - query_normed * means[:total, None]) * query_scale
+    grad_key_pre = (key_in - key_normed * means[total:, None]) * key_scale
+    grad_projected = jnp.concatenate(
+        [grad_query_pre, grad_key_pre, grad_values.reshape(total, cols)], axis=1
+    ).astype(bf16)
+    grad_projected = to_relative(grad_projected.reshape(4, 2, rows, -1)).reshape(total, -1)
+    grad_normed = scatter_seq(jnp.dot(grad_projected, own_attn.T, preferred_element_type=f32))
+    wgrad_attention = jnp.dot(normed_all.T, grad_projected, preferred_element_type=f32)
+    wgrad_attention = scatter_clip_low(
+        clip_relative(wgrad_attention.astype(bf16).reshape(2, 2, width // 4, -1))
+    )
+    wgrad_attention = lax.all_to_all(
+        wgrad_attention.reshape(8, -1, 3 * cols), seq_axes, 0, 0, tiled=True
+    )
+    wgrad_attention = (
+        jnp.transpose(wgrad_attention.reshape(8, -1, 3, cols), (1, 2, 0, 3))
+        .reshape(-1, 3 * width)
+        .astype(f32)
+    )
+    sum_zero = jnp.sum(grad_normed * token_normed, axis=0)
+    grad_in = grad_normed * gain_rows[0] * (1.0 + scale_attn)
+    grad_tokens = (
+        grad_residual
+        + (grad_in - token_normed * jnp.mean(grad_in * token_normed, axis=-1, keepdims=True))
+        * token_scale
+    )
+
+    wide = lax.dynamic_update_slice(
+        jnp.zeros((3, width), f32),
+        jnp.stack([sum_four, sum_five, sum_six]),
+        (0, seq_at * cols),
+    )
+    gate_wide = lax.dynamic_update_slice(
+        jnp.zeros((128,), f32), gate_sum, (seq_at * own_heads,)
+    )
+    sums = sum_seq(
+        jnp.concatenate([sum_zero, sum_one, sum_two, sum_three, wide.reshape(-1), gate_wide])
+    )
+    sum_zero, sum_one, sum_two, sum_three = sums[: 4 * width].reshape(4, width)
+    grad_mod_own = jnp.concatenate(
+        [
+            gain_rows[0] * sum_zero,
+            gain_rows[1] * sum_one * (1.0 - gate_attn * gate_attn),
+            gain_rows[2] * sum_two,
+            gain_rows[3] * sum_three * (1.0 - gate_ffn * gate_ffn),
+        ]
+    )
+    shared = jnp.concatenate(
+        [
+            (1.0 + scale_attn) * sum_zero,
+            gate_attn * sum_one,
+            (1.0 + scale_ffn) * sum_two,
+            gate_ffn * sum_three,
+            sums[4 * width :],
+        ]
+    )
+    gathered = gather_clip(jnp.concatenate([grad_mod_own, shared]))
+    grad_mod_row = gathered[:, : 4 * width]
+    shared = (gathered[0] + gathered[1] + gathered[2] + gathered[3])[4 * width :]
+    gain_grads = lax.dynamic_slice(
+        shared[: 7 * width].reshape(7, width), (0, owner * gain_cols), (7, gain_cols)
+    )
+    grad_gate_total = shared[7 * width : 7 * width + heads]
+    bias_grad = lax.dynamic_slice(
+        jnp.sum(grad_mod_row, axis=0), (owner * bias_len,), (bias_len,)
+    )
+    wgrad_modulation = jnp.dot(cond_own.astype(f32).T, grad_mod_row, precision=highest)
+    cond_back = jnp.dot(grad_mod_row, w_modulation.astype(f32).T, precision=highest)
+    cond_wide = lax.dynamic_update_slice(
+        jnp.zeros((4, cond_float.shape[0]), f32), cond_back, (0, owner * cond_rows)
+    )
+    cond_back = sum_seq(scatter_clip(cond_wide))
+    cond_sigmoid = jax.nn.sigmoid(cond_float)
+    grad_condition = cond_back * cond_sigmoid * (1.0 + cond_float * (1.0 - cond_sigmoid))
+
+    return (
+        block_out[None],
+        grad_tokens[None],
+        grad_caption,
+        grad_condition[None],
+        wgrad_modulation,
+        bias_grad,
+        wgrad_attention,
+        wgrad_output,
+        wgrad_caption,
+        gain_grads,
+        grad_gate_total,
+        wgrad_gateup,
+        wgrad_down,
+    )
+
+
+def scatter_clip_low(value):
+    pair = value[0].astype(f32) + flip(value[1], "y").astype(f32)
+    return (pair[0] + flip(pair[1].astype(bf16), "core").astype(f32)).astype(bf16)
+
+
+def specs(clip, seq):
+    both = clip + seq
+    placed = (
+        P(clip, seq, None),
+        P(clip, seq, None),
+        P(clip, None),
+        P(clip),
+        P(clip, None),
+        P(clip, None),
+        P(both, None),
+        P(both),
+        P(both, None),
+        P(both, None),
+        P(both, None),
+        P(None, both),
+        P(),
+        P(both, None),
+        P(both, None),
+        P(clip, seq, None),
+    )
+    given = (
+        P(clip, seq, None),
+        P(clip, seq, None),
+        P(clip, seq, None),
+        P(clip, None),
+        P(both, None),
+        P(both),
+        P(both, None),
+        P(both, None),
+        P(both, None),
+        P(None, both),
+        P(),
+        P(both, None),
+        P(both, None),
+    )
+    return placed, given
+
+
 def solution(mesh):
-    placed = (
-        P("clip", "seq", None),
-        P("clip", "seq", None),
-        P("clip", None),
-        P("clip"),
-        P("clip", None),
-        P("clip", None),
-        P(("clip", "seq"), None),
-        P(("clip", "seq")),
-        P(("clip", "seq"), None),
-        P(("clip", "seq"), None),
-        P(("clip", "seq"), None),
-        P(None, ("clip", "seq")),
-        P(),
-        P(("clip", "seq"), None),
-        P(("clip", "seq"), None),
-        P("clip", "seq", None),
-    )
-    return jax.shard_map(
-        local,
-        mesh=mesh,
-        in_specs=placed,
-        out_specs=(
-            P("clip", "seq", None),
-            P("clip", "seq", None),
-            P("clip", "seq", None),
-            P("clip", None),
-            P(("clip", "seq"), None),
-            P(("clip", "seq")),
-            P(("clip", "seq"), None),
-            P(("clip", "seq"), None),
-            P(("clip", "seq"), None),
-            P(None, ("clip", "seq")),
-            P(),
-            P(("clip", "seq"), None),
-            P(("clip", "seq"), None),
-        ),
-        check_vma=False,
-    )
+    if dict(mesh.shape) == {"clip": 4, "seq": 8}:
+        grid = Mesh(mesh.devices.reshape(2, 2, 4, 2), ("y", "core", "z", "x"))
+        placed, given = specs(("y", "core"), ("z", "x"))
+        return jax.shard_map(
+            local_fast, mesh=grid, in_specs=placed, out_specs=given, check_vma=False
+        )
+    placed, given = specs(("clip",), ("seq",))
+    return jax.shard_map(local, mesh=mesh, in_specs=placed, out_specs=given, check_vma=False)

time: 2520 us -> 857 us (0.34)
  waiting for transfers between devices: 1850 us -> 252 us
  blocking collectives: 297 us -> 26.4 us
  starting transfers between devices: 1.66 us -> 166 us
  matrix products: 242 us -> 96.6 us
  local copies, waits for them, and re-layouts: 47.9 us -> 163 us
  other arithmetic: 51.3 us -> 119 us
    reduce_scatter x13 -> x1, waiting for transfers between devices: 1060 us -> 0.01 us  [local_fast(): lax.psum_scatter(wgrad_down.astype(bf16), 'z', scatter_dimension=0, tiled...]
    all_gather x10 -> x4, waiting for transfers between devices: 670 us -> 18.1 us  [the longest x1 18.1 us: local_fast(): own_down = lax.all_gather(w_down, 'z', axis=0, tiled=True)]
    ppermute x0 -> x89, waiting for transfers between devices: none -> 210 us  [the longest x52 102 us: flip(): return lax.ppermute(value, axis, [(0, 1), (1, 0)])]
    all_gather x5 -> x0, blocking collectives: 172 us -> none  [the longest x1 63.7 us: local(): lax.all_gather(norm_gains, ('clip', 'seq'), axis=1, tiled=True)]
    dot_general x36 -> x29, matrix products: 240 us -> 93.4 us  [the longest x1 8.35 us: local_fast(): jnp.einsum('hqk,qhd->khd', probs_low, grad_mixed, preferred_element_type=...]
    ppermute x0 -> x89, starting transfers between devices: none -> 129 us  [the longest x52 68.5 us: flip(): return lax.ppermute(value, axis, [(0, 1), (1, 0)])]
    unnamed x29 -> x7, waiting for transfers between devices: 124 us -> 0.77 us
    unnamed x3 -> x0, blocking collectives: 72.1 us -> none
  transfers between devices with their start and end apart: 26 -> 102, of which waited for: 21 -> 42; matrix products, arithmetic and copies ran while one was open for 11% -> 40% of each run, Pallas kernels for 0% -> 0%
where the time goes in v1:
time: 857 us; the launch traced here: 843 us
  waiting for transfers between devices  252 us (29%)
  starting transfers between devices  166 us (19%)
  local copies, waits for them, and re-layouts  163 us (19%)
  other arithmetic  119 us (14%)
  matrix products  96.6 us (11%)
  blocking collectives  26.4 us (3%)
  between operations  20.4 us (2%)
    ppermute x52, waiting for transfers between devices, flip(): return lax.ppermute(value, axis, [(0, 1), (1, 0)])  102 us
    ppermute x24, waiting for transfers between devices, from_ahead(): lax.ppermute(value, axis, [((i + step) % count, i) for i in range(count)])  87.9 us
    ppermute x52, starting transfers between devices, flip(): return lax.ppermute(value, axis, [(0, 1), (1, 0)])  68.5 us
    ppermute x24, starting transfers between devices, from_ahead(): lax.ppermute(value, axis, [((i + step) % count, i) for i in range(count)])  42.2 us
    unnamed x299, local copies, waits for them, and re-layouts  41.1 us
    all_to_all x1, blocking collectives, local_fast(): lax.all_to_all(mixed.reshape(8, rows, cols), seq_axes, 0, 0, tiled=True)  26.4 us
    all_to_all x1, waiting for transfers between devices, local_fast(): lax.all_to_all(jnp.transpose(grad_mixed_own.reshape(rows, 8, cols), (1, 0...  18.8 us
    all_gather x1, waiting for transfers between devices, local_fast(): own_down = lax.all_gather(w_down, 'z', axis=0, tiled=True)  18.1 us
  transfers between devices with their start and end apart: 102, of which 42 were waited for; matrix products, arithmetic and copies ran while one was open for 40% of the time, Pallas kernels for 0%

profile of v1, /device:TPU:1, one launch (start us, length us, event | category | flops | bytes accessed | tf_op | source)
XLA Modules:
  0.0 842.6 jit_solution(5336743069575233486)
XLA Ops:
  115.0 8.2 all-to-all-start.3
  152.1 12.2 %collective-permute-done.16 = bf16[2,384,576]{1,2,0:T(8,128)(2,1)S(1)} collective-permute-done((bf16[2,384,576]{1,2,0:T(8,128)(2,1)}, bf16[2,384,576]{1,2,0:T(8,128)(2,1)S(1)}, u32[]{:S(2)}, u32[]{:S(2)}) %collective-permute-start.16) | collective-permute-done | bytes 884768 | tf_op jit(solution)/shard_map/ppermute | solution.py:525
  172.5 4.5 fusion.18
  199.2 11.7 %collective-permute-done.20 = bf16[2,32,384]{1,2,0:T(8,128)(2,1)S(1)} collective-permute-done((bf16[2,32,384]{1,2,0:T(8,128)(2,1)S(1)}, bf16[2,32,384]{1,2,0:T(8,128)(2,1)S(1)}, u32[]{:S(2)}, u32[]{:S(2)}) %collective-permute-start.20) | collective-permute-done | bytes 49184 | tf_op jit(solution)/shard_map/ppermute | solution.py:530
  259.5 8.0 add_convert_fusion
  268.3 26.4 %all_to_all.40 = bf16[8,128,192]{1,2,0:T(8,128)(2,1)S(1)} all-to-all(bf16[8,128,192]{1,2,0:T(8,128)(2,1)S(1)} %copy.221), channel_id=1, replica_groups=mesh['y'=2,'core'=2,'z'=4,'x'=2] {'z','x'}, dimensions={0} | all-to-all | bytes 786432 | tf_op jit(solution)/shard_map/all_to_all | solution.py:784
  302.4 4.5 collective-permute-done.31
  317.0 6.4 collective-permute-start.34
  329.6 6.4 fusion.154
  339.6 18.1 %all-gather.9.cloned.1.call-done = bf16[512,1536]{1,0:T(8,128)(2,1)} async-done(((bf16[128,1536]{1,0:T(8,128)(2,1)}), bf16[512,1536]{1,0:T(8,128)(2,1)}) %all-gather.9.cloned.1.call-update) | async-done | bytes 1572880 | tf_op jit(solution)/shard_map/all_gather | solution.py:720
  368.5 7.9 collective-permute-done.37
  387.5 5.6 collective-permute-done.41
  399.3 5.8 collective-permute-start.44
  419.2 6.0 convolution_convert_fusion
  425.3 4.7 fusion.135
  435.8 5.7 collective-permute-done.47
  466.6 18.8 %all-to-all-done.4 = bf16[8,128,192]{1,2,0:T(8,128)(2,1)S(1)} async-done(((bf16[8,128,192]{1,2,0:T(8,128)(2,1)}), bf16[8,128,192]{1,2,0:T(8,128)(2,1)S(1)}, u32[]{:S(2)}, u32[]{:S(2)}) %all-to-all-start.4) | async-done | bytes 393248 | tf_op jit(solution)/shard_map/all_to_all | solution.py:857
  490.4 8.3 fusion.30
  535.3 6.7 collective-permute-done.51
  556.7 4.8 fusion.153
  570.2 5.5 convolution_convert_fusion.1
  588.2 13.6 %collective-permute-done.71 = bf16[64,384]{0,1:T(8,128)(2,1)S(1)} collective-permute-done((bf16[64,384]{0,1:T(8,128)(2,1)S(1)}, bf16[64,384]{0,1:T(8,128)(2,1)S(1)}, u32[]{:S(2)}, u32[]{:S(2)}) %collective-permute-start.71) | collective-permute-done | bytes 49184 | tf_op jit(solution)/shard_map/ppermute | solution.py:530
  601.8 13.7 %collective-permute-start.70 = (bf16[64,384]{0,1:T(8,128)(2,1)S(1)}, bf16[64,384]{0,1:T(8,128)(2,1)S(1)}, u32[]{:S(2)}, u32[]{:S(2)}) collective-permute-start(bf16[64,384]{0,1:T(8,128)(2,1)S(1)} %pad_maximum_fusion.30), channel_id=1, source_target_pairs={{4,0},{6,2},{0,4},{2,6},{5,1},{7,3},{1,5},{3,7},{12,8},{14,10},{8,... | collective-permute-start | bytes 147464 | tf_op jit(solution)/shard_map/ppermute | solution.py:530
  615.6 4.9 collective-permute-done.70
  627.1 6.0 collective-permute-done.65
  636.6 5.9 all-to-all-start.7
  654.8 16.7 %collective-permute-done.58 = bf16[96,1536]{1,0:T(8,128)(2,1)S(1)} collective-permute-done((bf16[96,1536]{1,0:T(8,128)(2,1)S(1)}, bf16[96,1536]{1,0:T(8,128)(2,1)S(1)}, u32[]{:S(2)}, u32[]{:S(2)}) %collective-permute-start.58) | collective-permute-done | bytes 294944 | tf_op jit(solution)/shard_map/ppermute | solution.py:530
  671.5 28.7 %collective-permute-done.59 = bf16[96,1536]{1,0:T(8,128)(2,1)S(1)} collective-permute-done((bf16[96,1536]{1,0:T(8,128)(2,1)S(1)}, bf16[96,1536]{1,0:T(8,128)(2,1)S(1)}, u32[]{:S(2)}, u32[]{:S(2)}) %collective-permute-start.59) | collective-permute-done | bytes 294944 | tf_op jit(solution)/shard_map/ppermute | solution.py:530
  725.3 32.1 %collective-permute-done.78 = f32[2,17024]{1,0:T(2,128)S(1)} collective-permute-done((f32[2,17024]{1,0:T(2,128)S(1)}, f32[2,17024]{1,0:T(2,128)S(1)}, u32[]{:S(2)}, u32[]{:S(2)}) %collective-permute-start.78) | collective-permute-done | bytes 136224 | tf_op jit(solution)/shard_map/ppermute | solution.py:525
  761.8 6.1 all-to-all-start.6
  803.5 5.7 collective-permute-done.86
  828.9 4.7 collective-permute-done.88
  (787 shorter events, 497.8 us)
Async XLA Ops:
  9.0 88.3 %collective-permute-start.9 = (bf16[96,1536]{1,0:T(8,128)(2,1)}, bf16[96,1536]{1,0:T(8,128)(2,1)}, u32[]{:S(2)}, u32[]{:S(2)}) collective-permute-start(bf16[96,1536]{1,0:T(8,128)(2,1)} %slice_bitcast_fusion.17), channel_id=1, source_target_pairs={{2,0},{4,2},{6,4},{0,6},{3,1},{5,3},{7,5},{1,7},{10,8},{12,10},{14... | collective-permute-start | bytes 884744 | tf_op jit(solution)/shard_map/ppermute | solution.py:530
  13.1 86.5 %collective-permute-start.10 = (bf16[96,1536]{1,0:T(8,128)(2,1)}, bf16[96,1536]{1,0:T(8,128)(2,1)}, u32[]{:S(2)}, u32[]{:S(2)}) collective-permute-start(bf16[96,1536]{1,0:T(8,128)(2,1)} %slice_bitcast_fusion.17), channel_id=1, source_target_pairs={{4,0},{6,2},{0,4},{2,6},{5,1},{7,3},{1,5},{3,7},{12,8},{14,10},{8,... | collective-permute-start | bytes 884744 | tf_op jit(solution)/shard_map/ppermute | solution.py:530
  13.1 86.5 %collective-permute-start.11 = (bf16[96,1536]{1,0:T(8,128)(2,1)}, bf16[96,1536]{1,0:T(8,128)(2,1)}, u32[]{:S(2)}, u32[]{:S(2)}) collective-permute-start(bf16[96,1536]{1,0:T(8,128)(2,1)} %slice_bitcast_fusion.17), channel_id=1, source_target_pairs={{6,0},{0,2},{2,4},{4,6},{7,1},{1,3},{3,5},{5,7},{14,8},{8,10},{10,... | collective-permute-start | bytes 884744 | tf_op jit(solution)/shard_map/ppermute | solution.py:530
  14.8 27.0 %collective-permute-start = (bf16[1024]{0:T(1024)(128)(2,1)}, bf16[1024]{0:T(1024)(128)(2,1)S(1)}, u32[]{:S(2)}, u32[]{:S(2)}) collective-permute-start(bf16[1024]{0:T(1024)(128)(2,1)} %multiply_convert_fusion.11), channel_id=1, source_target_pairs={{0,8},{8,0},{1,9},{9,1},{2,10},{10,2},{3,11},{11,3},{4,12},{12,4},... | collective-permute-start | bytes 6152 | tf_op jit(solution)/shard_map/ppermute | solution.py:525
  16.4 90.8 %collective-permute-start.7 = (bf16[128,1536]{1,0:T(8,128)(2,1)}, bf16[128,1536]{1,0:T(8,128)(2,1)}, u32[]{:S(2)}, u32[]{:S(2)}) collective-permute-start(bf16[128,1536]{1,0:T(8,128)(2,1)} %bitcast.354), channel_id=1, source_target_pairs={{0,1},{1,0},{2,3},{3,2},{4,5},{5,4},{6,7},{7,6},{8,9},{9,8},{10,11... | collective-permute-start | bytes 1179656 | tf_op jit(solution)/shard_map/ppermute | solution.py:525
  19.2 67.1 %all-to-all-start.1 = ((bf16[32,16,128]{2,1,0:T(8,128)(2,1)}), bf16[32,16,128]{2,1,0:T(8,128)(2,1)}, u32[]{:S(2)}, u32[]{:S(2)}) async-start(bf16[32,16,128]{2,1,0:T(8,128)(2,1)} %bitcast.347), calls=%async_computation.1 | async-start | bytes 262144 | tf_op jit(solution)/shard_map/all_to_all | solution.py:725
  23.4 271.3 %all-gather.5.cloned.1.call-start = ((), (), s32[]{:S(2)}) async-start(), calls=%async_computation.9 | async-start | bytes 4866048 | tf_op jit(solution)/shard_map/all_gather | solution.py:717
  86.3 28.7 %all-to-all-start = ((bf16[8,48,576]{2,1,0:T(8,128)(2,1)}), bf16[8,48,576]{2,1,0:T(8,128)(2,1)}, u32[]{:S(2)}, u32[]{:S(2)}) async-start(bf16[8,48,576]{2,1,0:T(8,128)(2,1)} %reshape.569), calls=%async_computation | async-start | bytes 983040 | tf_op jit(solution)/shard_map/all_to_all | solution.py:674
  95.2 53.8 %collective-permute-start.17 = (bf16[2,128,8,384]{3,1,2,0:T(8,128)(2,1)}, bf16[2,128,8,384]{3,1,2,0:T(8,128)(2,1)}, u32[]{:S(2)}, u32[]{:S(2)}) collective-permute-start(bf16[2,128,8,384]{3,1,2,0:T(8,128)(2,1)} %slice.712), channel_id=1, source_target_pairs={{0,16},{16,0},{1,17},{17,1},{2,18},{18,2},{3,19},{19,3},{4,20},{20... | collective-permute-start | bytes 4718600 | tf_op jit(solution)/shard_map/ppermute | solution.py:525
  115.0 125.5 %all-to-all-start.3 = ((bf16[8,48,1024]{2,1,0:T(8,128)(2,1)}), bf16[8,48,1024]{2,1,0:T(8,128)(2,1)}, u32[]{:S(2)}, u32[]{:S(2)}) async-start(bf16[8,48,1024]{2,1,0:T(8,128)(2,1)} %reshape.582), calls=%async_computation.3 | async-start | bytes 1572864 | tf_op jit(solution)/shard_map/all_to_all | solution.py:715
  123.2 206.4 %all-gather.7.cloned.1.call-start = ((), (), s32[]{:S(2)}) async-start(), calls=%async_computation.10 | async-start | bytes 3932160 | tf_op jit(solution)/shard_map/all_gather | solution.py:718
  151.0 33.3 %collective-permute-start.18 = (bf16[128,8,384]{2,0,1:T(8,128)(2,1)S(1)}, bf16[128,8,384]{2,0,1:T(8,128)(2,1)}, u32[]{:S(2)}, u32[]{:S(2)}) collective-permute-start(bf16[128,8,384]{2,0,1:T(8,128)(2,1)S(1)} %fusion.60), channel_id=1, source_target_pairs={{0,8},{8,0},{1,9},{9,1},{2,10},{10,2},{3,11},{11,3},{4,12},{12,4},... | collective-permute-start | bytes 2359304 | tf_op jit(solution)/shard_map/ppermute | solution.py:525
  240.5 117.2 %all-gather.9.cloned.1.call-start = ((), (), s32[]{:S(2)}) async-start(), calls=%async_computation.11 | async-start | bytes 1966080 | tf_op jit(solution)/shard_map/all_gather | solution.py:720
  323.5 310.3 %all-reduce.3.cloned.1.call-start = ((), (), s32[]{:S(2)}) async-start(), calls=%async_computation.14 | async-start | bytes 6291456
  425.2 217.3 %reduce-scatter.5.cloned.1.call-start = ((), (), s32[]{:S(2)}) async-start(), calls=%async_computation.13 | async-start | bytes 1966080 | tf_op jit(solution)/shard_map/reduce_scatter | solution.py:825
  463.7 336.3 %all-gather.11.cloned.1.call-start = ((), (), s32[]{:S(2)}) async-start(), calls=%async_computation.12 | async-start | bytes 3538944 | tf_op jit(solution)/shard_map/all_gather | solution.py:860
  528.6 54.0 %collective-permute-start.66 = (bf16[96,384]{0,1:T(8,128)(2,1)}, bf16[96,384]{0,1:T(8,128)(2,1)}, u32[]{:S(2)}, u32[]{:S(2)}) collective-permute-start(bf16[96,384]{0,1:T(8,128)(2,1)} %fusion.90), channel_id=1, source_target_pairs={{2,0},{4,2},{6,4},{0,6},{3,1},{5,3},{7,5},{1,7},{10,8},{12,10},{14... | collective-permute-start | bytes 221192 | tf_op jit(solution)/shard_map/ppermute | solution.py:530
  530.4 52.7 %collective-permute-start.67 = (bf16[96,384]{0,1:T(8,128)(2,1)}, bf16[96,384]{0,1:T(8,128)(2,1)}, u32[]{:S(2)}, u32[]{:S(2)}) collective-permute-start(bf16[96,384]{0,1:T(8,128)(2,1)} %fusion.90), channel_id=1, source_target_pairs={{4,0},{6,2},{0,4},{2,6},{5,1},{7,3},{1,5},{3,7},{12,8},{14,10},{8,... | collective-permute-start | bytes 221192 | tf_op jit(solution)/shard_map/ppermute | solution.py:530
  530.7 54.3 %collective-permute-start.68 = (bf16[96,384]{0,1:T(8,128)(2,1)}, bf16[96,384]{0,1:T(8,128)(2,1)}, u32[]{:S(2)}, u32[]{:S(2)}) collective-permute-start(bf16[96,384]{0,1:T(8,128)(2,1)} %fusion.90), channel_id=1, source_target_pairs={{6,0},{0,2},{2,4},{4,6},{7,1},{1,3},{3,5},{5,7},{14,8},{8,10},{10,... | collective-permute-start | bytes 221192 | tf_op jit(solution)/shard_map/ppermute | solution.py:530
  546.0 35.6 %collective-permute-start.64 = (bf16[128,384]{0,1:T(8,128)(2,1)}, bf16[128,384]{0,1:T(8,128)(2,1)}, u32[]{:S(2)}, u32[]{:S(2)}) collective-permute-start(bf16[128,384]{0,1:T(8,128)(2,1)} %pad_maximum_fusion.25), channel_id=1, source_target_pairs={{0,1},{1,0},{2,3},{3,2},{4,5},{5,4},{6,7},{7,6},{8,9},{9,8},{10,11... | collective-permute-start | bytes 294920 | tf_op jit(solution)/shard_map/ppermute | solution.py:525
  564.6 58.3 %collective-permute-start.53 = (bf16[2,32,1536]{2,1,0:T(8,128)(2,1)S(1)}, bf16[2,32,1536]{2,1,0:T(8,128)(2,1)}, u32[]{:S(2)}, u32[]{:S(2)}) collective-permute-start(bf16[2,32,1536]{2,1,0:T(8,128)(2,1)S(1)} %get-tuple-element.109), channel_id=1, source_target_pairs={{2,0},{4,2},{6,4},{0,6},{3,1},{5,3},{7,5},{1,7},{10,8},{12,10},{14... | collective-permute-start | bytes 589832 | tf_op jit(solution)/shard_map/ppermute | solution.py:530
  581.5 42.7 %collective-permute-start.54 = (bf16[2,32,1536]{2,1,0:T(8,128)(2,1)}, bf16[2,32,1536]{2,1,0:T(8,128)(2,1)S(1)}, u32[]{:S(2)}, u32[]{:S(2)}) collective-permute-start(bf16[2,32,1536]{2,1,0:T(8,128)(2,1)} %get-tuple-element.111), channel_id=1, source_target_pairs={{4,0},{6,2},{0,4},{2,6},{5,1},{7,3},{1,5},{3,7},{12,8},{14,10},{8,... | collective-permute-start | bytes 589832 | tf_op jit(solution)/shard_map/ppermute | solution.py:530
  582.6 41.6 %collective-permute-start.55 = (bf16[2,32,1536]{2,1,0:T(8,128)(2,1)}, bf16[2,32,1536]{2,1,0:T(8,128)(2,1)S(1)}, u32[]{:S(2)}, u32[]{:S(2)}) collective-permute-start(bf16[2,32,1536]{2,1,0:T(8,128)(2,1)} %get-tuple-element.110), channel_id=1, source_target_pairs={{6,0},{0,2},{2,4},{4,6},{7,1},{1,3},{3,5},{5,7},{14,8},{8,10},{10,... | collective-permute-start | bytes 589832 | tf_op jit(solution)/shard_map/ppermute | solution.py:530
  583.0 67.8 %collective-permute-start.57 = (bf16[3,96,1536]{2,1,0:T(8,128)(2,1)}, bf16[3,96,1536]{2,1,0:T(8,128)(2,1)}, u32[]{:S(2)}, u32[]{:S(2)}) collective-permute-start(bf16[3,96,1536]{2,1,0:T(8,128)(2,1)} %slice_bitcast_fusion.5), channel_id=1, source_target_pairs={{0,1},{1,0},{2,3},{3,2},{4,5},{5,4},{6,7},{7,6},{8,9},{9,8},{10,11... | collective-permute-start | bytes 2654216 | tf_op jit(solution)/shard_map/ppermute | solution.py:525
  620.6 83.1 %collective-permute-start.84 = (bf16[2,384,576]{1,2,0:T(8,128)(2,1)}, bf16[2,384,576]{1,2,0:T(8,128)(2,1)}, u32[]{:S(2)}, u32[]{:S(2)}) collective-permute-start(bf16[2,384,576]{1,2,0:T(8,128)(2,1)} %slice_bitcast_fusion.3), channel_id=1, source_target_pairs={{0,16},{16,0},{1,17},{17,1},{2,18},{18,2},{3,19},{19,3},{4,20},{20... | collective-permute-start | bytes 2654216 | tf_op jit(solution)/shard_map/ppermute | solution.py:525
  636.6 71.4 %all-to-all-start.7 = ((bf16[8,48,1024]{2,1,0:T(8,128)(2,1)}), bf16[8,48,1024]{2,1,0:T(8,128)(2,1)}, u32[]{:S(2)}, u32[]{:S(2)}) async-start(bf16[8,48,1024]{2,1,0:T(8,128)(2,1)} %bitcast.130), calls=%async_computation.7 | async-start | bytes 1572864 | tf_op jit(solution)/shard_map/all_to_all | solution.py:832
  649.4 66.7 %collective-permute-start.72 = (bf16[8,128,384]{1,2,0:T(8,128)(2,1)S(1)}, bf16[8,128,384]{1,2,0:T(8,128)(2,1)}, u32[]{:S(2)}, u32[]{:S(2)}) collective-permute-start(bf16[8,128,384]{1,2,0:T(8,128)(2,1)S(1)} %copy.240), channel_id=1, source_target_pairs={{0,8},{8,0},{1,9},{9,1},{2,10},{10,2},{3,11},{11,3},{4,12},{12,4},... | collective-permute-start | bytes 2359304 | tf_op jit(solution)/shard_map/ppermute | solution.py:525
  653.3 46.9 %collective-permute-start.59 = (bf16[96,1536]{1,0:T(8,128)(2,1)S(1)}, bf16[96,1536]{1,0:T(8,128)(2,1)S(1)}, u32[]{:S(2)}, u32[]{:S(2)}) collective-permute-start(bf16[96,1536]{1,0:T(8,128)(2,1)S(1)} %get-tuple-element.138), channel_id=1, source_target_pairs={{4,0},{6,2},{0,4},{2,6},{5,1},{7,3},{1,5},{3,7},{12,8},{14,10},{8,... | collective-permute-start | bytes 884744 | tf_op jit(solution)/shard_map/ppermute | solution.py:530
  653.4 46.8 %collective-permute-start.60 = (bf16[96,1536]{1,0:T(8,128)(2,1)S(1)}, bf16[96,1536]{1,0:T(8,128)(2,1)S(1)}, u32[]{:S(2)}, u32[]{:S(2)}) collective-permute-start(bf16[96,1536]{1,0:T(8,128)(2,1)S(1)} %get-tuple-element.137), channel_id=1, source_target_pairs={{6,0},{0,2},{2,4},{4,6},{7,1},{1,3},{3,5},{5,7},{14,8},{8,10},{10,... | collective-permute-start | bytes 884744 | tf_op jit(solution)/shard_map/ppermute | solution.py:530
  707.1 52.3 %collective-permute-start.85 = (bf16[384,576]{0,1:T(8,128)(2,1)}, bf16[384,576]{0,1:T(8,128)(2,1)}, u32[]{:S(2)}, u32[]{:S(2)}) collective-permute-start(bf16[384,576]{0,1:T(8,128)(2,1)} %fusion.69), channel_id=1, source_target_pairs={{0,8},{8,0},{1,9},{9,1},{2,10},{10,2},{3,11},{11,3},{4,12},{12,4},... | collective-permute-start | bytes 1327112 | tf_op jit(solution)/shard_map/ppermute | solution.py:525
  718.5 68.8 %collective-permute-start.73 = (bf16[8,256,384]{1,2,0:T(8,128)(2,1)}, bf16[8,256,384]{1,2,0:T(8,128)(2,1)}, u32[]{:S(2)}, u32[]{:S(2)}) collective-permute-start(bf16[8,256,384]{1,2,0:T(8,128)(2,1)} %pad_maximum_fusion.3), channel_id=1, source_target_pairs={{0,16},{16,0},{1,17},{17,1},{2,18},{18,2},{3,19},{19,3},{4,20},{20... | collective-permute-start | bytes 4718600 | tf_op jit(solution)/shard_map/ppermute | solution.py:525
  722.8 34.6 %collective-permute-start.78 = (f32[2,17024]{1,0:T(2,128)S(1)}, f32[2,17024]{1,0:T(2,128)S(1)}, u32[]{:S(2)}, u32[]{:S(2)}) collective-permute-start(f32[2,17024]{1,0:T(2,128)S(1)} %pad_maximum_fusion.23), channel_id=1, source_target_pairs={{0,16},{16,0},{1,17},{17,1},{2,18},{18,2},{3,19},{19,3},{4,20},{20... | collective-permute-start | bytes 408584 | tf_op jit(solution)/shard_map/ppermute | solution.py:525
  (201 other events, 2427.7 us)
Sparse Core Ops, SparseCore 0:
  27.3 66.8 all-gather.4
  240.6 73.8 all-gather.6
  323.6 34.0 all-gather.8
  425.3 135.4 all-reduce.2
  563.6 46.6 reduce-scatter.4
  612.3 85.2 all-gather.10

commit v2 on v1

--- a/solution.py
+++ b/solution.py
@@ -1,8 +1,11 @@
+import functools
 import math
 
 import jax
 import jax.numpy as jnp
 from jax import lax
+from jax.experimental import pallas as pl
+from jax.experimental.pallas import tpu as pltpu
 from jax.sharding import Mesh
 from jax.sharding import PartitionSpec as P
 
@@ -540,24 +543,8 @@
     return value + swap_z(value, 2)
 
 
-def to_relative(value):
-    value = jnp.where(lax.axis_index("x") == 0, value, value[:, ::-1])
-    return jnp.roll(value, -lax.axis_index("z"), axis=0)
-
-
-def to_absolute(value):
-    value = jnp.where(lax.axis_index("x") == 0, value, value[:, ::-1])
-    return jnp.roll(value, lax.axis_index("z"), axis=0)
-
-
-def clip_relative(value):
-    value = jnp.where(lax.axis_index("y") == 0, value, value[::-1])
-    return jnp.where(lax.axis_index("core") == 0, value, value[:, ::-1])
-
-
 def gather_plane(value):
-    rows = value.shape[0]
-    half = rows // 2
+    half = value.shape[0] // 2
     from_x = flip(value, "x")
     from_y = flip(value, "y")
     far_front = flip(from_y[:half], "x")
@@ -580,40 +567,9 @@
     return own + jnp.concatenate([last_y, last_x])
 
 
-def gather_seq(value):
-    rows = value.shape[0]
-    early = rows // 4
-    rest = rows - early
-    ahead = [from_ahead(value[early:], "z", k) for k in (1, 2, 3)]
-    other = flip(value, "x")
-    both = jnp.concatenate([value[:early], other[:early]], axis=0)
-    early_ahead = [from_ahead(both, "z", k) for k in (1, 2, 3)]
-    other_ahead = flip(jnp.concatenate(ahead, axis=0), "x")
-    pieces = [value, other]
-    for k in range(3):
-        pieces += [
-            early_ahead[k][:early],
-            ahead[k],
-            early_ahead[k][early:],
-            other_ahead[k * rest : (k + 1) * rest],
-        ]
-    return jnp.concatenate(pieces, axis=0)
-
-
-def scatter_seq(value):
-    rows = value.shape[0] // 8
-    early = rows // 4
-    parts = value.reshape(4, 2, rows, value.shape[1])
-    low = parts.astype(bf16)
-    other = flip(low[1:, 1, early:], "x").astype(f32)
-    front = [from_ahead(low[(4 - k) % 4, :, :early], "z", k).astype(f32) for k in (1, 2, 3)]
-    front_sum = parts[0, :, :early] + front[0] + front[1] + front[2]
-    back_sum = (parts[1:, 0, early:] + other).astype(bf16)
-    back = [from_ahead(back_sum[3 - k], "z", k).astype(f32) for k in (1, 2, 3)]
-    last = flip(jnp.concatenate([front_sum[1].astype(bf16), low[0, 1, early:]]), "x").astype(f32)
-    out_front = front_sum[0] + last[:early]
-    out_back = parts[0, 0, early:] + last[early:] + back[0] + back[1] + back[2]
-    return jnp.concatenate([out_front, out_back])
+def gather_clip(value):
+    pair = jnp.stack([value, flip(value, "core")])
+    return jnp.concatenate([pair, flip(pair, "y")])
 
 
 def scatter_clip(value):
@@ -621,13 +577,433 @@
     return pair[0] + flip(pair[1], "core")
 
 
-def gather_clip(value):
-    pair = jnp.stack([value, flip(value, "core")])
-    return jnp.concatenate([pair, flip(pair, "y")])
-
-
 def rms_scale(square_mean):
     return lax.rsqrt(square_mean + epsilon)
+
+
+def on_chip(body, outs, *operands, scalars=0, scratch=()):
+    held = pl.BlockSpec(memory_space=pltpu.SMEM)
+    whole = pl.BlockSpec(memory_space=pltpu.VMEM)
+    return pl.pallas_call(
+        body,
+        out_shape=[jax.ShapeDtypeStruct(shape, kind) for shape, kind in outs],
+        in_specs=[held] * scalars + [whole] * (len(operands) - scalars),
+        out_specs=[whole] * len(outs),
+        scratch_shapes=list(scratch),
+        compiler_params=pltpu.CompilerParams(vmem_limit_bytes=50 * 2**20),
+    )(*operands)
+
+
+def dot(a, b):
+    return jnp.dot(a, b, preferred_element_type=f32)
+
+
+def dot_rows(a, b):
+    return lax.dot_general(a, b, (((1,), (1,)), ((), ())), preferred_element_type=f32)
+
+
+def dot_cols(a, b):
+    return lax.dot_general(a, b, (((0,), (0,)), ((), ())), preferred_element_type=f32)
+
+
+def round_up(value):
+    return -(-value // 128) * 128
+
+
+def prep_body(attn, gateup, cap, attn_out, ffn_out, cap_out):
+    width = attn.shape[1] // 3
+    cols = width // 8
+    pad = attn_out.shape[2] - 3 * cols
+    for s in range(8):
+        parts = [attn[:, p * width + s * cols : p * width + (s + 1) * cols] for p in range(3)]
+        parts.append(jnp.zeros((attn.shape[0], pad), bf16))
+        attn_out[s] = jnp.concatenate(parts, axis=1)
+    own = gateup.shape[1] // 64
+    for g in range(8):
+        for part in range(2):
+            for z in range(4):
+                source = (part * 32 + (g // 2) * 8 + z * 2 + g % 2) * own
+                target = (part * 4 + z) * own
+                ffn_out[g, :, target : target + own] = gateup[:, source : source + own]
+    own = cap_out.shape[2]
+    for o in range(32):
+        cap_out[o] = cap[:, o * own : (o + 1) * own]
+
+
+def caption_slice(weight, s):
+    cols = weight.shape[1] // 16
+    return jnp.concatenate(
+        [weight[:, (p * 8 + s) * cols : (p * 8 + s + 1) * cols] for p in range(2)], axis=1
+    )
+
+
+def caption_body(place, cap, weight, keep_out, send_out):
+    for s in range(8):
+        own = caption_slice(weight, s)
+        for r in range(4):
+            part = dot(cap[place[0] ^ r], own).astype(bf16)
+            if r % 2:
+                send_out[r // 2, s] = part
+            else:
+                keep_out[r // 2, s] = part
+
+
+def qkv_body(
+    place, token, w0, w1, w2, w3, vectors, text, normed_out, proj_out, text_out, stats_out
+):
+    total, width = token.shape
+    step = total // 4
+    block = width // 4
+    cols = width // 8
+    gain, scale = vectors[0:1], vectors[1:2]
+    for b in range(4):
+        at = slice(b * step, (b + 1) * step)
+        value = token[at].astype(f32)
+        inverse = rms_scale(jnp.mean(value * value, axis=1, keepdims=True))
+        normed_out[at] = (value * inverse * gain * (1.0 + scale)).astype(bf16)
+    for b in range(4):
+        at = slice(b * step, (b + 1) * step)
+        part = jnp.zeros((step, w0.shape[1]), f32)
+        for r, weight in enumerate((w0, w1, w2, w3)):
+            from_col = pl.multiple_of((place[0] ^ r) * block, 128)
+            part = part + dot(normed_out[at, pl.ds(from_col, block)], weight[...])
+        proj_out[:, at] = part.T
+    text_sum = text[0].astype(f32)
+    for s in range(1, 8):
+        text_sum = text_sum + text[s].astype(f32)
+    text_out[...] = text_sum.T
+    stats_out[...] = jnp.zeros(stats_out.shape, f32)
+    query, key, caption_key = proj_out[:cols], proj_out[cols : 2 * cols], text_out[:cols]
+    stats_out[0:1, :] = jnp.sum(query * query, axis=0, keepdims=True)
+    stats_out[1:2, :] = jnp.sum(key * key, axis=0, keepdims=True)
+    stats_out[2:3, : text.shape[1]] = jnp.sum(caption_key * caption_key, axis=0, keepdims=True)
+
+
+def turn(value, cosine, sine):
+    half = value.shape[0] // 2
+    front, back = value[:half], value[half:]
+    return jnp.concatenate([front * cosine - back * sine, back * cosine + front * sine], axis=0)
+
+
+def text_softmax(scores, length):
+    place = lax.broadcasted_iota(jnp.int32, scores.shape, 0)
+    scores = jnp.where(place < length, scores, -1e30)
+    shifted = jnp.exp(scores - jnp.max(scores, axis=0, keepdims=True))
+    return shifted / jnp.sum(shifted, axis=0, keepdims=True)
+
+
+def attend_body(
+    heads,
+    gate,
+    length,
+    proj,
+    stats,
+    text,
+    gains,
+    cosine,
+    sine,
+    mixed_out,
+    query_out,
+    key_out,
+    value_out,
+    self_out,
+    cross_out,
+    sum_out,
+    text_key_out,
+    text_value_out,
+):
+    total = proj.shape[1]
+    cols = query_out.shape[0]
+    dim = cols // heads
+    width = cols * 8
+    step = total // 2
+    score_scale = dim ** (-0.5)
+    scales = rms_scale(stats[0:3, :] / width)
+    query_scale, key_scale = scales[0:1], scales[1:2]
+    text_scale = scales[2:3, : text.shape[1]]
+    text_key_out[...] = (text[:cols] * text_scale * gains[:, 2:3]).astype(bf16)
+    text_value_out[...] = text[cols : 2 * cols].astype(bf16)
+    value_out[...] = proj[2 * cols : 3 * cols].astype(bf16)
+    sum_out[...] = jnp.zeros(sum_out.shape, f32)
+    for h in range(heads):
+        at = slice(h * dim, (h + 1) * dim)
+        query = proj[at] * query_scale * gains[at, 0:1]
+        query_out[at] = turn(query, cosine[...], sine[...]).astype(bf16)
+        key = proj[cols + h * dim : cols + (h + 1) * dim] * key_scale * gains[at, 1:2]
+        key_out[at] = turn(key, cosine[...], sine[...]).astype(bf16)
+        key_rows = key_out[at].T
+        text_rows = text_key_out[at].T
+        for b in range(2):
+            to = slice(b * step, (b + 1) * step)
+            block = query_out[at, to]
+            scores = dot(key_rows, block) * score_scale
+            most = jnp.max(scores, axis=0, keepdims=True)
+            weights = jnp.exp(scores - most)
+            whole = jnp.sum(weights, axis=0, keepdims=True)
+            sum_out[h : h + 1, to] = most + jnp.log(whole)
+            own = dot(value_out[at], weights.astype(bf16)) * (1.0 / whole)
+            text_weights = text_softmax(dot(text_rows, block) * score_scale, length[0])
+            cross = dot(text_value_out[at], text_weights.astype(bf16))
+            self_out[at, to] = own
+            cross_out[at, to] = cross
+            mixed = (own + gate[h] * cross).astype(bf16)
+            piece = mixed_out.shape[2]
+            for s in range(step // piece):
+                mixed_out[b * (step // piece) + s, at] = mixed[:, s * piece : (s + 1) * piece]
+
+
+def text_back_body(
+    heads,
+    gate,
+    length,
+    pieces,
+    query,
+    text_key,
+    text_value,
+    cross,
+    text,
+    stats,
+    gains,
+    grad_out,
+    query_out,
+    key_out,
+    value_out,
+    stats_out,
+    gain_out,
+    gate_out,
+):
+    cols, total = query.shape
+    dim = cols // heads
+    width = cols * 8
+    step = total // 2
+    score_scale = dim ** (-0.5)
+    piece = pieces.shape[2]
+    for s in range(pieces.shape[0]):
+        grad_out[:, s * piece : (s + 1) * piece] = pieces[s]
+    gate_out[...] = jnp.zeros(gate_out.shape, f32)
+    for h in range(heads):
+        at = slice(h * dim, (h + 1) * dim)
+        text_rows, value_rows = text_key[at].T, text_value[at].T
+        grad = grad_out[at].astype(f32)
+        gate_sum = jnp.sum(jnp.sum(grad * cross[at], axis=0, keepdims=True), axis=1, keepdims=True)
+        gate_out[h : h + 1, :] = jnp.broadcast_to(
+            gate_sum * (1.0 - gate[h] * gate[h]), (1, gate_out.shape[1])
+        )
+        key_grad = jnp.zeros((dim, text_key.shape[1]), f32)
+        value_grad = jnp.zeros((dim, text_key.shape[1]), f32)
+        for b in range(2):
+            to = slice(b * step, (b + 1) * step)
+            block, back = query[at, to], grad_out[at, to]
+            weights = text_softmax(dot(text_rows, block) * score_scale, length[0])
+            upstream = dot(value_rows, back) * gate[h]
+            center = jnp.sum(weights * upstream, axis=0, keepdims=True)
+            score_grad = (weights * (upstream - center)).astype(bf16)
+            query_out[at, to] = dot(text_key[at], score_grad)
+            key_grad = key_grad + dot_rows(block, score_grad)
+            value_grad = value_grad + dot_rows(back, weights.astype(bf16))
+        key_out[at] = key_grad * score_scale
+        value_out[at] = value_grad * gate[h]
+    text_scale = rms_scale(stats[2:3, : text.shape[1]] / width)
+    normed = text[:cols] * text_scale
+    gain_out[...] = jnp.broadcast_to(
+        jnp.sum(key_out[...] * normed, axis=1, keepdims=True), gain_out.shape
+    )
+    key_out[...] = key_out[...] * gains[:, 2:3]
+    stats_out[...] = jnp.broadcast_to(
+        jnp.sum(key_out[...] * normed, axis=0, keepdims=True), stats_out.shape
+    )
+
+
+def text_proj_back_body(key, value, text, stats, means, grad_out):
+    cols = key.shape[0]
+    width = cols * 8
+    text_scale = rms_scale(stats[2:3, : text.shape[1]] / width)
+    normed = text[:cols] * text_scale
+    before = (key[...] - normed * (means[0:1, :] / width)) * text_scale
+    grad_out[...] = jnp.concatenate([before, value[...]], axis=0).T.astype(bf16)
+
+
+def caption_back_body(cap, grads, weight, weight_out, cap_out):
+    cols = weight.shape[1] // 16
+    for s in range(8):
+        own = caption_slice(weight, s)
+        part = jnp.zeros((cap.shape[2], 2 * cols), f32)
+        for c in range(4):
+            grad = grads[c, s]
+            part = part + dot_cols(cap[c], grad)
+            back = dot_rows(grad, own)
+            if s == 0:
+                cap_out[c] = back
+            else:
+                cap_out[c] = cap_out[c] + back
+        for p in range(2):
+            weight_out[:, (p * 8 + s) * cols : (p * 8 + s + 1) * cols] = part[
+                :, p * cols : (p + 1) * cols
+            ]
+
+
+def attend_back_body(
+    heads,
+    grad,
+    query,
+    key,
+    value,
+    self_out,
+    sums,
+    text_query,
+    proj,
+    stats,
+    gains,
+    cosine,
+    sine,
+    query_in_out,
+    key_in_out,
+    value_grad_out,
+    stats_out,
+    gain_out,
+):
+    cols, total = query.shape
+    dim = cols // heads
+    width = cols * 8
+    step = total // 2
+    score_scale = dim ** (-0.5)
+    scales = rms_scale(stats[0:2, :] / width)
+    stats_out[...] = jnp.zeros(stats_out.shape, f32)
+    gain_out[...] = jnp.zeros(gain_out.shape, f32)
+    query_total = jnp.zeros((1, total), f32)
+    key_total = jnp.zeros((1, total), f32)
+    for h in range(heads):
+        at = slice(h * dim, (h + 1) * dim)
+        key_rows, value_rows = key[at].T, value[at].T
+        delta = jnp.sum(grad[at].astype(f32) * self_out[at], axis=0, keepdims=True)
+        key_grad = jnp.zeros((dim, total), f32)
+        value_grad = jnp.zeros((dim, total), f32)
+        query_parts = []
+        for b in range(2):
+            to = slice(b * step, (b + 1) * step)
+            block, back = query[at, to], grad[at, to]
+            weights = jnp.exp(dot(key_rows, block) * score_scale - sums[h : h + 1, to])
+            value_grad = value_grad + dot_rows(back, weights.astype(bf16))
+            score_grad = (weights * (dot(value_rows, back) - delta[:, to])).astype(bf16)
+            key_grad = key_grad + dot_rows(block, score_grad)
+            query_parts.append(dot(key[at], score_grad))
+        value_grad_out[at] = value_grad.astype(bf16)
+        query_grad = (jnp.concatenate(query_parts, axis=1) + text_query[at]) * score_scale
+        query_grad = turn(query_grad, cosine[...], -sine[...])
+        key_grad = turn(key_grad * score_scale, cosine[...], -sine[...])
+        query_normed = proj[at] * scales[0:1]
+        key_normed = proj[cols + h * dim : cols + (h + 1) * dim] * scales[1:2]
+        gain_out[at, 0:1] = jnp.sum(query_grad * query_normed, axis=1, keepdims=True)
+        gain_out[at, 1:2] = jnp.sum(key_grad * key_normed, axis=1, keepdims=True)
+        query_grad = query_grad * gains[at, 0:1]
+        key_grad = key_grad * gains[at, 1:2]
+        query_in_out[at] = query_grad
+        key_in_out[at] = key_grad
+        query_total = query_total + jnp.sum(query_grad * query_normed, axis=0, keepdims=True)
+        key_total = key_total + jnp.sum(key_grad * key_normed, axis=0, keepdims=True)
+    stats_out[0:1, :] = query_total
+    stats_out[1:2, :] = key_total
+
+
+def project_back_body(
+    place,
+    query_in,
+    key_in,
+    value_grad,
+    proj,
+    stats,
+    means,
+    normed,
+    w0,
+    w1,
+    w2,
+    w3,
+    own_out,
+    keep_out,
+    side_out,
+    front1_out,
+    front2_out,
+    front3_out,
+    near_out,
+    far_out,
+    low,
+    turned,
+):
+    cols, total = query_in.shape
+    width = normed.shape[1]
+    block = width // 4
+    rows = total // 8
+    early = front1_out.shape[1]
+    scales = rms_scale(stats[0:2, :] / width)
+    low[...] = jnp.zeros(low.shape, bf16)
+    low[:cols] = (
+        (query_in[...] - proj[:cols] * scales[0:1] * (means[0:1, :] / width)) * scales[0:1]
+    ).astype(bf16)
+    low[cols : 2 * cols] = (
+        (key_in[...] - proj[cols : 2 * cols] * scales[1:2] * (means[1:2, :] / width)) * scales[1:2]
+    ).astype(bf16)
+    low[2 * cols : 3 * cols] = value_grad[...]
+    turned[...] = low[...].T
+    weights = (w0, w1, w2, w3)
+    fronts = (front1_out, front2_out, front3_out)
+    for k in range(4):
+        for j in range(2):
+            source = (((place[1] + k) % 4) * 2 + (place[2] ^ j)) * rows
+            lines = turned[pl.ds(pl.multiple_of(source, 128), rows), :]
+            for r in range(4):
+                to_col = pl.ds(pl.multiple_of((place[0] ^ r) * block, 128), block)
+                part = dot_rows(lines, weights[r][...]).astype(bf16)
+                if k == 0:
+                    own_out[j, :, to_col] = part
+                else:
+                    fronts[k - 1][j, :, to_col] = part[:early]
+                    if j == 0:
+                        keep_out[k - 1, :, to_col] = part[early:]
+                    else:
+                        side_out[k - 1, :, to_col] = part[early:]
+    for r in range(4):
+        from_col = pl.ds(pl.multiple_of((place[0] ^ r) * block, 128), block)
+        part = dot(low[...], normed[:, from_col]).T.astype(bf16)
+        if r % 2:
+            far_out[r // 2] = part
+        else:
+            near_out[r // 2] = part
+
+
+def attention_grad_body(pieces, grad_out):
+    cols = grad_out.shape[1] // 24
+    for s in range(8):
+        for p in range(3):
+            grad_out[:, (p * 8 + s) * cols : (p * 8 + s + 1) * cols] = pieces[
+                s, :, p * cols : (p + 1) * cols
+            ].astype(f32)
+
+
+def gateup_grad_body(pieces, grad_out):
+    own = grad_out.shape[1] // 64
+    for g in range(8):
+        for part in range(2):
+            for z in range(4):
+                target = (part * 32 + (g // 2) * 8 + z * 2 + g % 2) * own
+                source = (part * 4 + z) * own
+                grad_out[:, target : target + own] = pieces[g, :, source : source + own].astype(f32)
+
+
+def caption_grad_body(pieces, grad_out):
+    own = pieces.shape[2]
+    for o in range(32):
+        grad_out[:, o * own : (o + 1) * own] = pieces[o]
+
+
+def output_grad_body(place, mixed, grad, weight_out):
+    rows = mixed.shape[2]
+    total = None
+    for r in range(8):
+        core, y, x = r // 4, (r // 2) % 2, r % 2
+        source = ((place[3] ^ y) * 2 + (place[4] ^ core)) * 2 + (place[2] ^ x)
+        part = dot(mixed[source], grad[r * rows : (r + 1) * rows])
+        total = part if total is None else total + part
+    weight_out[...] = total.astype(bf16)
 
 
 def local_fast(
@@ -649,8 +1025,7 @@
     cotangent,
 ):
     seq_axes = ("z", "x")
-    clip_axes = ("y", "core")
-    all_axes = clip_axes + seq_axes
+    all_axes = ("y", "core") + seq_axes
     plane_axes = ("y", "core", "x")
     rows, width = tokens.shape[1:]
     total = rows * 8
@@ -658,23 +1033,43 @@
     head_dim = width // heads
     own_heads = heads // 8
     cols = own_heads * head_dim
-    score_scale = head_dim ** (-0.5)
+    wide_cols = round_up(3 * cols)
     text_rows = caption.shape[1]
     text_total = text_rows * 8
+    attn_rows = w_attention.shape[0]
     z_at, x_at = lax.axis_index("z"), lax.axis_index("x")
+    y_at, core_at = lax.axis_index("y"), lax.axis_index("core")
     seq_at = z_at * 2 + x_at
-    owner = (lax.axis_index("y") * 2 + lax.axis_index("core")) * 8 + seq_at
+    clip_at = y_at * 2 + core_at
+    owner = clip_at * 8 + seq_at
+    place = jnp.stack([clip_at, z_at, x_at, y_at, core_at]).astype(jnp.int32)
 
     own_tokens = tokens[0]
-    token_all = gather_seq(own_tokens)
-
-    attn_piece = jnp.transpose(
-        w_attention.reshape(-1, 3, 8, cols), (2, 0, 1, 3)
-    ).reshape(8, -1, 3 * cols)
-    attn_piece = lax.all_to_all(attn_piece, seq_axes, 0, 0, tiled=True)
-    attn_piece = attn_piece.reshape(1, 1, -1, 3 * cols)
-    own_attn = gather_clip(attn_piece[0, 0]).reshape(2, 2, -1, 3 * cols)
-    own_attn = clip_relative(own_attn).reshape(width, 3 * cols)
+    token_all = lax.all_gather(own_tokens, seq_axes, axis=0, tiled=True)
+    full_out = lax.all_gather(w_output, all_axes, axis=0, tiled=True)
+
+    cap_cols = w_caption.shape[0]
+    hidden_own = w_down.shape[0]
+    hidden = 4 * hidden_own
+    attn_piece, ffn_piece, cap_piece = on_chip(
+        prep_body,
+        [
+            ((8, attn_rows, wide_cols), bf16),
+            ((8, w_gateup.shape[0], 8 * hidden_own), bf16),
+            ((32, text_rows, cap_cols), bf16),
+        ],
+        w_attention,
+        w_gateup,
+        caption[0],
+    )
+    cap_all = lax.all_to_all(cap_piece, all_axes, 0, 0, tiled=True).reshape(
+        4, text_total, cap_cols
+    )
+    attn_0 = lax.all_to_all(attn_piece, seq_axes, 0, 0, tiled=True).reshape(-1, wide_cols)
+    attn_2 = flip(attn_0, "y")
+    attn_1 = flip(attn_0, "core")
+    attn_3 = flip(attn_2, "core")
+    attn_parts = (attn_0, attn_1, attn_2, attn_3)
 
     cond_float = condition[0].astype(f32)
     cond_act = jax.nn.silu(cond_float).astype(bf16)
@@ -702,88 +1097,87 @@
     gate_attn = jnp.tanh(modulation[1])
     scale_ffn = modulation[2]
     gate_ffn = jnp.tanh(modulation[3])
-    gain_query = lax.dynamic_slice_in_dim(gain_rows[4], seq_at * cols, cols)
-    gain_key = lax.dynamic_slice_in_dim(gain_rows[5], seq_at * cols, cols)
-    gain_text = lax.dynamic_slice_in_dim(gain_rows[6], seq_at * cols, cols)
+    own_gains = lax.dynamic_slice_in_dim(gain_rows[4:], seq_at * cols, cols, 1).T
     head_low = lax.dynamic_slice_in_dim(head_gate, seq_at * own_heads, own_heads)
     tanh_gate = jnp.tanh(head_low.astype(f32))
 
-    hidden_own = w_down.shape[0]
-    ffn_piece = jnp.transpose(
-        w_gateup.reshape(-1, 2, 2, 2, 4, 2, hidden_own), (2, 3, 5, 0, 1, 4, 6)
-    ).reshape(8, -1, 8 * hidden_own)
     ffn_piece = lax.all_to_all(ffn_piece, plane_axes, 0, 0, tiled=True)
     block = 2 * ffn_piece.shape[1]
-    full_out = lax.all_gather(w_output, all_axes, axis=0, tiled=True)
     own_gateup = lax.all_gather(ffn_piece.reshape(4, block, -1), "z", axis=0)
     own_gateup = jnp.transpose(own_gateup, (1, 0, 2, 3)).reshape(width, -1)
     own_down = lax.all_gather(w_down, "z", axis=0, tiled=True)
-    hidden = 4 * hidden_own
-
-    cap_cols = w_caption.shape[0]
-    cap_piece = jnp.transpose(caption[0].reshape(text_rows, 32, cap_cols), (1, 0, 2))
-    cap_piece = lax.all_to_all(cap_piece, all_axes, 0, 0, tiled=True)
-    cap_all = clip_relative(cap_piece.reshape(2, 2, text_total, cap_cols)).reshape(
-        4 * text_total, cap_cols
-    )
-    cap_weight = to_relative(
-        jnp.transpose(w_caption.reshape(cap_cols, 2, 4, 2, cols), (2, 3, 0, 1, 4))
-    ).reshape(8, cap_cols, 2 * cols)
-    text_part = jnp.einsum("tk,skn->tsn", cap_all, cap_weight, preferred_element_type=f32)
-    text_part = text_part.reshape(4, text_total, 8, 2 * cols).astype(bf16)
-    text_pair = text_part[:2].astype(f32) + flip(text_part[2:], "y").astype(f32)
-    text_one = text_pair[0] + flip(text_pair[1].astype(bf16), "core").astype(f32)
-    text_proj = scatter_seq(jnp.transpose(text_one, (1, 0, 2)).reshape(8 * text_total, 2 * cols))
-    text_key_pre = text_proj[:, :cols]
-    text_square = jnp.sum(text_key_pre * text_key_pre, axis=1)
-
-    token_float = token_all.astype(f32)
-    normed_all = (rms_norm(token_float) * gain_rows[0] * (1.0 + scale_attn)).astype(bf16)
-    projected = jnp.dot(normed_all, own_attn, preferred_element_type=f32)
-    projected = to_absolute(projected.reshape(4, 2, rows, 3 * cols)).reshape(total, 3 * cols)
-    query_pre = projected[:, :cols]
-    key_pre = projected[:, cols : 2 * cols]
-    squares = jnp.concatenate(
-        [jnp.sum(query_pre * query_pre, axis=1), jnp.sum(key_pre * key_pre, axis=1), text_square]
-    )
-    squares = sum_seq(squares) / width
-    scales = rms_scale(squares)
-    query_scale = scales[:total, None]
-    key_scale = scales[total : 2 * total, None]
-    text_scale = scales[2 * total :, None]
-    query_normed = query_pre * query_scale
-    key_normed = key_pre * key_scale
-    text_key_normed = text_key_pre * text_scale
+
+    cap_keep, cap_send = on_chip(
+        caption_body,
+        [((2, 8, text_total, 2 * cols), bf16)] * 2,
+        place,
+        cap_all,
+        w_caption,
+        scalars=1,
+    )
+    cap_pair = cap_keep.astype(f32) + flip(cap_send, "core").astype(f32)
+    cap_one = cap_pair[0] + flip(cap_pair[1].astype(bf16), "y").astype(f32)
+    text_pieces = lax.all_to_all(cap_one.astype(bf16), seq_axes, 0, 0, tiled=True)
+
+    normed_all, projected, text_proj, squares = on_chip(
+        qkv_body,
+        [
+            ((total, width), bf16),
+            ((wide_cols, total), f32),
+            ((2 * cols, text_total), f32),
+            ((8, total), f32),
+        ],
+        place,
+        token_all,
+        *attn_parts,
+        jnp.stack([gain_rows[0], scale_attn]),
+        text_pieces,
+        scalars=1,
+    )
+    squares = sum_seq(squares)
     position = jnp.arange(total, dtype=jnp.int32)
-    angles = rope_angles(frame_shape[0], rope_shift[0], position, head_dim // 2)
-    cosine = jnp.cos(angles)[:, None, :]
-    sine_table = jnp.sin(angles)[:, None, :]
-    split = (total, own_heads, head_dim)
-    queries = rotate((query_normed * gain_query).reshape(split), cosine, sine_table).astype(bf16)
-    key_rows = rotate((key_normed * gain_key).reshape(split), cosine, sine_table).astype(bf16)
-    values = projected[:, 2 * cols :].reshape(split).astype(bf16)
-    text_split = (text_total, own_heads, head_dim)
-    text_keys = (text_key_normed * gain_text).astype(bf16).reshape(text_split)
-    text_values = text_proj[:, cols:].astype(bf16).reshape(text_split)
-
-    scores = jnp.einsum("qhd,khd->hqk", queries, key_rows, preferred_element_type=f32) * score_scale
-    row_max = jnp.max(scores, axis=-1)
-    log_sum = row_max + jnp.log(jnp.sum(jnp.exp(scores - row_max[..., None]), axis=-1))
-    probs = jnp.exp(scores - log_sum[..., None])
-    probs_low = probs.astype(bf16)
-    self_out = jnp.einsum("hqk,khd->qhd", probs_low, values, preferred_element_type=f32)
-    usable = jnp.arange(text_total, dtype=jnp.int32) < caption_len[0]
-    text_scores = (
-        jnp.einsum("qhd,khd->hqk", queries, text_keys, preferred_element_type=f32) * score_scale
-    )
-    text_weights = soft_weights(jnp.where(usable[None, None, :], text_scores, -1e30))
-    text_low = text_weights.astype(bf16)
-    cross_out = jnp.einsum("hqk,khd->qhd", text_low, text_values, preferred_element_type=f32)
-    mixed = (self_out + tanh_gate[None, :, None] * cross_out).astype(bf16).reshape(total, cols)
-
-    mixed_own = lax.all_to_all(mixed.reshape(8, rows, cols), seq_axes, 0, 0, tiled=True)
-    mixed_own = jnp.transpose(mixed_own, (1, 0, 2)).reshape(rows, width)
-    attn_proj = jnp.dot(mixed_own, full_out, preferred_element_type=f32)
+    angles = rope_angles(frame_shape[0], rope_shift[0], position, head_dim // 2).T
+    cosine = jnp.cos(angles)
+    sine = jnp.sin(angles)
+    flat = (cols, total)
+    (
+        mixed_pieces,
+        queries,
+        key_rows,
+        values,
+        self_out,
+        cross_out,
+        log_sum,
+        text_keys,
+        text_values,
+    ) = on_chip(
+        functools.partial(attend_body, own_heads),
+        [
+            ((8, cols, rows), bf16),
+            (flat, bf16),
+            (flat, bf16),
+            (flat, bf16),
+            (flat, f32),
+            (flat, f32),
+            ((8, total), f32),
+            ((cols, text_total), bf16),
+            ((cols, text_total), bf16),
+        ],
+        tanh_gate,
+        caption_len,
+        projected,
+        squares,
+        text_proj,
+        own_gains,
+        cosine,
+        sine,
+        scalars=2,
+    )
+
+    mixed_own = lax.all_to_all(mixed_pieces, seq_axes, 0, 0, tiled=True).reshape(width, rows)
+    attn_proj = lax.dot_general(
+        mixed_own, full_out, (((0,), (0,)), ((), ())), preferred_element_type=f32
+    )
     attn_scale = rms_scale(jnp.mean(attn_proj * attn_proj, axis=-1, keepdims=True))
     attn_normed = attn_proj * attn_scale
     own_float = own_tokens.astype(f32)
@@ -822,23 +1216,17 @@
         jnp.dot(grad_gate_up, own_gateup.T, preferred_element_type=f32)
     )
     wgrad_gateup = jnp.dot(normed_ffn_all.T, grad_gate_up, preferred_element_type=f32)
+    wgrad_gateup = jnp.transpose(
+        wgrad_gateup.astype(bf16).reshape(4, 4, block, -1), (1, 0, 2, 3)
+    )
+    wgrad_gateup = lax.psum_scatter(wgrad_gateup, "z", scatter_dimension=0, tiled=False)
+    wgrad_gateup = lax.all_to_all(
+        wgrad_gateup.reshape(8, block // 2, -1), plane_axes, 0, 0, tiled=True
+    )
+    (wgrad_gateup,) = on_chip(gateup_grad_body, [(w_gateup.shape, f32)], wgrad_gateup)
     wgrad_down = lax.psum_scatter(
         wgrad_down.astype(bf16), "z", scatter_dimension=0, tiled=True
     ).astype(f32)
-    wgrad_gateup = jnp.transpose(
-        wgrad_gateup.astype(bf16).reshape(4, 4, block, -1), (1, 0, 2, 3)
-    )
-    wgrad_gateup = lax.psum_scatter(wgrad_gateup, "z", scatter_dimension=0, tiled=False)
-    wgrad_gateup = lax.all_to_all(
-        wgrad_gateup.reshape(8, block // 2, -1), plane_axes, 0, 0, tiled=True
-    )
-    wgrad_gateup = (
-        jnp.transpose(
-            wgrad_gateup.reshape(2, 2, 2, block // 2, 2, 4, hidden_own), (3, 4, 0, 1, 5, 2, 6)
-        )
-        .reshape(block // 2, -1)
-        .astype(f32)
-    )
 
     sum_two = jnp.sum(grad_normed_ffn * residual_normed, axis=0)
     grad_in = grad_normed_ffn * gain_rows[2] * (1.0 + scale_ffn)
@@ -853,99 +1241,155 @@
         (grad_in - attn_normed * jnp.mean(grad_in * attn_normed, axis=-1, keepdims=True))
         * attn_scale
     ).astype(bf16)
-    grad_mixed_own = jnp.dot(grad_attn, full_out.T, preferred_element_type=f32).astype(bf16)
-    grad_mixed = lax.all_to_all(
-        jnp.transpose(grad_mixed_own.reshape(rows, 8, cols), (1, 0, 2)), seq_axes, 0, 0, tiled=True
-    ).reshape(split)
-    grad_attn_all = lax.all_gather(grad_attn, seq_axes, axis=0, tiled=True)
-    wgrad_output = jnp.dot(mixed.T, grad_attn_all, preferred_element_type=f32)
-    wgrad_output = wgrad_output.reshape(4, -1, width).astype(bf16)
-    wgrad_output = scatter_clip_low(clip_relative(wgrad_output.reshape(2, 2, -1, width)))
-    wgrad_output = lax.ppermute(
-        wgrad_output,
-        all_axes,
-        [(c * 8 + s, 4 * s + c) for c in range(4) for s in range(8)],
-    ).astype(f32)
-
-    grad_float = grad_mixed.astype(f32)
-    gate_sum = jnp.sum(grad_float * cross_out, axis=(0, 2)) * (1.0 - tanh_gate * tanh_gate)
-    text_grad = (
-        jnp.einsum("qhd,khd->hqk", grad_mixed, text_values, preferred_element_type=f32)
-        * tanh_gate[:, None, None]
-    )
-    text_center = jnp.sum(text_weights * text_grad, axis=-1, keepdims=True)
-    grad_text_scores = (text_weights * (text_grad - text_center)).astype(bf16)
-    grad_text_keys = (
-        jnp.einsum("hqk,qhd->khd", grad_text_scores, queries, preferred_element_type=f32)
-        * score_scale
-    ).reshape(text_total, cols)
-    grad_text_values = (
-        jnp.einsum("hqk,qhd->khd", text_low, grad_mixed, preferred_element_type=f32)
-        * tanh_gate[None, :, None]
-    ).reshape(text_total, cols)
-    grad_queries = jnp.einsum(
-        "hqk,khd->qhd", grad_text_scores, text_keys, preferred_element_type=f32
-    )
-    sum_six = jnp.sum(grad_text_keys * text_key_normed, axis=0)
-    grad_in = grad_text_keys * gain_text
-    text_mean = sum_seq(jnp.sum(grad_in * text_key_normed, axis=1)) / width
-    grad_text_pre = (grad_in - text_key_normed * text_mean[:, None]) * text_scale
-    grad_text_proj = jnp.concatenate([grad_text_pre, grad_text_values], axis=1).astype(bf16)
-    text_seq = gather_seq(grad_text_proj).reshape(8, text_total, 2 * cols)
-    text_all = jnp.concatenate([text_seq, flip(text_seq, "core")], axis=1)
-    text_all = jnp.concatenate([text_all, flip(text_all, "y")], axis=1)
-    wgrad_caption = jnp.einsum("tk,stn->skn", cap_all, text_all, preferred_element_type=f32)
-    wgrad_caption = jnp.transpose(
-        to_absolute(wgrad_caption.reshape(4, 2, cap_cols, 2, cols)), (2, 3, 0, 1, 4)
-    ).reshape(cap_cols, 2 * width)
-    grad_caption = jnp.einsum("stn,skn->tk", text_all, cap_weight, preferred_element_type=f32)
-    grad_caption = clip_relative(grad_caption.reshape(2, 2, text_total, cap_cols))
+    grad_mixed = lax.dot_general(
+        full_out, grad_attn, (((1,), (1,)), ((), ())), preferred_element_type=f32
+    ).astype(bf16)
+    grad_pieces = lax.all_to_all(grad_mixed.reshape(8, cols, rows), seq_axes, 0, 0, tiled=True)
+
+    (
+        grad_mixed,
+        text_query,
+        text_key_in,
+        text_value_grad,
+        text_stats,
+        text_gain,
+        gate_sum,
+    ) = on_chip(
+        functools.partial(text_back_body, own_heads),
+        [
+            (flat, bf16),
+            (flat, f32),
+            ((cols, text_total), f32),
+            ((cols, text_total), f32),
+            ((8, text_total), f32),
+            ((cols, 128), f32),
+            ((8, 128), f32),
+        ],
+        tanh_gate,
+        caption_len,
+        grad_pieces,
+        queries,
+        text_keys,
+        text_values,
+        cross_out,
+        text_proj,
+        squares,
+        own_gains,
+        scalars=2,
+    )
+    text_stats = sum_seq(text_stats)
+    (grad_text_proj,) = on_chip(
+        text_proj_back_body,
+        [((text_total, 2 * cols), bf16)],
+        text_key_in,
+        text_value_grad,
+        text_proj,
+        squares,
+        text_stats,
+    )
+    text_all = lax.all_gather(grad_text_proj, all_axes, axis=0)
+    wgrad_caption, grad_caption = on_chip(
+        caption_back_body,
+        [(w_caption.shape, f32), ((4, text_total, cap_cols), f32)],
+        cap_all,
+        text_all.reshape(4, 8, text_total, 2 * cols),
+        w_caption,
+    )
     grad_caption = lax.all_to_all(
         grad_caption.reshape(32, text_rows, cap_cols), all_axes, 0, 0, tiled=True
     )
-    grad_caption = jnp.transpose(grad_caption, (1, 0, 2)).reshape(1, text_rows, 32 * cap_cols)
-
-    delta = jnp.sum(grad_float * self_out, axis=-1).T
-    grad_values = jnp.einsum("hqk,qhd->khd", probs_low, grad_mixed, preferred_element_type=f32)
-    grad_probs = jnp.einsum("qhd,khd->hqk", grad_mixed, values, preferred_element_type=f32)
-    grad_scores = (probs * (grad_probs - delta[..., None])).astype(bf16)
-    grad_keys = (
-        jnp.einsum("hqk,qhd->khd", grad_scores, queries, preferred_element_type=f32) * score_scale
-    )
-    grad_queries = (
-        grad_queries
-        + jnp.einsum("hqk,khd->qhd", grad_scores, key_rows, preferred_element_type=f32)
-    ) * score_scale
-    grad_query_rot = rotate(grad_queries, cosine, -sine_table).reshape(total, cols)
-    grad_key_rot = rotate(grad_keys, cosine, -sine_table).reshape(total, cols)
-    sum_four = jnp.sum(grad_query_rot * query_normed, axis=0)
-    sum_five = jnp.sum(grad_key_rot * key_normed, axis=0)
-    query_in = grad_query_rot * gain_query
-    key_in = grad_key_rot * gain_key
-    means = sum_seq(
-        jnp.concatenate(
-            [jnp.sum(query_in * query_normed, axis=1), jnp.sum(key_in * key_normed, axis=1)]
-        )
-    ) / width
-    grad_query_pre = (query_in - query_normed * means[:total, None]) * query_scale
-    grad_key_pre = (key_in - key_normed * means[total:, None]) * key_scale
-    grad_projected = jnp.concatenate(
-        [grad_query_pre, grad_key_pre, grad_values.reshape(total, cols)], axis=1
-    ).astype(bf16)
-    grad_projected = to_relative(grad_projected.reshape(4, 2, rows, -1)).reshape(total, -1)
-    grad_normed = scatter_seq(jnp.dot(grad_projected, own_attn.T, preferred_element_type=f32))
-    wgrad_attention = jnp.dot(normed_all.T, grad_projected, preferred_element_type=f32)
-    wgrad_attention = scatter_clip_low(
-        clip_relative(wgrad_attention.astype(bf16).reshape(2, 2, width // 4, -1))
-    )
+    (grad_caption,) = on_chip(caption_grad_body, [((text_rows, 32 * cap_cols), f32)], grad_caption)
+
+    query_in, key_in, value_grad, means, own_gain_sums = on_chip(
+        functools.partial(attend_back_body, own_heads),
+        [
+            (flat, f32),
+            (flat, f32),
+            (flat, bf16),
+            ((8, total), f32),
+            ((cols, 128), f32),
+        ],
+        grad_mixed,
+        queries,
+        key_rows,
+        values,
+        self_out,
+        log_sum,
+        text_query,
+        projected,
+        squares,
+        own_gains,
+        cosine,
+        sine,
+    )
+    means = sum_seq(means)
+    early = rows // 4
+    rest = rows - early
+    quarter = width // 4
+    own_part, keep_part, side_part, front_1, front_2, front_3, near_part, far_part = on_chip(
+        project_back_body,
+        [
+            ((2, rows, width), bf16),
+            ((3, rest, width), bf16),
+            ((3, rest, width), bf16),
+            ((2, early, width), bf16),
+            ((2, early, width), bf16),
+            ((2, early, width), bf16),
+            ((2, quarter, wide_cols), bf16),
+            ((2, quarter, wide_cols), bf16),
+        ],
+        place,
+        query_in,
+        key_in,
+        value_grad,
+        projected,
+        squares,
+        means,
+        normed_all,
+        *attn_parts,
+        scalars=1,
+        scratch=[
+            pltpu.VMEM((wide_cols, total), bf16),
+            pltpu.VMEM((total, wide_cols), bf16),
+        ],
+    )
+    side = flip(side_part, "x")
+    fronts = [from_ahead((front_3, front_2, front_1)[k - 1], "z", k) for k in (1, 2, 3)]
+    back_sum = keep_part.astype(f32) + side.astype(f32)
+    backs = [from_ahead(back_sum[3 - k].astype(bf16), "z", k) for k in (1, 2, 3)]
+    front_sum = own_part[:, :early].astype(f32)
+    for front in fronts:
+        front_sum = front_sum + front.astype(f32)
+    last = flip(jnp.concatenate([front_sum[1].astype(bf16), own_part[1, early:]]), "x").astype(f32)
+    back_total = own_part[0, early:].astype(f32) + last[early:]
+    for back in backs:
+        back_total = back_total + back.astype(f32)
+    grad_normed = jnp.concatenate([front_sum[0] + last[:early], back_total])
+
+    wgrad_pair = near_part.astype(f32) + flip(far_part, "core").astype(f32)
+    wgrad_one = wgrad_pair[0] + flip(wgrad_pair[1].astype(bf16), "y").astype(f32)
     wgrad_attention = lax.all_to_all(
-        wgrad_attention.reshape(8, -1, 3 * cols), seq_axes, 0, 0, tiled=True
-    )
-    wgrad_attention = (
-        jnp.transpose(wgrad_attention.reshape(8, -1, 3, cols), (1, 2, 0, 3))
-        .reshape(-1, 3 * width)
-        .astype(f32)
-    )
+        wgrad_one.astype(bf16).reshape(8, attn_rows, wide_cols), seq_axes, 0, 0, tiled=True
+    )
+    (wgrad_attention,) = on_chip(attention_grad_body, [(w_attention.shape, f32)], wgrad_attention)
+
+    mixed_plane = jnp.transpose(
+        mixed_own.reshape(2, 2, 4, 2, attn_rows, rows), (0, 1, 3, 2, 4, 5)
+    ).reshape(8, 4 * attn_rows, rows)
+    mixed_plane = lax.all_to_all(mixed_plane, plane_axes, 0, 0, tiled=True)
+    grad_attn_plane = gather_plane(grad_attn)
+    (wgrad_output,) = on_chip(
+        output_grad_body,
+        [((4 * attn_rows, width), bf16)],
+        place,
+        mixed_plane,
+        grad_attn_plane,
+        scalars=1,
+    )
+    wgrad_output = lax.psum_scatter(
+        wgrad_output, "z", scatter_dimension=0, tiled=True
+    ).astype(f32)
+
     sum_zero = jnp.sum(grad_normed * token_normed, axis=0)
     grad_in = grad_normed * gain_rows[0] * (1.0 + scale_attn)
     grad_tokens = (
@@ -956,11 +1400,11 @@
 
     wide = lax.dynamic_update_slice(
         jnp.zeros((3, width), f32),
-        jnp.stack([sum_four, sum_five, sum_six]),
+        jnp.stack([own_gain_sums[:, 0], own_gain_sums[:, 1], text_gain[:, 0]]),
         (0, seq_at * cols),
     )
     gate_wide = lax.dynamic_update_slice(
-        jnp.zeros((128,), f32), gate_sum, (seq_at * own_heads,)
+        jnp.zeros((128,), f32), gate_sum[:own_heads, 0], (seq_at * own_heads,)
     )
     sums = sum_seq(
         jnp.concatenate([sum_zero, sum_one, sum_two, sum_three, wide.reshape(-1), gate_wide])
@@ -1005,7 +1449,7 @@
     return (
         block_out[None],
         grad_tokens[None],
-        grad_caption,
+        grad_caption[None],
         grad_condition[None],
         wgrad_modulation,
         bias_grad,
@@ -1017,11 +1461,6 @@
         wgrad_gateup,
         wgrad_down,
     )
-
-
-def scatter_clip_low(value):
-    pair = value[0].astype(f32) + flip(value[1], "y").astype(f32)
-    return (pair[0] + flip(pair[1].astype(bf16), "core").astype(f32)).astype(bf16)
 
 
 def specs(clip, seq):

time: 857 us -> 615 us (0.72)
  local copies, waits for them, and re-layouts: 163 us -> 62.1 us
  other arithmetic: 119 us -> 43.7 us
  Pallas kernels: 0 us -> 63.2 us
  matrix products: 96.6 us -> 33.5 us
  waiting for transfers between devices: 252 us -> 210 us
  blocking collectives: 26.4 us -> 11.4 us
    pallas_call x0 -> x13, Pallas kernels: none -> 63.2 us  [on_chip(): pl.pallas_call(body, out_shape=[jax.ShapeDtypeStruct(shape, kind) for sha...]
    dot_general x20 -> x2, matrix products: 65.5 us -> 7.73 us  [the longest x1 4.08 us: local_fast(): lax.dot_general(full_out, grad_attn, (((1,), (1,)), ((), ())), preferred_...]
    ppermute x24 -> x6, waiting for transfers between devices: 87.9 us -> 43.2 us  [from_ahead(): lax.ppermute(value, axis, [((i + step) % count, i) for i in range(count)])]
    ppermute x24 -> x6, starting transfers between devices: 42.2 us -> 6.45 us  [from_ahead(): lax.ppermute(value, axis, [((i + step) % count, i) for i in range(count)])]
    reshape x15 -> x1, local copies, waits for them, and re-layouts: 31.9 us -> 2.05 us  [local_fast(): wgrad_gateup.astype(bf16).reshape(4, 4, block, -1)]
    ppermute x52 -> x48, waiting for transfers between devices: 102 us -> 79.1 us  [flip(): return lax.ppermute(value, axis, [(0, 1), (1, 0)])]
    concatenate x19 -> x1, other arithmetic: 16.3 us -> 0.03 us  [local_fast(): jnp.concatenate([front_sum[1].astype(bf16), own_part[1, early:]])]
    all_to_all x1, blocking collectives: 26.4 us -> 11.4 us  [local_fast(): lax.all_to_all(mixed_pieces, seq_axes, 0, 0, tiled=True)]
  transfers between devices with their start and end apart: 102 -> 83, of which waited for: 42 -> 45; matrix products, arithmetic and copies ran while one was open for 40% -> 16% of each run, Pallas kernels for 0% -> 10%
where the time goes in v2:
time: 615 us; the launch traced here: 605 us
  waiting for transfers between devices  210 us (34%)
  starting transfers between devices  162 us (26%)
  Pallas kernels  63.2 us (10%)
  local copies, waits for them, and re-layouts  62.1 us (10%)
  other arithmetic  43.7 us (7%)
  matrix products  33.5 us (5%)
  between operations  19.2 us (3%)
  blocking collectives  11.4 us (2%)
    ppermute x48, starting transfers between devices, flip(): return lax.ppermute(value, axis, [(0, 1), (1, 0)])  80.3 us
    ppermute x48, waiting for transfers between devices, flip(): return lax.ppermute(value, axis, [(0, 1), (1, 0)])  79.1 us
    pallas_call x13, Pallas kernels, on_chip(): pl.pallas_call(body, out_shape=[jax.ShapeDtypeStruct(shape, kind) for sha...  63.2 us
    ppermute x6, waiting for transfers between devices, from_ahead(): lax.ppermute(value, axis, [((i + step) % count, i) for i in range(count)])  43.2 us
    unnamed x210, local copies, waits for them, and re-layouts  36.1 us
    all_gather x1, waiting for transfers between devices, local_fast(): own_down = lax.all_gather(w_down, 'z', axis=0, tiled=True)  26.1 us
    ppermute x12, waiting for transfers between devices, swap_z(): return lax.ppermute(value, 'z', [(i, i ^ bit) for i in range(4)])  25.7 us
    all_to_all x1, starting transfers between devices, local_fast(): ffn_piece = lax.all_to_all(ffn_piece, plane_axes, 0, 0, tiled=True)  17.3 us
  transfers between devices with their start and end apart: 83, of which 45 were waited for; matrix products, arithmetic and copies ran while one was open for 16% of the time, Pallas kernels for 10%

profile of v2, /device:TPU:1, one launch (start us, length us, event | category | flops | bytes accessed | tf_op | source)
XLA Modules:
  0.0 605.0 jit_solution(6155867788826308586)
XLA Ops:
  14.4 7.1 %all-to-all-start.1 = ((bf16[32,16,128]{2,1,0:T(8,128)(2,1)}), bf16[32,16,128]{2,1,0:T(8,128)(2,1)S(1)}, u32[]{:S(2)}, u32[]{:S(2)}) async-start(bf16[32,16,128]{2,1,0:T(8,128)(2,1)} %get-tuple-element.54), calls=%async_computation.1 | async-start | bytes 262144 | tf_op jit(solution)/shard_map/all_to_all | solution.py:1065
  33.9 5.4 all-to-all-start
  51.5 17.3 %all-to-all-start.4 = ((bf16[8,48,1024]{2,1,0:T(8,128)(2,1)}), bf16[8,48,1024]{2,1,0:T(8,128)(2,1)S(1)}, u32[]{:S(2)}, u32[]{:S(2)}) async-start(bf16[8,48,1024]{2,1,0:T(8,128)(2,1)} %get-tuple-element.61), calls=%async_computation.4 | async-start | bytes 1572864 | tf_op jit(solution)/shard_map/all_to_all | solution.py:1104
  73.9 6.3 %all-to-all-done.4 = bf16[8,48,1024]{2,1,0:T(8,128)(2,1)S(1)} async-done(((bf16[8,48,1024]{2,1,0:T(8,128)(2,1)}), bf16[8,48,1024]{2,1,0:T(8,128)(2,1)S(1)}, u32[]{:S(2)}, u32[]{:S(2)}) %all-to-all-start.4) | async-done | bytes 786464 | tf_op jit(solution)/shard_map/all_to_all | solution.py:1104
  94.2 6.4 %collective-permute-done.5 = f32[16896]{0:T(1024)S(1)} collective-permute-done((f32[16896]{0:T(1024)S(1)}, f32[16896]{0:T(1024)S(1)}, u32[]{:S(2)}, u32[]{:S(2)}) %collective-permute-start.5) | collective-permute-done | bytes 67616 | tf_op jit(solution)/shard_map/ppermute | solution.py:537
  100.7 4.9 collective-permute-start.6
  111.3 10.0 %shard_map.257 = (bf16[1024,1536]{1,0:T(8,128)(2,1)}, f32[640,1024]{1,0:T(8,128)}, f32[384,128]{1,0:T(8,128)S(1)}, f32[8,1024]{1,0:T(8,128)S(1)}) custom-call(s32[5]{0:T(128)S(1)} %stack.47.place, bf16[1024,1536]{1,0:T(8,128)(2,1)} %bitcast.140, bf16[384,640]{1,0:T(8,128)(2,1)S(1)} %bitcast.127, bf16[384,640]{1,0:T(8,128)(2,1)} %collective-permute-done.7.w1, ...), custom_call_target="tpu_custom_call" | custom-call | tf_op jit(solution)/shard_map/pallas_call | solution.py:587
  131.4 9.8 %shard_map.258 = (bf16[8,192,128]{2,1,0:T(8,128)(2,1)S(1)}, bf16[192,1024]{1,0:T(8,128)(2,1)S(1)}, bf16[192,1024]{1,0:T(8,128)(2,1)S(1)}, bf16[192,1024]{1,0:T(8...) custom-call(f32[3]{0:T(128)S(1)} %convert_tanh_fusion.gate, ...), custom_call_target="tpu_custom_call" | custom-call | tf_op jit(solution)/shard_map/pallas_call | solution.py:587
  146.4 11.4 %all_to_all.50 = bf16[8,192,128]{2,1,0:T(8,128)(2,1)} all-to-all(bf16[8,192,128]{2,1,0:T(8,128)(2,1)S(1)} %get-tuple-element.60), channel_id=1, replica_groups=mesh['y'=2,'core'=2,'z'=4,'x'=2] {'z','x'}, dimensions={0} | all-to-all | bytes 786432 | tf_op jit(solution)/shard_map/all_to_all | solution.py:1177
  164.9 5.4 collective-permute-done.16
  179.0 20.5 %collective-permute-start.19 = (bf16[512,1536]{1,0:T(8,128)(2,1)}, bf16[512,1536]{1,0:T(8,128)(2,1)}, u32[]{:S(2)}, u32[]{:S(2)}) collective-permute-start(bf16[512,1536]{1,0:T(8,128)(2,1)} %get-tuple-element.162), channel_id=1, source_target_pairs={{0,8},{8,0},{1,9},{9,1},{2,10},{10,2},{3,11},{11,3},{4,12},{12,4},... | collective-permute-start | bytes 4718600 | tf_op jit(solution)/shard_map/ppermute | solution.py:528
  205.6 11.3 %all-gather.10.cloned.1.call-done = bf16[4,4,96,1024]{3,2,0,1:T(8,128)(2,1)} async-done(((bf16[1,4,96,1024]{3,2,0,1:T(8,128)(2,1)}), bf16[4,4,96,1024]{3,2,0,1:T(8,128)(2,1)}) %all-gather.10.cloned.1.call-update) | async-done | bytes 3145744 | tf_op jit(solution)/shard_map/all_gather | solution.py:1106
  216.9 6.5 %fusion.71 = f32[1024,1024]{0,1:T(8,128)S(1)} fusion(bf16[1024,1536]{1,0:T(8,128)(2,1)} %constant_dynamic-update-slice_fusion.5, bf16[1536,1024]{1,0:T(8,128)(2,1)} %bitcast.157), kind=kOutput, calls=%fused_computation.234 | convolution fusion | flops 3221225472 | bytes 10485760 | tf_op jit(solution)/shard_map/dot_general | solution.py:1192
  227.0 26.1 %all-gather.12.cloned.1.call-done = bf16[512,1536]{1,0:T(8,128)(2,1)} async-done(((bf16[128,1536]{1,0:T(8,128)(2,1)}), bf16[512,1536]{1,0:T(8,128)(2,1)}) %all-gather.12.cloned.1.call-update) | async-done | bytes 1572880 | tf_op jit(solution)/shard_map/all_gather | solution.py:1108
  264.0 7.8 %collective-permute-done.22 = bf16[128,1536]{1,0:T(8,128)(2,1)S(1)} collective-permute-done((bf16[128,1536]{1,0:T(8,128)(2,1)S(1)}, bf16[128,1536]{1,0:T(8,128)(2,1)S(1)}, u32[]{:S(2)}, u32[]{:S(2)}) %collective-permute-start.22) | collective-permute-done | bytes 393248 | tf_op jit(solution)/shard_map/ppermute | solution.py:528
  283.0 5.6 collective-permute-done.26
  294.8 5.8 collective-permute-start.29
  317.6 4.7 fusion.61
  325.1 4.6 convolution_convert_fusion
  368.0 11.5 %all-to-all-done.5.pieces = bf16[8,192,128]{2,1,0:T(8,128)(2,1)S(1)} async-done(((bf16[8,192,128]{2,1,0:T(8,128)(2,1)}), bf16[8,192,128]{2,1,0:T(8,128)(2,1)S(1)}, u32[]{:S(2)}, u32[]{:S(2)}) %all-to-all-start.5) | async-done | bytes 393248 | tf_op jit(solution)/shard_map/all_to_all | solution.py:1247
  380.2 8.2 %all-to-all-start.8 = ((bf16[8,192,128]{2,1,0:T(8,128)(2,1)}), bf16[8,192,128]{2,1,0:T(8,128)(2,1)S(1)}, u32[]{:S(2)}, u32[]{:S(2)}) async-start(bf16[8,192,128]{2,1,0:T(8,128)(2,1)} %bitcast.142), calls=%async_computation.8 | async-start | bytes 786432 | tf_op jit(solution)/shard_map/all_to_all | solution.py:1379
  398.6 10.9 %shard_map.260 = (f32[192,1024]{1,0:T(8,128)S(1)}, f32[192,1024]{1,0:T(8,128)S(1)}, bf16[192,1024]{1,0:T(8,128)(2,1)S(1)}, f32[8,1024]{1,0:T(8,128)S(1)}, f32[192,128]{1,0:T(8,128)S(1)}) custom-call(bf16[192,1024]{1,0:T(8,128)(2,1)S(1)} %get-tuple-element.66.grad, bf16[192,1024]{1,0:T(8,128)(2,1)S(1)} %get-tuple-element.62.query, ...), custom_call_target="tpu_custom_call" | custom-call | tf_op jit(solution)/shard_map/pallas_call | solution.py:587
  420.5 13.1 %shard_map.261 = (bf16[2,128,1536]{2,1,0:T(8,128)(2,1)S(1)}, bf16[3,96,1536]{2,1,0:T(8,128)(2,1)}, bf16[3,96,1536]{2,1,0:T(8,128)(2,1)}, bf16[2,32,1536]{2,1,0:T...) custom-call(s32[5]{0:T(128)S(1)} %stack.47.place, ...), custom_call_target="tpu_custom_call" | custom-call | tf_op jit(solution)/shard_map/pallas_call | solution.py:587
  439.7 13.7 %collective-permute-done.39 = bf16[2,32,1536]{2,1,0:T(8,128)(2,1)S(1)} collective-permute-done((bf16[2,32,1536]{2,1,0:T(8,128)(2,1)S(1)}, bf16[2,32,1536]{2,1,0:T(8,128)(2,1)S(1)}, u32[]{:S(2)}, u32[]{:S(2)}) %collective-permute-start.39) | collective-permute-done | bytes 196640 | tf_op jit(solution)/shard_map/ppermute | solution.py:533
  455.4 9.8 %collective-permute-done.46 = f32[8,128]{1,0:T(8,128)S(1)} collective-permute-done((f32[8,128]{1,0:T(8,128)S(1)}, f32[8,128]{1,0:T(8,128)S(1)}, u32[]{:S(2)}, u32[]{:S(2)}) %collective-permute-start.46) | collective-permute-done | bytes 4128 | tf_op jit(solution)/shard_map/ppermute | solution.py:528
  472.4 5.0 collective-permute-start.59
  485.3 7.2 %collective-permute-done.43 = bf16[96,1536]{1,0:T(8,128)(2,1)S(1)} collective-permute-done((bf16[96,1536]{1,0:T(8,128)(2,1)S(1)}, bf16[96,1536]{1,0:T(8,128)(2,1)S(1)}, u32[]{:S(2)}, u32[]{:S(2)}) %collective-permute-start.43) | collective-permute-done | bytes 294944 | tf_op jit(solution)/shard_map/ppermute | solution.py:533
  492.5 21.0 %collective-permute-done.44 = bf16[96,1536]{1,0:T(8,128)(2,1)S(1)} collective-permute-done((bf16[96,1536]{1,0:T(8,128)(2,1)S(1)}, bf16[96,1536]{1,0:T(8,128)(2,1)S(1)}, u32[]{:S(2)}, u32[]{:S(2)}) %collective-permute-start.44) | collective-permute-done | bytes 294944 | tf_op jit(solution)/shard_map/ppermute | solution.py:533
  533.5 6.7 %collective-permute-done.53 = f32[2,17024]{1,0:T(2,128)S(1)} collective-permute-done((f32[2,17024]{1,0:T(2,128)S(1)}, f32[2,17024]{1,0:T(2,128)S(1)}, u32[]{:S(2)}, u32[]{:S(2)}) %collective-permute-start.53) | collective-permute-done | bytes 136224 | tf_op jit(solution)/shard_map/ppermute | solution.py:528
  557.8 5.5 all-to-all-start.9
  565.2 9.1 %collective-permute-done.56 = f32[1024]{0:T(1024)S(1)} collective-permute-done((f32[1024]{0:T(1024)S(1)}, f32[1024]{0:T(1024)S(1)}, u32[]{:S(2)}, u32[]{:S(2)}) %collective-permute-start.56) | collective-permute-done | bytes 4128 | tf_op jit(solution)/shard_map/ppermute | solution.py:528
  574.8 5.4 shard_map.263
  (541 shorter events, 281.8 us)
Async XLA Ops:
  7.2 104.0 %all-gather.14.cloned.1.call-start = ((), (), s32[]{:S(2)}) async-start(), calls=%async_computation.19 | async-start | bytes 3538944 | tf_op jit(solution)/shard_map/all_gather | solution.py:1048
  8.0 149.8 %all-gather.8.cloned.1.call-start = ((), (), s32[]{:S(2)}) async-start(), calls=%async_computation.13 | async-start | bytes 4866048 | tf_op jit(solution)/shard_map/all_gather | solution.py:1049
  9.4 16.9 %collective-permute-start = (bf16[1024]{0:T(1024)(128)(2,1)S(1)}, bf16[1024]{0:T(1024)(128)(2,1)S(1)}, u32[]{:S(2)}, u32[]{:S(2)}) collective-permute-start(bf16[1024]{0:T(1024)(128)(2,1)S(1)} %multiply_convert_fusion.5), channel_id=1, source_target_pairs={{0,8},{8,0},{1,9},{9,1},{2,10},{10,2},{3,11},{11,3},{4,12},{12,4},... | collective-permute-start | bytes 6152 | tf_op jit(solution)/shard_map/ppermute | solution.py:528
  14.4 19.5 %all-to-all-start.1 = ((bf16[32,16,128]{2,1,0:T(8,128)(2,1)}), bf16[32,16,128]{2,1,0:T(8,128)(2,1)S(1)}, u32[]{:S(2)}, u32[]{:S(2)}) async-start(bf16[32,16,128]{2,1,0:T(8,128)(2,1)} %get-tuple-element.54), calls=%async_computation.1 | async-start | bytes 262144 | tf_op jit(solution)/shard_map/all_to_all | solution.py:1065
  33.9 17.6 %all-to-all-start = ((bf16[8,48,640]{2,1,0:T(8,128)(2,1)}), bf16[8,48,640]{2,1,0:T(8,128)(2,1)S(1)}, u32[]{:S(2)}, u32[]{:S(2)}) async-start(bf16[8,48,640]{2,1,0:T(8,128)(2,1)} %get-tuple-element.53), calls=%async_computation | async-start | bytes 983040 | tf_op jit(solution)/shard_map/all_to_all | solution.py:1068
  48.5 22.8 %collective-permute-start.11 = (bf16[8,128,384]{2,1,0:T(8,128)(2,1)}, bf16[8,128,384]{2,1,0:T(8,128)(2,1)}, u32[]{:S(2)}, u32[]{:S(2)}) collective-permute-start(bf16[8,128,384]{2,1,0:T(8,128)(2,1)} %fusion.23), channel_id=1, source_target_pairs={{0,16},{16,0},{1,17},{17,1},{2,18},{18,2},{3,19},{19,3},{4,20},{20... | collective-permute-start | bytes 2359304 | tf_op jit(solution)/shard_map/ppermute | solution.py:528
  51.5 28.6 %all-to-all-start.4 = ((bf16[8,48,1024]{2,1,0:T(8,128)(2,1)}), bf16[8,48,1024]{2,1,0:T(8,128)(2,1)S(1)}, u32[]{:S(2)}, u32[]{:S(2)}) async-start(bf16[8,48,1024]{2,1,0:T(8,128)(2,1)} %get-tuple-element.61), calls=%async_computation.4 | async-start | bytes 1572864 | tf_op jit(solution)/shard_map/all_to_all | solution.py:1104
  69.5 15.5 %collective-permute-start.3 = (f32[16896]{0:T(1024)}, f32[16896]{0:T(1024)}, u32[]{:S(2)}, u32[]{:S(2)}) collective-permute-start(f32[16896]{0:T(1024)} %pad_maximum_fusion.14), channel_id=1, source_target_pairs={{0,8},{8,0},{1,9},{9,1},{2,10},{10,2},{3,11},{11,3},{4,12},{12,4},... | collective-permute-start | bytes 202760 | tf_op jit(solution)/shard_map/ppermute | solution.py:528
  69.5 39.5 %collective-permute-start.8 = (bf16[384,640]{1,0:T(8,128)(2,1)S(1)}, bf16[384,640]{1,0:T(8,128)(2,1)S(1)}, u32[]{:S(2)}, u32[]{:S(2)}) collective-permute-start(bf16[384,640]{1,0:T(8,128)(2,1)S(1)} %bitcast.125), channel_id=1, source_target_pairs={{0,16},{16,0},{1,17},{17,1},{2,18},{18,2},{3,19},{19,3},{4,20},{20... | collective-permute-start | bytes 1474568 | tf_op jit(solution)/shard_map/ppermute | solution.py:528
  81.0 30.2 %all-to-all-start.2 = ((bf16[8,128,384]{2,1,0:T(8,128)(2,1)}), bf16[8,128,384]{2,1,0:T(8,128)(2,1)S(1)}, u32[]{:S(2)}, u32[]{:S(2)}) async-start(bf16[8,128,384]{2,1,0:T(8,128)(2,1)} %fusion.2), calls=%async_computation.2 | async-start | bytes 1572864 | tf_op jit(solution)/shard_map/all_to_all | solution.py:1120
  85.0 131.9 %all-gather.10.cloned.1.call-start = ((), (), s32[]{:S(2)}) async-start(), calls=%async_computation.14 | async-start | bytes 3932160 | tf_op jit(solution)/shard_map/all_gather | solution.py:1106
  110.9 142.1 %all-gather.12.cloned.1.call-start = ((), (), s32[]{:S(2)}) async-start(), calls=%async_computation.15 | async-start | bytes 1966080 | tf_op jit(solution)/shard_map/all_gather | solution.py:1108
  179.0 23.9 %collective-permute-start.19 = (bf16[512,1536]{1,0:T(8,128)(2,1)}, bf16[512,1536]{1,0:T(8,128)(2,1)}, u32[]{:S(2)}, u32[]{:S(2)}) collective-permute-start(bf16[512,1536]{1,0:T(8,128)(2,1)} %get-tuple-element.162), channel_id=1, source_target_pairs={{0,8},{8,0},{1,9},{9,1},{2,10},{10,2},{3,11},{11,3},{4,12},{12,4},... | collective-permute-start | bytes 4718600 | tf_op jit(solution)/shard_map/ppermute | solution.py:528
  199.5 278.0 %reduce-scatter.8.cloned.1.call-start = ((), (), s32[]{:S(2)}) async-start(), calls=%async_computation.18 | async-start | bytes 1966080 | tf_op jit(solution)/shard_map/reduce_scatter | solution.py:1227
  317.2 240.6 %reduce-scatter.6.cloned.1.call-start = ((), (), s32[]{:S(2)}) async-start(), calls=%async_computation.17 | async-start | bytes 3932160 | tf_op jit(solution)/shard_map/reduce_scatter | solution.py:1222
  355.4 24.0 %all-to-all-start.5 = ((bf16[8,192,128]{2,1,0:T(8,128)(2,1)}), bf16[8,192,128]{2,1,0:T(8,128)(2,1)S(1)}, u32[]{:S(2)}, u32[]{:S(2)}) async-start(bf16[8,192,128]{2,1,0:T(8,128)(2,1)} %bitcast.143), calls=%async_computation.5 | async-start | bytes 786432 | tf_op jit(solution)/shard_map/all_to_all | solution.py:1247
  362.3 50.7 %collective-permute-start.63 = (bf16[64,1536]{1,0:T(8,128)(2,1)}, bf16[64,1536]{1,0:T(8,128)(2,1)}, u32[]{:S(2)}, u32[]{:S(2)}) collective-permute-start(bf16[64,1536]{1,0:T(8,128)(2,1)} %slice.490), channel_id=1, source_target_pairs={{0,1},{1,0},{2,3},{3,2},{4,5},{5,4},{6,7},{7,6},{8,9},{9,8},{10,11... | collective-permute-start | bytes 589832 | tf_op jit(solution)/shard_map/ppermute | solution.py:528
  365.3 51.9 %collective-permute-start.64 = (bf16[64,1536]{1,0:T(8,128)(2,1)}, bf16[64,1536]{1,0:T(8,128)(2,1)}, u32[]{:S(2)}, u32[]{:S(2)}) collective-permute-start(bf16[64,1536]{1,0:T(8,128)(2,1)} %slice.491), channel_id=1, source_target_pairs={{0,16},{16,0},{1,17},{17,1},{2,18},{18,2},{3,19},{19,3},{4,20},{20... | collective-permute-start | bytes 589832 | tf_op jit(solution)/shard_map/ppermute | solution.py:528
  380.2 160.1 %all-to-all-start.8 = ((bf16[8,192,128]{2,1,0:T(8,128)(2,1)}), bf16[8,192,128]{2,1,0:T(8,128)(2,1)S(1)}, u32[]{:S(2)}, u32[]{:S(2)}) async-start(bf16[8,192,128]{2,1,0:T(8,128)(2,1)} %bitcast.142), calls=%async_computation.8 | async-start | bytes 786432 | tf_op jit(solution)/shard_map/all_to_all | solution.py:1379
  388.4 186.3 %all-gather.16.cloned.1.call-start = ((), (), s32[]{:S(2)}) async-start(), calls=%async_computation.20 | async-start | bytes 3244032 | tf_op jit(solution)/shard_map/all_gather | solution.py:1290
  418.9 127.6 %collective-permute-start.65 = (bf16[512,1536]{1,0:T(8,128)(2,1)}, bf16[512,1536]{1,0:T(8,128)(2,1)}, u32[]{:S(2)}, u32[]{:S(2)}) collective-permute-start(bf16[512,1536]{1,0:T(8,128)(2,1)} %get-tuple-element.154), channel_id=1, source_target_pairs={{0,8},{8,0},{1,9},{9,1},{2,10},{10,2},{3,11},{11,3},{4,12},{12,4},... | collective-permute-start | bytes 4718600 | tf_op jit(solution)/shard_map/ppermute | solution.py:528
  436.6 16.8 %collective-permute-start.39 = (bf16[2,32,1536]{2,1,0:T(8,128)(2,1)S(1)}, bf16[2,32,1536]{2,1,0:T(8,128)(2,1)S(1)}, u32[]{:S(2)}, u32[]{:S(2)}) collective-permute-start(bf16[2,32,1536]{2,1,0:T(8,128)(2,1)S(1)} %get-tuple-element.79), channel_id=1, source_target_pairs={{4,0},{6,2},{0,4},{2,6},{5,1},{7,3},{1,5},{3,7},{12,8},{14,10},{8,... | collective-permute-start | bytes 589832 | tf_op jit(solution)/shard_map/ppermute | solution.py:533
  436.6 16.8 %collective-permute-start.40 = (bf16[2,32,1536]{2,1,0:T(8,128)(2,1)S(1)}, bf16[2,32,1536]{2,1,0:T(8,128)(2,1)S(1)}, u32[]{:S(2)}, u32[]{:S(2)}) collective-permute-start(bf16[2,32,1536]{2,1,0:T(8,128)(2,1)S(1)} %get-tuple-element.80), channel_id=1, source_target_pairs={{6,0},{0,2},{2,4},{4,6},{7,1},{1,3},{3,5},{5,7},{14,8},{8,10},{10,... | collective-permute-start | bytes 589832 | tf_op jit(solution)/shard_map/ppermute | solution.py:533
  437.0 43.5 %collective-permute-start.42 = (bf16[3,96,1536]{2,1,0:T(8,128)(2,1)}, bf16[3,96,1536]{2,1,0:T(8,128)(2,1)}, u32[]{:S(2)}, u32[]{:S(2)}) collective-permute-start(bf16[3,96,1536]{2,1,0:T(8,128)(2,1)} %get-tuple-element.82), channel_id=1, source_target_pairs={{0,1},{1,0},{2,3},{3,2},{4,5},{5,4},{6,7},{7,6},{8,9},{9,8},{10,11... | collective-permute-start | bytes 2654216 | tf_op jit(solution)/shard_map/ppermute | solution.py:528
  453.5 25.9 %collective-permute-start.41 = (bf16[128,1536]{1,0:T(8,128)(2,1)S(1)}, bf16[128,1536]{1,0:T(8,128)(2,1)}, u32[]{:S(2)}, u32[]{:S(2)}) collective-permute-start(bf16[128,1536]{1,0:T(8,128)(2,1)S(1)} %pad_maximum_fusion.8), channel_id=1, source_target_pairs={{0,1},{1,0},{2,3},{3,2},{4,5},{5,4},{6,7},{7,6},{8,9},{9,8},{10,11... | collective-permute-start | bytes 1179656 | tf_op jit(solution)/shard_map/ppermute | solution.py:528
  472.4 42.9 %collective-permute-start.59 = (bf16[2,384,640]{2,1,0:T(8,128)(2,1)}, bf16[2,384,640]{2,1,0:T(8,128)(2,1)}, u32[]{:S(2)}, u32[]{:S(2)}) collective-permute-start(bf16[2,384,640]{2,1,0:T(8,128)(2,1)} %get-tuple-element.91), channel_id=1, source_target_pairs={{0,8},{8,0},{1,9},{9,1},{2,10},{10,2},{3,11},{11,3},{4,12},{12,4},... | collective-permute-start | bytes 2949128 | tf_op jit(solution)/shard_map/ppermute | solution.py:528
  484.7 28.7 %collective-permute-start.44 = (bf16[96,1536]{1,0:T(8,128)(2,1)S(1)}, bf16[96,1536]{1,0:T(8,128)(2,1)S(1)}, u32[]{:S(2)}, u32[]{:S(2)}) collective-permute-start(bf16[96,1536]{1,0:T(8,128)(2,1)S(1)} %get-tuple-element.139), channel_id=1, source_target_pairs={{4,0},{6,2},{0,4},{2,6},{5,1},{7,3},{1,5},{3,7},{12,8},{14,10},{8,... | collective-permute-start | bytes 884744 | tf_op jit(solution)/shard_map/ppermute | solution.py:533
  485.3 28.2 %collective-permute-start.45 = (bf16[96,1536]{1,0:T(8,128)(2,1)S(1)}, bf16[96,1536]{1,0:T(8,128)(2,1)S(1)}, u32[]{:S(2)}, u32[]{:S(2)}) collective-permute-start(bf16[96,1536]{1,0:T(8,128)(2,1)S(1)} %get-tuple-element.138), channel_id=1, source_target_pairs={{6,0},{0,2},{2,4},{4,6},{7,1},{1,3},{3,5},{5,7},{14,8},{8,10},{10,... | collective-permute-start | bytes 884744 | tf_op jit(solution)/shard_map/ppermute | solution.py:533
  541.1 16.7 %all-to-all-start.7 = ((bf16[8,48,640]{2,1,0:T(8,128)(2,1)}), bf16[8,48,640]{2,1,0:T(8,128)(2,1)S(1)}, u32[]{:S(2)}, u32[]{:S(2)}) async-start(bf16[8,48,640]{2,1,0:T(8,128)(2,1)} %bitcast.51), calls=%async_computation.7 | async-start | bytes 983040 | tf_op jit(solution)/shard_map/all_to_all | solution.py:1371
  544.8 49.5 %reduce-scatter.4.cloned.1.call-start = ((), (), s32[]{:S(2)}) async-start(), calls=%async_computation.16 | async-start | bytes 737280 | tf_op jit(solution)/shard_map/reduce_scatter | solution.py:1389
  557.8 22.4 %all-to-all-start.9 = ((bf16[8,48,1024]{2,1,0:T(8,128)(2,1)}), bf16[8,48,1024]{2,1,0:T(8,128)(2,1)S(1)}, u32[]{:S(2)}, u32[]{:S(2)}) async-start(bf16[8,48,1024]{2,1,0:T(8,128)(2,1)} %bitcast.144), calls=%async_computation.11 | async-start | bytes 1572864 | tf_op jit(solution)/shard_map/all_to_all | solution.py:1223
  580.2 17.0 %all-to-all-start.6 = ((f32[32,16,128]{2,1,0:T(8,128)}), f32[32,16,128]{2,1,0:T(8,128)S(1)}, u32[]{:S(2)}, u32[]{:S(2)}) async-start(f32[32,16,128]{2,1,0:T(8,128)} %bitcast.44), calls=%async_computation.6 | async-start | bytes 524288 | tf_op jit(solution)/shard_map/all_to_all | solution.py:1298
  (146 other events, 1310.3 us)
Sparse Core Ops, SparseCore 0:
  10.3 69.1 all-gather.13
  82.4 66.1 all-gather.7
  150.8 66.0 all-gather.9
  218.3 34.7 all-gather.11
  317.3 32.5 reduce-scatter.7
  352.1 65.9 reduce-scatter.5
  472.6 77.8 all-gather.15
  553.3 21.1 reduce-scatter.3

commit v3 on v2

--- a/solution.py
+++ b/solution.py
@@ -537,61 +537,84 @@
     return lax.ppermute(value, "z", [(i, i ^ bit) for i in range(4)])
 
 
-def sum_seq(value):
+def seq_terms(value):
     value = value + flip(value, "x")
-    value = value + swap_z(value, 1)
-    return value + swap_z(value, 2)
-
-
-def gather_plane(value):
-    half = value.shape[0] // 2
-    from_x = flip(value, "x")
+    return [value] + [from_ahead(value, "z", k) for k in (1, 2, 3)]
+
+
+def share(copies):
+    return lax.all_to_all(copies, ("z", "x"), 0, 0, tiled=True)
+
+
+def eight_sum(parts):
+    total = parts[0]
+    for s in range(1, 8):
+        total = total + parts[s]
+    return total
+
+
+def spread(out):
+    for s in range(1, 8):
+        out[s] = out[0]
+
+
+def four_sum(parts):
+    return (parts[0] + parts[2]) + (parts[1] + parts[3])
+
+
+def gather_chips(value):
     from_y = flip(value, "y")
-    far_front = flip(from_y[:half], "x")
-    far_back = flip(from_x[half:], "y")
-    four = jnp.concatenate([value, from_x, from_y, far_front, far_back], axis=0)
-    return jnp.concatenate([four, flip(four, "core")], axis=0)
-
-
-def scatter_plane(value):
-    count = value.shape[0] // 2
-    rows = count // 4
-    half = rows // 2
-    four = value[:count] + flip(value[count:].astype(bf16), "core").astype(f32)
-    own, for_x, for_y, far = [four[i * rows : (i + 1) * rows] for i in range(4)]
-    by_x = flip(jnp.concatenate([for_x[:half], far[:half]]).astype(bf16), "x").astype(f32)
-    by_y = flip(jnp.concatenate([for_y[half:], far[half:]]).astype(bf16), "y").astype(f32)
-    own = own + jnp.concatenate([by_x[:half], by_y[:half]])
-    last_y = flip((for_y[:half] + by_x[half:]).astype(bf16), "y").astype(f32)
-    last_x = flip((for_x[half:] + by_y[half:]).astype(bf16), "x").astype(f32)
-    return own + jnp.concatenate([last_y, last_x])
+    return [value, flip(value, "x"), from_y, flip(from_y, "x")]
 
 
 def gather_clip(value):
-    pair = jnp.stack([value, flip(value, "core")])
-    return jnp.concatenate([pair, flip(pair, "y")])
-
-
-def scatter_clip(value):
-    pair = value[:2] + flip(value[2:], "y")
-    return pair[0] + flip(pair[1], "core")
+    from_y = flip(value, "y")
+    return [value, flip(value, "core"), from_y, flip(from_y, "core")]
+
+
+def together(*values):
+    return lax.optimization_barrier(values)
 
 
 def rms_scale(square_mean):
     return lax.rsqrt(square_mean + epsilon)
 
 
-def on_chip(body, outs, *operands, scalars=0, scratch=()):
-    held = pl.BlockSpec(memory_space=pltpu.SMEM)
-    whole = pl.BlockSpec(memory_space=pltpu.VMEM)
-    return pl.pallas_call(
-        body,
-        out_shape=[jax.ShapeDtypeStruct(shape, kind) for shape, kind in outs],
-        in_specs=[held] * scalars + [whole] * (len(operands) - scalars),
-        out_specs=[whole] * len(outs),
-        scratch_shapes=list(scratch),
-        compiler_params=pltpu.CompilerParams(vmem_limit_bytes=50 * 2**20),
-    )(*operands)
+def whole(shape):
+    return pl.BlockSpec(shape, lambda step: (0,) * len(shape), pipeline_mode=pl.Buffered(1))
+
+
+class Line:
+    def __init__(self):
+        self.last = ()
+
+    def __call__(self, body, outs, *operands, scalars=0, scratch=(), after=(), far=0):
+        held = pl.BlockSpec(memory_space=pltpu.SMEM)
+        unread = pl.BlockSpec(memory_space=pl.ANY)
+        waits = tuple(after) + self.last
+        count, skip = len(operands), len(waits)
+
+        def run(*refs):
+            body(*refs[:count], *refs[count + skip :])
+
+        given = pl.pallas_call(
+            run,
+            out_shape=[jax.ShapeDtypeStruct(shape, kind) for shape, kind in outs],
+            grid=(1,),
+            in_specs=[held] * scalars
+            + [whole(value.shape) for value in operands[scalars : count - far]]
+            + [unread] * far
+            + [unread] * skip,
+            out_specs=[whole(shape) for shape, kind in outs],
+            scratch_shapes=list(scratch),
+            compiler_params=pltpu.CompilerParams(vmem_limit_bytes=50 * 2**20),
+        )(*operands, *waits)
+        self.last = (min(given, key=lambda value: value.size),)
+        return given
+
+
+def alone(*args, **kinds):
+    return Line()(*args, **kinds)
 
 
 def dot(a, b):
@@ -610,7 +633,7 @@
     return -(-value // 128) * 128
 
 
-def prep_body(attn, gateup, cap, attn_out, ffn_out, cap_out):
+def prep_body(attn, gateup, cap, mod, extra, attn_out, ffn_out, cap_out, mod_out):
     width = attn.shape[1] // 3
     cols = width // 8
     pad = attn_out.shape[2] - 3 * cols
@@ -628,6 +651,58 @@
     own = cap_out.shape[2]
     for o in range(32):
         cap_out[o] = cap[:, o * own : (o + 1) * own]
+    span = mod.shape[1]
+    mod_out[:, :span] = mod[...]
+    mod_out[:, span:] = extra[...]
+
+
+def owner_of(place, r):
+    return (place[0] ^ r) * 8 + place[5]
+
+
+def modulate_body(place, cond, p0, p1, p2, p3, out):
+    span = p0.shape[1] - 384
+    chunk = span // 32
+    gain = chunk // 4
+    total = jnp.zeros((8, span), f32)
+    for r, piece in enumerate((p0, p1, p2, p3)):
+        row = cond[pl.ds(owner_of(place, r), 1), :]
+        row = (row / (1.0 + jnp.exp(-row))).astype(bf16).astype(f32)
+        row = jnp.broadcast_to(row, (8, row.shape[1])).astype(bf16)
+        total = total + dot(row, piece[:, :span])
+    out[...] = jnp.zeros(out.shape, f32)
+    for i in range(32):
+        out[i : i + 1, :chunk] = total[0:1, i * chunk : (i + 1) * chunk]
+    for r, piece in enumerate((p0, p1, p2, p3)):
+        extra = piece[0:16, span : span + 256].astype(f32)
+        at = pl.ds(owner_of(place, r), 1)
+        parts = [extra[0:1, :256]] + [extra[8 + g : 9 + g, :gain] for g in range(7)]
+        parts.append(jnp.zeros((1, out.shape[1] - 256 - 7 * gain), f32))
+        out[at, :] = out[at, :] + jnp.concatenate(parts, axis=1)
+
+
+def vector_body(place, a, b, c, d, vector_out, column_out, small, turned):
+    chunk = vector_out.shape[1] // 8
+    gain = chunk // 4
+    small[...] = four_sum([a[...], b[...], c[...], d[...]])
+    vector_out[...] = jnp.zeros(vector_out.shape, f32)
+    for i in range(32):
+        to = (i % 8) * chunk
+        vector_out[i // 8 : i // 8 + 1, to : to + chunk] = small[i : i + 1, :chunk]
+        for g in range(7):
+            vector_out[4 + g : 5 + g, i * gain : (i + 1) * gain] = small[
+                i : i + 1, 256 + g * gain : 256 + (g + 1) * gain
+            ]
+    vector_out[1:2] = jnp.tanh(vector_out[1:2])
+    vector_out[3:4] = jnp.tanh(vector_out[3:4])
+    turned[...] = jnp.zeros(turned.shape, f32)
+    for j in range(4):
+        row = small[pl.ds(place[5] * 4 + j, 1), :]
+        for p in range(3):
+            turned[p : p + 1, j * gain : (j + 1) * gain] = row[
+                :, 256 + (4 + p) * gain : 256 + (5 + p) * gain
+            ]
+    column_out[...] = turned[...].T
 
 
 def caption_slice(weight, s):
@@ -640,43 +715,51 @@
 def caption_body(place, cap, weight, keep_out, send_out):
     for s in range(8):
         own = caption_slice(weight, s)
+        j, k = (s % 2) ^ place[2], (s // 2 - place[1] + 4) % 4
         for r in range(4):
             part = dot(cap[place[0] ^ r], own).astype(bf16)
             if r % 2:
-                send_out[r // 2, s] = part
+                send_out[r // 2, j, k] = part
             else:
-                keep_out[r // 2, s] = part
-
-
-def qkv_body(
-    place, token, w0, w1, w2, w3, vectors, text, normed_out, proj_out, text_out, stats_out
-):
-    total, width = token.shape
+                keep_out[r // 2, j, k] = part
+
+
+def qkv_body(place, tokens, *refs):
+    weights = refs[:4]
+    vector, normed_out, proj_out, stats_out = refs[4:]
+    total, width = tokens.shape
     step = total // 4
     block = width // 4
     cols = width // 8
-    gain, scale = vectors[0:1], vectors[1:2]
+    scale, gain = vector[0:1], vector[4:5]
     for b in range(4):
         at = slice(b * step, (b + 1) * step)
-        value = token[at].astype(f32)
+        value = tokens[at].astype(f32)
         inverse = rms_scale(jnp.mean(value * value, axis=1, keepdims=True))
         normed_out[at] = (value * inverse * gain * (1.0 + scale)).astype(bf16)
     for b in range(4):
         at = slice(b * step, (b + 1) * step)
-        part = jnp.zeros((step, w0.shape[1]), f32)
-        for r, weight in enumerate((w0, w1, w2, w3)):
+        part = jnp.zeros((step, weights[0].shape[1]), f32)
+        for r, weight in enumerate(weights):
             from_col = pl.multiple_of((place[0] ^ r) * block, 128)
             part = part + dot(normed_out[at, pl.ds(from_col, block)], weight[...])
         proj_out[:, at] = part.T
-    text_sum = text[0].astype(f32)
-    for s in range(1, 8):
-        text_sum = text_sum + text[s].astype(f32)
-    text_out[...] = text_sum.T
     stats_out[...] = jnp.zeros(stats_out.shape, f32)
-    query, key, caption_key = proj_out[:cols], proj_out[cols : 2 * cols], text_out[:cols]
+    query, key = proj_out[:cols], proj_out[cols : 2 * cols]
     stats_out[0:1, :] = jnp.sum(query * query, axis=0, keepdims=True)
     stats_out[1:2, :] = jnp.sum(key * key, axis=0, keepdims=True)
-    stats_out[2:3, : text.shape[1]] = jnp.sum(caption_key * caption_key, axis=0, keepdims=True)
+
+
+def add_four_body(keep, got, *outs):
+    for k, out in enumerate(outs):
+        out[...] = (keep[k].astype(f32) + got[k].astype(f32)).astype(bf16)
+
+
+def text_body(a, b, c, d, text_out, stats_out):
+    total = four_sum([v[...].astype(f32) for v in (a, b, c, d)])
+    text_out[...] = total.T
+    key = text_out[: text_out.shape[0] // 2]
+    stats_out[...] = jnp.broadcast_to(jnp.sum(key * key, axis=0, keepdims=True), stats_out.shape)
 
 
 def turn(value, cosine, sine):
@@ -694,23 +777,20 @@
 
 def attend_body(
     heads,
-    gate,
-    length,
     proj,
-    stats,
-    text,
+    stats_a,
+    stats_b,
+    stats_c,
+    stats_d,
     gains,
     cosine,
     sine,
-    mixed_out,
     query_out,
     key_out,
     value_out,
     self_out,
-    cross_out,
     sum_out,
-    text_key_out,
-    text_value_out,
+    stats_out,
 ):
     total = proj.shape[1]
     cols = query_out.shape[0]
@@ -718,38 +798,266 @@
     width = cols * 8
     step = total // 2
     score_scale = dim ** (-0.5)
-    scales = rms_scale(stats[0:3, :] / width)
-    query_scale, key_scale = scales[0:1], scales[1:2]
-    text_scale = scales[2:3, : text.shape[1]]
-    text_key_out[...] = (text[:cols] * text_scale * gains[:, 2:3]).astype(bf16)
-    text_value_out[...] = text[cols : 2 * cols].astype(bf16)
+    stats_out[...] = four_sum([stats_a[...], stats_b[...], stats_c[...], stats_d[...]])
+    scales = rms_scale(stats_out[0:2, :] / width)
     value_out[...] = proj[2 * cols : 3 * cols].astype(bf16)
     sum_out[...] = jnp.zeros(sum_out.shape, f32)
     for h in range(heads):
         at = slice(h * dim, (h + 1) * dim)
-        query = proj[at] * query_scale * gains[at, 0:1]
+        query = proj[at] * scales[0:1] * gains[at, 0:1]
         query_out[at] = turn(query, cosine[...], sine[...]).astype(bf16)
-        key = proj[cols + h * dim : cols + (h + 1) * dim] * key_scale * gains[at, 1:2]
+        key = proj[cols + h * dim : cols + (h + 1) * dim] * scales[1:2] * gains[at, 1:2]
         key_out[at] = turn(key, cosine[...], sine[...]).astype(bf16)
         key_rows = key_out[at].T
-        text_rows = text_key_out[at].T
         for b in range(2):
             to = slice(b * step, (b + 1) * step)
-            block = query_out[at, to]
-            scores = dot(key_rows, block) * score_scale
+            scores = dot(key_rows, query_out[at, to]) * score_scale
             most = jnp.max(scores, axis=0, keepdims=True)
             weights = jnp.exp(scores - most)
             whole = jnp.sum(weights, axis=0, keepdims=True)
             sum_out[h : h + 1, to] = most + jnp.log(whole)
-            own = dot(value_out[at], weights.astype(bf16)) * (1.0 / whole)
-            text_weights = text_softmax(dot(text_rows, block) * score_scale, length[0])
+            self_out[at, to] = dot(value_out[at], weights.astype(bf16)) * (1.0 / whole)
+
+
+def cross_body(
+    heads,
+    gate,
+    length,
+    query,
+    self_out,
+    text,
+    stats_a,
+    stats_b,
+    stats_c,
+    stats_d,
+    squares,
+    gains,
+    mixed_out,
+    cross_out,
+    text_key_out,
+    text_value_out,
+    stats_out,
+):
+    cols, total = query.shape
+    dim = cols // heads
+    width = cols * 8
+    step = total // 2
+    piece = mixed_out.shape[2]
+    score_scale = dim ** (-0.5)
+    text_stats = four_sum([stats_a[...], stats_b[...], stats_c[...], stats_d[...]])
+    stats_out[...] = squares[...]
+    stats_out[2:3, : text.shape[1]] = text_stats[0:1]
+    text_scale = rms_scale(text_stats[0:1] / width)
+    text_key_out[...] = (text[:cols] * text_scale * gains[:cols, 2:3]).astype(bf16)
+    text_value_out[...] = text[cols : 2 * cols].astype(bf16)
+    for h in range(heads):
+        at = slice(h * dim, (h + 1) * dim)
+        text_rows = text_key_out[at].T
+        for b in range(2):
+            to = slice(b * step, (b + 1) * step)
+            text_weights = text_softmax(dot(text_rows, query[at, to]) * score_scale, length[0])
             cross = dot(text_value_out[at], text_weights.astype(bf16))
-            self_out[at, to] = own
             cross_out[at, to] = cross
-            mixed = (own + gate[h] * cross).astype(bf16)
-            piece = mixed_out.shape[2]
+            mixed = (self_out[at, to] + gate[h] * cross).astype(bf16)
             for s in range(step // piece):
                 mixed_out[b * (step // piece) + s, at] = mixed[:, s * piece : (s + 1) * piece]
+
+
+def stack_body(*refs):
+    rows = refs[0].shape[0]
+    for i, piece in enumerate(refs[:-1]):
+        refs[-1][i * rows : (i + 1) * rows] = piece[...]
+
+
+def all_ahead(value):
+    return [value] + [from_ahead(value, "z", k) for k in (1, 2, 3)]
+
+
+def output_weight_body(place, *refs):
+    own = refs[0].shape[0] // 8
+    for r in range(4):
+        for j in range(2):
+            for k in range(4):
+                owner = ((place[0] ^ r) * 4 + (place[1] ^ k)) * 2 + (place[2] ^ j)
+                at = (j * 4 + k) * own
+                refs[4][pl.ds(pl.multiple_of(owner * own, 16), own), :] = refs[r][at : at + own, :]
+
+
+def output_body(
+    mixed, weight, token, vector, proj_out, residual_out, normed_out, plane_out
+):
+    proj = dot_cols(mixed[...], weight[...])
+    proj_out[...] = proj
+    normed = proj * rms_scale(jnp.mean(proj * proj, axis=1, keepdims=True))
+    residual = token[...].astype(f32) + vector[1:2] * normed * vector[5:6]
+    residual_out[...] = residual
+    normed = residual * rms_scale(jnp.mean(residual * residual, axis=1, keepdims=True))
+    normed_out[...] = (normed * vector[6:7] * (1.0 + vector[2:3])).astype(bf16)
+    own = plane_out.shape[1] // 4
+    for g in range(8):
+        for z in range(4):
+            source = (((g // 2) * 4 + z) * 2 + g % 2) * own
+            plane_out[g, z * own : (z + 1) * own] = mixed[source : source + own, :]
+
+
+def spread_out(parts, own_out, mid_out, x_out, y_out):
+    half = own_out.shape[0] // 2
+    own, for_x, for_y, far = parts
+    own_out[...] = own
+    mid_out[:half] = for_y[:half]
+    mid_out[half:] = for_x[half:]
+    x_out[:half] = for_x[:half].astype(bf16)
+    x_out[half:] = far[:half].astype(bf16)
+    y_out[:half] = for_y[half:].astype(bf16)
+    y_out[half:] = far[half:].astype(bf16)
+
+
+def feed_body(*refs):
+    pieces, gateups, downs = refs[:4], refs[4:6], refs[6:8]
+    normed_out, gate_up_out, active_out = refs[8:11]
+    rows = pieces[0].shape[0]
+    hidden = downs[0].shape[0]
+    step = rows * 2
+    for r in range(4):
+        normed_out[r * rows : (r + 1) * rows] = pieces[r][...]
+    parts = []
+    for b in range(2):
+        at = slice(b * step, (b + 1) * step)
+        total = None
+        for core in range(2):
+            both = dot(normed_out[at], gateups[core][...])
+            gate_up_out[core, at] = both
+            gate, up = both[:, :hidden], both[:, hidden:]
+            active = (gate * jax.nn.sigmoid(gate) * up).astype(bf16)
+            active_out[core, at] = active
+            part = dot(active, downs[core][...])
+            total = part if total is None else total + part
+        parts += [total[:rows], total[rows:]]
+    spread_out(parts, *refs[11:])
+
+
+def scatter_two_body(own, mid, by_x, by_y, own_out, y_out, x_out):
+    half = own.shape[0] // 2
+    own_out[:half] = own[:half] + by_x[:half].astype(f32)
+    own_out[half:] = own[half:] + by_y[:half].astype(f32)
+    y_out[...] = (mid[:half] + by_x[half:].astype(f32)).astype(bf16)
+    x_out[...] = (mid[half:] + by_y[half:].astype(f32)).astype(bf16)
+
+
+def scatter_chips(line, own, mid, to_x, to_y, between=None):
+    rows, width = own.shape
+    by_x, by_y = flip(to_x, "x"), flip(to_y, "y")
+    if between is not None:
+        between()
+    own, to_y, to_x = line(
+        scatter_two_body,
+        [((rows, width), f32), ((rows // 2, width), bf16), ((rows // 2, width), bf16)],
+        own,
+        mid,
+        by_x,
+        by_y,
+    )
+    return own, flip(to_y, "y"), flip(to_x, "x")
+
+
+def whole_sum(own, by_y, by_x):
+    half = own.shape[0] // 2
+    return jnp.concatenate(
+        [own[:half] + by_y[...].astype(f32), own[half:] + by_x[...].astype(f32)], axis=0
+    )
+
+
+def rms_pull(normed, inverse, grad):
+    return (grad - normed * jnp.mean(grad * normed, axis=1, keepdims=True)) * inverse
+
+
+def middle_body(own, by_y, by_x, residual, cot, vector, block_out, grad_out, sum_out):
+    down = whole_sum(own, by_y, by_x)
+    inverse = rms_scale(jnp.mean(down * down, axis=1, keepdims=True))
+    normed = down * inverse
+    gate, gain = vector[3:4], vector[7:8]
+    block_out[...] = residual[...] + gate * normed * gain
+    upstream = cot[...].astype(f32)
+    sum_out[...] = jnp.broadcast_to(
+        jnp.sum(upstream * normed, axis=0, keepdims=True), sum_out.shape
+    )
+    grad_out[...] = rms_pull(normed, inverse, upstream * gate * gain).astype(bf16)
+
+
+def feed_back_body(*refs):
+    pieces, gateups, downs, gate_up = refs[:4], refs[4:6], refs[6:8], refs[8]
+    grad_out, hidden_out = refs[9:11]
+    rows = pieces[0].shape[0]
+    hidden = downs[0].shape[0]
+    step = rows * 2
+    for r in range(4):
+        grad_out[r * rows : (r + 1) * rows] = pieces[r][...]
+    parts = []
+    for b in range(2):
+        at = slice(b * step, (b + 1) * step)
+        total = None
+        for core in range(2):
+            active_grad = dot_rows(grad_out[at], downs[core][...])
+            gate, up = gate_up[core, at, :hidden], gate_up[core, at, hidden:]
+            sigmoid = jax.nn.sigmoid(gate)
+            gate_grad = active_grad * up * sigmoid * (1.0 + gate * (1.0 - sigmoid))
+            hidden_out[core, at, :hidden] = gate_grad.astype(bf16)
+            hidden_out[core, at, hidden:] = (active_grad * gate * sigmoid).astype(bf16)
+            part = dot_rows(hidden_out[core, at], gateups[core][...])
+            total = part if total is None else total + part
+        parts += [total[:rows], total[rows:]]
+    spread_out(parts, *refs[11:])
+
+
+def feed_weight_body(active, down_grad, normed, hidden_grad, *outs):
+    width = normed.shape[1]
+    block = width // 4
+    own = block // 4
+    for core in range(2):
+        down_out, gateup_out = outs[core], outs[2 + core]
+        down_out[...] = dot_cols(active[core], down_grad[...]).astype(bf16)
+        for c in range(4):
+            part = dot_cols(normed[:, c * block : (c + 1) * block], hidden_grad[core]).astype(bf16)
+            for z in range(4):
+                gateup_out[z, c * own : (c + 1) * own] = part[z * own : (z + 1) * own]
+
+
+def add_two_body(a, b, c, d, first_out, second_out):
+    first_out[...] = (a[...].astype(f32) + b[...].astype(f32)).astype(bf16)
+    second_out[...] = (c[...].astype(f32) + d[...].astype(f32)).astype(bf16)
+
+
+def residual_back_body(
+    own,
+    by_y,
+    by_x,
+    residual,
+    proj,
+    cot,
+    vector,
+    weight,
+    residual_grad_out,
+    grad_out,
+    mixed_out,
+    sum_out,
+):
+    grad = whole_sum(own, by_y, by_x)
+    value = residual[...]
+    inverse = rms_scale(jnp.mean(value * value, axis=1, keepdims=True))
+    normed = value * inverse
+    sum_out[...] = jnp.zeros(sum_out.shape, f32)
+    sum_out[1:2] = jnp.sum(grad * normed, axis=0, keepdims=True)
+    grad = cot[...].astype(f32) + rms_pull(
+        normed, inverse, grad * vector[6:7] * (1.0 + vector[2:3])
+    )
+    residual_grad_out[...] = grad
+    value = proj[...]
+    inverse = rms_scale(jnp.mean(value * value, axis=1, keepdims=True))
+    normed = value * inverse
+    sum_out[0:1] = jnp.sum(grad * normed, axis=0, keepdims=True)
+    grad = rms_pull(normed, inverse, grad * vector[1:2] * vector[5:6]).astype(bf16)
+    grad_out[...] = grad
+    mixed_out[...] = dot_rows(weight[...], grad).astype(bf16)
 
 
 def text_back_body(
@@ -805,10 +1113,11 @@
         value_out[at] = value_grad * gate[h]
     text_scale = rms_scale(stats[2:3, : text.shape[1]] / width)
     normed = text[:cols] * text_scale
-    gain_out[...] = jnp.broadcast_to(
-        jnp.sum(key_out[...] * normed, axis=1, keepdims=True), gain_out.shape
-    )
-    key_out[...] = key_out[...] * gains[:, 2:3]
+    gain_out[...] = jnp.zeros(gain_out.shape, f32)
+    gain_out[:cols] = jnp.broadcast_to(
+        jnp.sum(key_out[...] * normed, axis=1, keepdims=True), (cols, gain_out.shape[1])
+    )
+    key_out[...] = key_out[...] * gains[:cols, 2:3]
     stats_out[...] = jnp.broadcast_to(
         jnp.sum(key_out[...] * normed, axis=0, keepdims=True), stats_out.shape
     )
@@ -819,27 +1128,43 @@
     width = cols * 8
     text_scale = rms_scale(stats[2:3, : text.shape[1]] / width)
     normed = text[:cols] * text_scale
-    before = (key[...] - normed * (means[0:1, :] / width)) * text_scale
+    mean = eight_sum(means)[2:3, : text.shape[1]] / width
+    before = (key[...] - normed * mean) * text_scale
     grad_out[...] = jnp.concatenate([before, value[...]], axis=0).T.astype(bf16)
 
 
-def caption_back_body(cap, grads, weight, weight_out, cap_out):
+def caption_back_body(place, cap, *refs):
+    grads, (weight, cond, weight_out, piece_out, blocks) = refs[:4], refs[4:]
     cols = weight.shape[1] // 16
+    rows = cap.shape[1]
+    own_rows = rows // 8
+    for j in range(2):
+        for k in range(4):
+            at = slice((j * 4 + k) * rows, (j * 4 + k + 1) * rows)
+            part = None
+            for r in range(4):
+                term = dot_cols(cap[place[0] ^ r], grads[r][at, :])
+                part = term if part is None else part + term
+            blocks[(place[1] + k) % 4 * 2 + (place[2] ^ j)] = part
     for s in range(8):
-        own = caption_slice(weight, s)
-        part = jnp.zeros((cap.shape[2], 2 * cols), f32)
-        for c in range(4):
-            grad = grads[c, s]
-            part = part + dot_cols(cap[c], grad)
-            back = dot_rows(grad, own)
-            if s == 0:
-                cap_out[c] = back
-            else:
-                cap_out[c] = cap_out[c] + back
         for p in range(2):
-            weight_out[:, (p * 8 + s) * cols : (p * 8 + s + 1) * cols] = part[
-                :, p * cols : (p + 1) * cols
+            weight_out[:, (p * 8 + s) * cols : (p * 8 + s + 1) * cols] = blocks[
+                s, :, p * cols : (p + 1) * cols
             ]
+    for s in range(8):
+        blocks[s] = caption_slice(weight, s).astype(f32)
+    for r in range(4):
+        clip = place[0] ^ r
+        total = None
+        for j in range(2):
+            for k in range(4):
+                at = slice((j * 4 + k) * rows, (j * 4 + k + 1) * rows)
+                own = blocks[(place[1] + k) % 4 * 2 + (place[2] ^ j)].astype(bf16)
+                term = dot_rows(grads[r][at, :], own)
+                total = term if total is None else total + term
+        for s in range(8):
+            piece_out[clip * 8 + s, :own_rows] = total[s * own_rows : (s + 1) * own_rows]
+            piece_out[clip * 8 + s, own_rows:] = cond[clip]
 
 
 def attend_back_body(
@@ -851,6 +1176,7 @@
     self_out,
     sums,
     text_query,
+    text_stats,
     proj,
     stats,
     gains,
@@ -868,7 +1194,7 @@
     step = total // 2
     score_scale = dim ** (-0.5)
     scales = rms_scale(stats[0:2, :] / width)
-    stats_out[...] = jnp.zeros(stats_out.shape, f32)
+    stats_out[0] = jnp.zeros(stats_out.shape[1:], f32)
     gain_out[...] = jnp.zeros(gain_out.shape, f32)
     query_total = jnp.zeros((1, total), f32)
     key_total = jnp.zeros((1, total), f32)
@@ -901,66 +1227,46 @@
         key_in_out[at] = key_grad
         query_total = query_total + jnp.sum(query_grad * query_normed, axis=0, keepdims=True)
         key_total = key_total + jnp.sum(key_grad * key_normed, axis=0, keepdims=True)
-    stats_out[0:1, :] = query_total
-    stats_out[1:2, :] = key_total
-
-
-def project_back_body(
-    place,
-    query_in,
-    key_in,
-    value_grad,
-    proj,
-    stats,
-    means,
-    normed,
-    w0,
-    w1,
-    w2,
-    w3,
-    own_out,
-    keep_out,
-    side_out,
-    front1_out,
-    front2_out,
-    front3_out,
-    near_out,
-    far_out,
-    low,
-    turned,
-):
+    stats_out[0, 0:1, :] = query_total
+    stats_out[0, 1:2, :] = key_total
+    stats_out[0, 2:3, : text_stats.shape[1]] = text_stats[0:1]
+    spread(stats_out)
+
+
+def project_back_body(place, *refs):
+    tokens, weights = refs[0], refs[1:5]
+    query_in, key_in, value_grad, proj, stats = refs[5:10]
+    mean_parts, normed, vector = refs[10:13]
+    middle_sums, residual_sums, own_gains, text_gains, gate_sums = refs[13:18]
+    part_out, near_out, far_out, sums_out = refs[18:22]
+    low, turned, unit, sum_out = refs[22:]
     cols, total = query_in.shape
     width = normed.shape[1]
     block = width // 4
     rows = total // 8
-    early = front1_out.shape[1]
     scales = rms_scale(stats[0:2, :] / width)
+    means = eight_sum(mean_parts) / width
     low[...] = jnp.zeros(low.shape, bf16)
     low[:cols] = (
-        (query_in[...] - proj[:cols] * scales[0:1] * (means[0:1, :] / width)) * scales[0:1]
+        (query_in[...] - proj[:cols] * scales[0:1] * means[0:1, :]) * scales[0:1]
     ).astype(bf16)
     low[cols : 2 * cols] = (
-        (key_in[...] - proj[cols : 2 * cols] * scales[1:2] * (means[1:2, :] / width)) * scales[1:2]
+        (key_in[...] - proj[cols : 2 * cols] * scales[1:2] * means[1:2, :]) * scales[1:2]
     ).astype(bf16)
     low[2 * cols : 3 * cols] = value_grad[...]
     turned[...] = low[...].T
-    weights = (w0, w1, w2, w3)
-    fronts = (front1_out, front2_out, front3_out)
-    for k in range(4):
-        for j in range(2):
-            source = (((place[1] + k) % 4) * 2 + (place[2] ^ j)) * rows
-            lines = turned[pl.ds(pl.multiple_of(source, 128), rows), :]
-            for r in range(4):
-                to_col = pl.ds(pl.multiple_of((place[0] ^ r) * block, 128), block)
-                part = dot_rows(lines, weights[r][...]).astype(bf16)
-                if k == 0:
-                    own_out[j, :, to_col] = part
-                else:
-                    fronts[k - 1][j, :, to_col] = part[:early]
-                    if j == 0:
-                        keep_out[k - 1, :, to_col] = part[early:]
-                    else:
-                        side_out[k - 1, :, to_col] = part[early:]
+    sum_out[...] = jnp.zeros(sum_out.shape, f32)
+    for b in range(4):
+        at = slice(b * 2 * rows, (b + 1) * 2 * rows)
+        value = tokens[at].astype(f32)
+        unit[...] = value * rms_scale(jnp.mean(value * value, axis=1, keepdims=True))
+        for r in range(4):
+            to_col = pl.ds(pl.multiple_of((place[0] ^ r) * block, 128), block)
+            part = dot_rows(turned[at], weights[r][...])
+            sum_out[0:1, to_col] = sum_out[0:1, to_col] + jnp.sum(
+                part * unit[:, to_col], axis=0, keepdims=True
+            )
+            part_out[at, to_col] = part.astype(bf16)
     for r in range(4):
         from_col = pl.ds(pl.multiple_of((place[0] ^ r) * block, 128), block)
         part = dot(low[...], normed[:, from_col]).T.astype(bf16)
@@ -968,6 +1274,100 @@
             far_out[r // 2] = part
         else:
             near_out[r // 2] = part
+    sum_out[1:3] = residual_sums[0:2]
+    sum_out[3:4] = middle_sums[0:1]
+    lane = lax.broadcasted_iota(jnp.int32, (1, width), 1)
+    mine = lane // cols == place[5]
+    own_rows, text_row = own_gains[...].T, text_gains[...].T
+    for at, row in ((4, own_rows[0:1]), (5, own_rows[1:2]), (6, text_row[0:1])):
+        wide = jnp.concatenate([row[:, :cols]] * 8, axis=1)
+        sum_out[at : at + 1] = jnp.where(mine, wide, 0.0)
+    heads = 3
+    gates = jnp.zeros((1, width), f32)
+    for h in range(heads):
+        gates = jnp.where(lane == place[5] * heads + h, gate_sums[h : h + 1, 0:1], gates)
+    sum_out[7:8] = gates
+    for s in range(8):
+        sums_out[s] = sum_out[...]
+
+
+def add_body(a, b, out):
+    out[...] = (a[...].astype(f32) + b[...].astype(f32)).astype(bf16)
+
+
+def add_pair_body(keep, got, keep_out, send_out):
+    keep_out[...] = (keep[0].astype(f32) + got[0].astype(f32)).astype(bf16)
+    send_out[...] = (keep[1].astype(f32) + got[1].astype(f32)).astype(bf16)
+
+
+def final_body(grad_normed, residual_grad, token, vector, out):
+    grad = grad_normed[...].astype(f32)
+    value = token[...].astype(f32)
+    inverse = rms_scale(jnp.mean(value * value, axis=1, keepdims=True))
+    out[...] = residual_grad[...] + rms_pull(
+        value * inverse, inverse, grad * vector[4:5] * (1.0 + vector[0:1])
+    )
+
+
+def modulation_back_body(parts, vector, shared_out):
+    sums = eight_sum(parts)
+    width = sums.shape[1]
+    scale_attn, gate_attn, scale_ffn, gate_ffn = [vector[i : i + 1] for i in range(4)]
+    gains = [vector[4 + i : 5 + i] for i in range(4)]
+    zero, one, two, three = [sums[i : i + 1] for i in range(4)]
+    rows = [
+        gains[0] * zero,
+        gains[1] * one * (1.0 - gate_attn * gate_attn),
+        gains[2] * two,
+        gains[3] * three * (1.0 - gate_ffn * gate_ffn),
+    ]
+    shared_out[...] = jnp.zeros(shared_out.shape, f32)
+    for i in range(4):
+        shared_out[i : i + 1] = rows[i]
+    shared_out[4:5] = (1.0 + scale_attn) * zero
+    shared_out[5:6] = gate_attn * one
+    shared_out[6:7] = (1.0 + scale_ffn) * two
+    shared_out[7:8] = gate_ffn * three
+    shared_out[8:12] = sums[4:8]
+
+
+def modulation_weight_body(
+    place, t0, t1, t2, t3, p0, p1, p2, p3, weight_out, total_out, cond_out, square
+):
+    width = t0.shape[1]
+    rows = weight_out.shape[0]
+    span = 4 * width
+    owner = owner_of(place, 0)
+    total_out[...] = (t0[...] + t1[...]) + (t2[...] + t3[...])
+    lane = lax.broadcasted_iota(jnp.int32, (rows, square.shape[0]), 1)
+    columns = []
+    for piece in (p0, p1, p2, p3):
+        cond = piece[:, span + 256 : span + 384].astype(f32)
+        cond = (cond / (1.0 + jnp.exp(-cond))).astype(bf16).astype(f32)
+        square[...] = jnp.zeros(square.shape, f32)
+        square[:rows] = cond
+        turned = square[...].T[:rows]
+        columns.append(jnp.sum(jnp.where(lane == owner, turned, 0.0), axis=1, keepdims=True))
+    for i in range(4):
+        part = None
+        for column, shared in zip(columns, (t0, t1, t2, t3)):
+            term = column * shared[i : i + 1, :]
+            part = term if part is None else part + term
+        weight_out[:, i * width : (i + 1) * width] = part
+    lanes = cond_out.shape[2]
+    for r, shared in enumerate((t0, t1, t2, t3)):
+        back = jnp.zeros((8, rows), f32)
+        for i in range(4):
+            back = back + lax.dot_general(
+                jnp.broadcast_to(shared[i : i + 1, :], (8, width)),
+                p0[:, i * width : (i + 1) * width].astype(f32),
+                (((1,), (1,)), ((), ())),
+                precision=highest,
+                preferred_element_type=f32,
+            )
+        cond_out[place[0] ^ r] = jnp.concatenate(
+            [back, jnp.zeros((8, lanes - rows), f32)], axis=1
+        )
 
 
 def attention_grad_body(pieces, grad_out):
@@ -989,21 +1389,39 @@
                 grad_out[:, target : target + own] = pieces[g, :, source : source + own].astype(f32)
 
 
-def caption_grad_body(pieces, grad_out):
+def caption_grad_body(pieces, grad_out, cond_out):
     own = pieces.shape[2]
+    rows = grad_out.shape[0]
     for o in range(32):
-        grad_out[:, o * own : (o + 1) * own] = pieces[o]
-
-
-def output_grad_body(place, mixed, grad, weight_out):
+        grad_out[:, o * own : (o + 1) * own] = pieces[o, :rows]
+        cond_out[o : o + 1] = pieces[o, rows : rows + 1]
+
+
+def output_grad_body(place, mixed, *refs):
+    grads, weight_outs, held, done = refs[:8], refs[8:12], refs[12], refs[13]
     rows = mixed.shape[2]
+    copies = [
+        pltpu.make_async_copy(grads[r], held.at[pl.ds(r * rows, rows)], done.at[r])
+        for r in range(8)
+    ]
+    for copy in copies:
+        copy.start()
     total = None
     for r in range(8):
+        copies[r].wait()
         core, y, x = r // 4, (r // 2) % 2, r % 2
         source = ((place[3] ^ y) * 2 + (place[4] ^ core)) * 2 + (place[2] ^ x)
-        part = dot(mixed[source], grad[r * rows : (r + 1) * rows])
+        part = dot(mixed[source], held[r * rows : (r + 1) * rows])
         total = part if total is None else total + part
-    weight_out[...] = total.astype(bf16)
+    own = total.shape[0] // 4
+    held[: total.shape[0]] = total.astype(bf16)
+    for k in range(4):
+        source = pl.multiple_of((place[1] + k) % 4 * own, 16)
+        weight_outs[k][...] = held[pl.ds(source, own), :]
+
+
+def output_sum_body(a, b, c, d, out):
+    out[...] = four_sum([v[...].astype(f32) for v in (a, b, c, d)])
 
 
 def local_fast(
@@ -1042,209 +1460,278 @@
     seq_at = z_at * 2 + x_at
     clip_at = y_at * 2 + core_at
     owner = clip_at * 8 + seq_at
-    place = jnp.stack([clip_at, z_at, x_at, y_at, core_at]).astype(jnp.int32)
-
+    place = jnp.stack([clip_at, z_at, x_at, y_at, core_at, seq_at]).astype(jnp.int32)
+
+    line = Line()
     own_tokens = tokens[0]
     token_all = lax.all_gather(own_tokens, seq_axes, axis=0, tiled=True)
-    full_out = lax.all_gather(w_output, all_axes, axis=0, tiled=True)
 
     cap_cols = w_caption.shape[0]
     hidden_own = w_down.shape[0]
     hidden = 4 * hidden_own
-    attn_piece, ffn_piece, cap_piece = on_chip(
+    cond_rows, span = w_modulation.shape
+    bias_len = mod_bias.shape[0]
+    gain_cols = norm_gains.shape[1]
+    cond_square = condition.reshape(32, cond_rows)
+    extra = jnp.concatenate(
+        [
+            jnp.pad(mod_bias[None], ((0, 31), (0, 256 - bias_len)))
+            + jnp.pad(norm_gains, ((8, 17), (0, 256 - gain_cols))),
+            jnp.pad(cond_square, ((0, 0), (0, 128 - cond_rows))),
+        ],
+        axis=1,
+    )
+    attn_piece, ffn_piece, cap_piece, mod_piece = alone(
         prep_body,
         [
             ((8, attn_rows, wide_cols), bf16),
             ((8, w_gateup.shape[0], 8 * hidden_own), bf16),
             ((32, text_rows, cap_cols), bf16),
+            ((cond_rows, span + 384), bf16),
         ],
         w_attention,
         w_gateup,
         caption[0],
-    )
-    cap_all = lax.all_to_all(cap_piece, all_axes, 0, 0, tiled=True).reshape(
-        4, text_total, cap_cols
-    )
+        w_modulation,
+        extra,
+    )
+    mod_y, mod_core = flip(mod_piece, "y"), flip(mod_piece, "core")
     attn_0 = lax.all_to_all(attn_piece, seq_axes, 0, 0, tiled=True).reshape(-1, wide_cols)
-    attn_2 = flip(attn_0, "y")
-    attn_1 = flip(attn_0, "core")
+    mod_piece, mod_y, mod_core, attn_0, cap_piece, ffn_piece = together(
+        mod_piece, mod_y, mod_core, attn_0, cap_piece, ffn_piece
+    )
+
+    mod_parts = [mod_piece, mod_core, mod_y, flip(mod_y, "core")]
+    attn_2, attn_1 = flip(attn_0, "y"), flip(attn_0, "core")
+    cap_all = lax.all_to_all(cap_piece, all_axes, 0, 0, tiled=True)
+    (small,) = line(
+        modulate_body,
+        [((32, 640), f32)],
+        place,
+        cond_square.astype(f32),
+        *mod_parts,
+        scalars=1,
+    )
+    vector, own_gains = line(
+        vector_body,
+        [((16, width), f32), ((256, 128), f32)],
+        place,
+        *seq_terms(small),
+        scalars=1,
+        scratch=[pltpu.VMEM((32, 640), f32), pltpu.VMEM((128, 256), f32)],
+    )
+    vector, attn_0, attn_1, attn_2, cap_all, ffn_piece, own_out, w_down = together(
+        vector, attn_0, attn_1, attn_2, cap_all, ffn_piece, w_output, w_down
+    )
+
+    cap_all = cap_all.reshape(4, text_total, cap_cols)
     attn_3 = flip(attn_2, "core")
-    attn_parts = (attn_0, attn_1, attn_2, attn_3)
-
-    cond_float = condition[0].astype(f32)
-    cond_act = jax.nn.silu(cond_float).astype(bf16)
-    cond_all = gather_clip(cond_act)
-    cond_rows = w_modulation.shape[0]
-    cond_own = lax.dynamic_slice_in_dim(cond_all, owner * cond_rows, cond_rows, 1)
-    mod_part = jnp.dot(cond_own, w_modulation, preferred_element_type=f32)
-    bias_len = mod_bias.shape[0]
-    bias_wide = lax.dynamic_update_slice(
-        jnp.zeros((4 * width,), f32), mod_bias.astype(f32), (owner * bias_len,)
-    )
-    mod_part = mod_part + bias_wide[None]
-    gain_cols = norm_gains.shape[1]
-    gain_wide = lax.dynamic_update_slice(
-        jnp.zeros((7, width), f32), norm_gains.astype(f32), (0, owner * gain_cols)
-    ).reshape(-1)
-    sent = flip(jnp.concatenate([mod_part[2:].reshape(-1), gain_wide]), "y")
-    mod_pair = mod_part[:2] + sent[: 8 * width].reshape(2, -1)
-    gain_wide = gain_wide + sent[8 * width :]
-    sent = flip(jnp.concatenate([mod_pair[1], gain_wide]), "core")
-    small = sum_seq(jnp.concatenate([mod_pair[0], gain_wide]) + sent)
-    modulation = small[: 4 * width].reshape(4, width)
-    gain_rows = small[4 * width :].reshape(7, width)
-    scale_attn = modulation[0]
-    gate_attn = jnp.tanh(modulation[1])
-    scale_ffn = modulation[2]
-    gate_ffn = jnp.tanh(modulation[3])
-    own_gains = lax.dynamic_slice_in_dim(gain_rows[4:], seq_at * cols, cols, 1).T
-    head_low = lax.dynamic_slice_in_dim(head_gate, seq_at * own_heads, own_heads)
-    tanh_gate = jnp.tanh(head_low.astype(f32))
-
-    ffn_piece = lax.all_to_all(ffn_piece, plane_axes, 0, 0, tiled=True)
-    block = 2 * ffn_piece.shape[1]
-    own_gateup = lax.all_gather(ffn_piece.reshape(4, block, -1), "z", axis=0)
-    own_gateup = jnp.transpose(own_gateup, (1, 0, 2, 3)).reshape(width, -1)
-    own_down = lax.all_gather(w_down, "z", axis=0, tiled=True)
-
-    cap_keep, cap_send = on_chip(
+    four_text = (4, text_total, 2 * cols)
+    cap_keep, cap_send = line(
         caption_body,
-        [((2, 8, text_total, 2 * cols), bf16)] * 2,
+        [((2, 2) + four_text, bf16)] * 2,
         place,
         cap_all,
         w_caption,
         scalars=1,
     )
-    cap_pair = cap_keep.astype(f32) + flip(cap_send, "core").astype(f32)
-    cap_one = cap_pair[0] + flip(cap_pair[1].astype(bf16), "y").astype(f32)
-    text_pieces = lax.all_to_all(cap_one.astype(bf16), seq_axes, 0, 0, tiled=True)
-
-    normed_all, projected, text_proj, squares = on_chip(
+    out_near = swap_z(own_out, 1)
+    ffn_piece = lax.all_to_all(ffn_piece, plane_axes, 0, 0, tiled=True)
+    block = 2 * ffn_piece.shape[1]
+    cap_keep, cap_send = line(
+        add_pair_body, [((2,) + four_text, bf16)] * 2, cap_keep, flip(cap_send, "core")
+    )
+    attn_3, cap_send, cap_keep = together(attn_3, cap_send, cap_keep)
+
+    attn_parts = (attn_0, attn_1, attn_2, attn_3)
+    cap_send = flip(cap_send, "y")
+    normed_all, projected, squares = line(
         qkv_body,
-        [
-            ((total, width), bf16),
-            ((wide_cols, total), f32),
-            ((2 * cols, text_total), f32),
-            ((8, total), f32),
-        ],
+        [((total, width), bf16), ((wide_cols, total), f32), ((8, total), f32)],
         place,
         token_all,
         *attn_parts,
-        jnp.stack([gain_rows[0], scale_attn]),
-        text_pieces,
+        vector,
         scalars=1,
     )
-    squares = sum_seq(squares)
+    squares = seq_terms(squares)
+    (out_pair,) = line(
+        stack_body, [((2 * attn_rows, width), bf16)], own_out, out_near, after=(squares[0],)
+    )
+    out_far = swap_z(out_pair, 2)
+    cap_keep, cap_send = line(add_pair_body, [(four_text, bf16)] * 2, cap_keep, cap_send)
+    cap_send = flip(cap_send, "x")
+    text_parts = line(
+        add_four_body, [(four_text[1:], bf16)] * 4, cap_keep, cap_send, after=tuple(squares[1:])
+    )
+    out_far, squares, text_parts, ffn_piece = together(out_far, squares, text_parts, ffn_piece)
+    own_gateup = lax.all_gather(ffn_piece.reshape(4, block, -1), "z", axis=0)
+
+    text_parts = [text_parts[0]] + [from_ahead(text_parts[4 - k], "z", k) for k in (1, 2, 3)]
+    (out_z,) = line(stack_body, [((4 * attn_rows, width), bf16)], out_pair, out_far)
+    out_x = flip(out_z, "x")
+
+    head_low = lax.dynamic_slice_in_dim(head_gate, seq_at * own_heads, own_heads)
+    tanh_gate = jnp.tanh(head_low.astype(f32))
     position = jnp.arange(total, dtype=jnp.int32)
     angles = rope_angles(frame_shape[0], rope_shift[0], position, head_dim // 2).T
     cosine = jnp.cos(angles)
     sine = jnp.sin(angles)
     flat = (cols, total)
-    (
-        mixed_pieces,
-        queries,
-        key_rows,
-        values,
-        self_out,
-        cross_out,
-        log_sum,
-        text_keys,
-        text_values,
-    ) = on_chip(
+    queries, key_rows, values, self_out, log_sum, squares = line(
         functools.partial(attend_body, own_heads),
         [
-            ((8, cols, rows), bf16),
             (flat, bf16),
             (flat, bf16),
             (flat, bf16),
             (flat, f32),
+            ((8, total), f32),
+            ((8, total), f32),
+        ],
+        projected,
+        *squares,
+        own_gains,
+        cosine,
+        sine,
+    )
+    self_out, out_x = together(self_out, out_x)
+    (out_0,) = line(stack_body, [((8 * attn_rows, width), bf16)], out_z, out_x)
+    out_2 = flip(out_0, "y")
+
+    text_proj, text_squares = line(
+        text_body, [((2 * cols, text_total), f32), ((8, text_total), f32)], *text_parts
+    )
+    text_squares = seq_terms(text_squares)
+    mixed_pieces, cross_out, text_keys, text_values, squares = line(
+        functools.partial(cross_body, own_heads),
+        [
+            ((8, cols, rows), bf16),
             (flat, f32),
-            ((8, total), f32),
             ((cols, text_total), bf16),
             ((cols, text_total), bf16),
+            ((8, total), f32),
         ],
         tanh_gate,
         caption_len,
-        projected,
+        queries,
+        self_out,
+        text_proj,
+        *text_squares,
         squares,
-        text_proj,
         own_gains,
-        cosine,
-        sine,
         scalars=2,
     )
-
+    mixed_pieces, out_2, out_0 = together(mixed_pieces, out_2, out_0)
     mixed_own = lax.all_to_all(mixed_pieces, seq_axes, 0, 0, tiled=True).reshape(width, rows)
-    attn_proj = lax.dot_general(
-        mixed_own, full_out, (((0,), (0,)), ((), ())), preferred_element_type=f32
-    )
-    attn_scale = rms_scale(jnp.mean(attn_proj * attn_proj, axis=-1, keepdims=True))
-    attn_normed = attn_proj * attn_scale
-    own_float = own_tokens.astype(f32)
-    token_scale = rms_scale(jnp.mean(own_float * own_float, axis=-1, keepdims=True))
-    token_normed = own_float * token_scale
-    residual = own_float + gate_attn * attn_normed * gain_rows[1]
-    residual_scale = rms_scale(jnp.mean(residual * residual, axis=-1, keepdims=True))
-    residual_normed = residual * residual_scale
-    normed_ffn = (residual_normed * gain_rows[2] * (1.0 + scale_ffn)).astype(bf16)
-
-    normed_ffn_all = gather_plane(normed_ffn)
-    gate_up = jnp.dot(normed_ffn_all, own_gateup, preferred_element_type=f32)
-    gate_part = gate_up[:, :hidden]
-    up_part = gate_up[:, hidden:]
-    gate_sigmoid = jax.nn.sigmoid(gate_part)
-    activated = (gate_part * gate_sigmoid * up_part).astype(bf16)
-    down_proj = scatter_plane(jnp.dot(activated, own_down, preferred_element_type=f32))
-    down_scale = rms_scale(jnp.mean(down_proj * down_proj, axis=-1, keepdims=True))
-    down_normed = down_proj * down_scale
-    block_out = residual + gate_ffn * down_normed * gain_rows[3]
-
-    upstream = cotangent[0].astype(f32)
-    sum_three = jnp.sum(upstream * down_normed, axis=0)
-    grad_in = upstream * gate_ffn * gain_rows[3]
-    grad_down = (
-        (grad_in - down_normed * jnp.mean(grad_in * down_normed, axis=-1, keepdims=True))
-        * down_scale
-    ).astype(bf16)
-    grad_down_all = gather_plane(grad_down)
-    wgrad_down = jnp.dot(activated.T, grad_down_all, preferred_element_type=f32)
-    grad_act = jnp.dot(grad_down_all, own_down.T, preferred_element_type=f32)
-    grad_gate_part = grad_act * up_part * gate_sigmoid * (1.0 + gate_part * (1.0 - gate_sigmoid))
-    grad_up_part = grad_act * gate_part * gate_sigmoid
-    grad_gate_up = jnp.concatenate([grad_gate_part, grad_up_part], axis=1).astype(bf16)
-    grad_normed_ffn = scatter_plane(
-        jnp.dot(grad_gate_up, own_gateup.T, preferred_element_type=f32)
-    )
-    wgrad_gateup = jnp.dot(normed_ffn_all.T, grad_gate_up, preferred_element_type=f32)
-    wgrad_gateup = jnp.transpose(
-        wgrad_gateup.astype(bf16).reshape(4, 4, block, -1), (1, 0, 2, 3)
+    out_1, out_3 = flip(out_0, "core"), flip(out_2, "core")
+    (full_out,) = line(
+        output_weight_body,
+        [((width, width), bf16)],
+        place,
+        out_0,
+        out_1,
+        out_2,
+        out_3,
+        scalars=1,
+    )
+    own_gateup, mixed_own, w_down, full_out = together(own_gateup, mixed_own, w_down, full_out)
+    own_down = lax.all_gather(w_down, "z", axis=0, tiled=True)
+    own_gateup = jnp.transpose(own_gateup, (1, 0, 2, 3)).reshape(width, -1)
+    gateups = (own_gateup, flip(own_gateup, "core"))
+    own_shape = (rows, width)
+    attn_proj, residual, normed_ffn, mixed_plane = line(
+        output_body,
+        [
+            (own_shape, f32),
+            (own_shape, f32),
+            (own_shape, bf16),
+            ((8, 4 * attn_rows, rows), bf16),
+        ],
+        mixed_own,
+        full_out,
+        own_tokens,
+        vector,
+    )
+
+    chip_shape = (4 * rows, width)
+    on_way = [(own_shape, f32), (own_shape, f32), (own_shape, bf16), (own_shape, bf16)]
+    normed_parts = gather_chips(normed_ffn)
+    own_down = together(own_down, normed_parts[1], normed_parts[3])[0]
+    downs = (own_down, flip(own_down, "core"))
+    normed_ffn_all, gate_up, activated, *parts = line(
+        feed_body,
+        [
+            (chip_shape, bf16),
+            ((2, 4 * rows, 2 * hidden), f32),
+            ((2, 4 * rows, hidden), bf16),
+        ]
+        + on_way,
+        *normed_parts,
+        *gateups,
+        *downs,
+    )
+    block_out, grad_down, middle_sums = line(
+        middle_body,
+        [(own_shape, f32), (own_shape, bf16), ((8, width), f32)],
+        *scatter_chips(line, *parts),
+        residual,
+        cotangent[0],
+        vector,
+    )
+
+    grad_down_all, grad_gate_up, *parts = line(
+        feed_back_body,
+        [(chip_shape, bf16), ((2, 4 * rows, 2 * hidden), bf16)] + on_way,
+        *gather_chips(grad_down),
+        *gateups,
+        *downs,
+        gate_up,
+    )
+    ffn_grads = []
+
+    def feed_weights():
+        ffn_grads.extend(
+            line(
+                feed_weight_body,
+                [((hidden, width), bf16)] * 2 + [((4, 4 * block, 2 * hidden), bf16)] * 2,
+                activated,
+                grad_down_all,
+                normed_ffn_all,
+                grad_gate_up,
+            )
+        )
+
+    ffn_parts = scatter_chips(line, *parts, feed_weights)
+    down_got, gateup_got = flip(ffn_grads[1], "core"), flip(ffn_grads[3], "core")
+
+    wgrad_down, wgrad_gateup = line(
+        add_two_body,
+        [((hidden, width), bf16), ((4, 4 * block, 2 * hidden), bf16)],
+        ffn_grads[0],
+        down_got,
+        ffn_grads[2],
+        gateup_got,
     )
     wgrad_gateup = lax.psum_scatter(wgrad_gateup, "z", scatter_dimension=0, tiled=False)
-    wgrad_gateup = lax.all_to_all(
-        wgrad_gateup.reshape(8, block // 2, -1), plane_axes, 0, 0, tiled=True
-    )
-    (wgrad_gateup,) = on_chip(gateup_grad_body, [(w_gateup.shape, f32)], wgrad_gateup)
-    wgrad_down = lax.psum_scatter(
-        wgrad_down.astype(bf16), "z", scatter_dimension=0, tiled=True
-    ).astype(f32)
-
-    sum_two = jnp.sum(grad_normed_ffn * residual_normed, axis=0)
-    grad_in = grad_normed_ffn * gain_rows[2] * (1.0 + scale_ffn)
-    grad_residual = (
-        upstream
-        + (grad_in - residual_normed * jnp.mean(grad_in * residual_normed, axis=-1, keepdims=True))
-        * residual_scale
-    )
-    sum_one = jnp.sum(grad_residual * attn_normed, axis=0)
-    grad_in = grad_residual * gate_attn * gain_rows[1]
-    grad_attn = (
-        (grad_in - attn_normed * jnp.mean(grad_in * attn_normed, axis=-1, keepdims=True))
-        * attn_scale
-    ).astype(bf16)
-    grad_mixed = lax.dot_general(
-        full_out, grad_attn, (((1,), (1,)), ((), ())), preferred_element_type=f32
-    ).astype(bf16)
+    wgrad_down = lax.psum_scatter(wgrad_down, "z", scatter_dimension=0, tiled=True)
+
+    grad_residual, grad_attn, grad_mixed, residual_sums = line(
+        residual_back_body,
+        [(own_shape, f32), (own_shape, bf16), ((width, rows), bf16), ((8, width), f32)],
+        *ffn_parts,
+        residual,
+        attn_proj,
+        cotangent[0],
+        vector,
+        full_out,
+    )
     grad_pieces = lax.all_to_all(grad_mixed.reshape(8, cols, rows), seq_axes, 0, 0, tiled=True)
+    grad_by_x, grad_by_y = flip(grad_attn, "x"), flip(grad_attn, "y")
+    grad_pieces, grad_by_x, grad_by_y, mixed_plane = together(
+        grad_pieces, grad_by_x, grad_by_y, mixed_plane
+    )
+    mixed_plane = lax.all_to_all(mixed_plane, plane_axes, 0, 0, tiled=True)
+    grad_far = flip(grad_by_y, "x")
 
     (
         grad_mixed,
@@ -1254,7 +1741,7 @@
         text_stats,
         text_gain,
         gate_sum,
-    ) = on_chip(
+    ) = line(
         functools.partial(text_back_body, own_heads),
         [
             (flat, bf16),
@@ -1262,7 +1749,7 @@
             ((cols, text_total), f32),
             ((cols, text_total), f32),
             ((8, text_total), f32),
-            ((cols, 128), f32),
+            ((256, 128), f32),
             ((8, 128), f32),
         ],
         tanh_gate,
@@ -1277,37 +1764,14 @@
         own_gains,
         scalars=2,
     )
-    text_stats = sum_seq(text_stats)
-    (grad_text_proj,) = on_chip(
-        text_proj_back_body,
-        [((text_total, 2 * cols), bf16)],
-        text_key_in,
-        text_value_grad,
-        text_proj,
-        squares,
-        text_stats,
-    )
-    text_all = lax.all_gather(grad_text_proj, all_axes, axis=0)
-    wgrad_caption, grad_caption = on_chip(
-        caption_back_body,
-        [(w_caption.shape, f32), ((4, text_total, cap_cols), f32)],
-        cap_all,
-        text_all.reshape(4, 8, text_total, 2 * cols),
-        w_caption,
-    )
-    grad_caption = lax.all_to_all(
-        grad_caption.reshape(32, text_rows, cap_cols), all_axes, 0, 0, tiled=True
-    )
-    (grad_caption,) = on_chip(caption_grad_body, [((text_rows, 32 * cap_cols), f32)], grad_caption)
-
-    query_in, key_in, value_grad, means, own_gain_sums = on_chip(
+    query_in, key_in, value_grad, means, own_gain_sums = line(
         functools.partial(attend_back_body, own_heads),
         [
             (flat, f32),
             (flat, f32),
             (flat, bf16),
-            ((8, total), f32),
-            ((cols, 128), f32),
+            ((8, 8, total), f32),
+            ((256, 128), f32),
         ],
         grad_mixed,
         queries,
@@ -1316,29 +1780,36 @@
         self_out,
         log_sum,
         text_query,
+        text_stats,
         projected,
         squares,
         own_gains,
         cosine,
         sine,
     )
-    means = sum_seq(means)
-    early = rows // 4
-    rest = rows - early
+    means, mixed_plane = together(means, mixed_plane)
+    means = share(means)
+    (grad_text_proj,) = line(
+        text_proj_back_body,
+        [((text_total, 2 * cols), bf16)],
+        text_key_in,
+        text_value_grad,
+        text_proj,
+        squares,
+        means,
+    )
+    means, grad_text_proj, grad_far = together(means, grad_text_proj, grad_far)
+
+    text_parts = all_ahead(grad_text_proj)
     quarter = width // 4
-    own_part, keep_part, side_part, front_1, front_2, front_3, near_part, far_part = on_chip(
+    grad_normed, near_part, far_part, sums = line(
         project_back_body,
-        [
-            ((2, rows, width), bf16),
-            ((3, rest, width), bf16),
-            ((3, rest, width), bf16),
-            ((2, early, width), bf16),
-            ((2, early, width), bf16),
-            ((2, early, width), bf16),
-            ((2, quarter, wide_cols), bf16),
-            ((2, quarter, wide_cols), bf16),
-        ],
+        [((total, width), bf16)]
+        + [((2, quarter, wide_cols), bf16)] * 2
+        + [((8, 8, width), f32)],
         place,
+        token_all,
+        *attn_parts,
         query_in,
         key_in,
         value_grad,
@@ -1346,103 +1817,109 @@
         squares,
         means,
         normed_all,
-        *attn_parts,
+        vector,
+        middle_sums,
+        residual_sums,
+        own_gain_sums,
+        text_gain,
+        gate_sum,
         scalars=1,
         scratch=[
             pltpu.VMEM((wide_cols, total), bf16),
             pltpu.VMEM((total, wide_cols), bf16),
+            pltpu.VMEM((2 * rows, width), f32),
+            pltpu.VMEM((8, width), f32),
         ],
     )
-    side = flip(side_part, "x")
-    fronts = [from_ahead((front_3, front_2, front_1)[k - 1], "z", k) for k in (1, 2, 3)]
-    back_sum = keep_part.astype(f32) + side.astype(f32)
-    backs = [from_ahead(back_sum[3 - k].astype(bf16), "z", k) for k in (1, 2, 3)]
-    front_sum = own_part[:, :early].astype(f32)
-    for front in fronts:
-        front_sum = front_sum + front.astype(f32)
-    last = flip(jnp.concatenate([front_sum[1].astype(bf16), own_part[1, early:]]), "x").astype(f32)
-    back_total = own_part[0, early:].astype(f32) + last[early:]
-    for back in backs:
-        back_total = back_total + back.astype(f32)
-    grad_normed = jnp.concatenate([front_sum[0] + last[:early], back_total])
-
-    wgrad_pair = near_part.astype(f32) + flip(far_part, "core").astype(f32)
-    wgrad_one = wgrad_pair[0] + flip(wgrad_pair[1].astype(bf16), "y").astype(f32)
+    grad_normed, far_part, sums, text_parts = together(grad_normed, far_part, sums, text_parts)
+
+    grad_normed = lax.psum_scatter(grad_normed, seq_axes, scatter_dimension=0, tiled=True)
+    (text_z,) = line(stack_body, [((4 * text_total, 2 * cols), bf16)], *text_parts)
+    text_x = flip(text_z, "x")
+    far_part = flip(far_part, "core")
+    wide = (quarter, wide_cols)
+    near_part, far_part = line(add_pair_body, [(wide, bf16)] * 2, near_part, far_part)
+    far_part, text_x, sums = together(far_part, text_x, sums)
+
+    far_part = flip(far_part, "y")
+    sums = share(sums)
+    (text_seq,) = line(stack_body, [((8 * text_total, 2 * cols), bf16)], text_z, text_x)
+    far_part, text_seq = together(far_part, text_seq)
+
+    text_y, text_core = flip(text_seq, "y"), flip(text_seq, "core")
+    (wgrad_attention,) = line(add_body, [(wide, bf16)], near_part, far_part)
+    (shared,) = line(modulation_back_body, [((16, width), f32)], sums, vector)
+    shared_y, shared_core = flip(shared, "y"), flip(shared, "core")
+    wgrad_attention = together(wgrad_attention, sums)[0]
     wgrad_attention = lax.all_to_all(
-        wgrad_one.astype(bf16).reshape(8, attn_rows, wide_cols), seq_axes, 0, 0, tiled=True
-    )
-    (wgrad_attention,) = on_chip(attention_grad_body, [(w_attention.shape, f32)], wgrad_attention)
-
-    mixed_plane = jnp.transpose(
-        mixed_own.reshape(2, 2, 4, 2, attn_rows, rows), (0, 1, 3, 2, 4, 5)
-    ).reshape(8, 4 * attn_rows, rows)
-    mixed_plane = lax.all_to_all(mixed_plane, plane_axes, 0, 0, tiled=True)
-    grad_attn_plane = gather_plane(grad_attn)
-    (wgrad_output,) = on_chip(
+        wgrad_attention.reshape(8, attn_rows, wide_cols), seq_axes, 0, 0, tiled=True
+    )
+    shared_y, shared_core, text_core, text_y, grad_attn, grad_by_x, grad_by_y, grad_far = together(
+        shared_y, shared_core, text_core, text_y, grad_attn, grad_by_x, grad_by_y, grad_far
+    )
+
+    grad_attn_parts = [grad_attn, grad_by_x, grad_by_y, grad_far]
+    grad_attn_parts = grad_attn_parts + [flip(piece, "core") for piece in grad_attn_parts]
+    wgrad_modulation, shared, cond_back = line(
+        modulation_weight_body,
+        [(w_modulation.shape, f32), ((16, width), f32), ((4, 8, cap_cols), f32)],
+        place,
+        shared,
+        shared_core,
+        shared_y,
+        flip(shared_y, "core"),
+        *mod_parts,
+        scalars=1,
+        scratch=[pltpu.VMEM((128, 128), f32)],
+    )
+    wgrad_caption, cap_pieces = line(
+        caption_back_body,
+        [(w_caption.shape, f32), ((32, text_rows + 8, cap_cols), f32)],
+        place,
+        cap_all,
+        text_seq,
+        text_core,
+        text_y,
+        flip(text_y, "core"),
+        w_caption,
+        cond_back,
+        scalars=1,
+        scratch=[pltpu.VMEM((8, cap_cols, 2 * cols), f32)],
+    )
+    cap_pieces, wgrad_attention = together(cap_pieces, wgrad_attention)
+
+    cap_pieces = lax.all_to_all(cap_pieces, all_axes, 0, 0, tiled=True)
+    wgrad_parts = line(
         output_grad_body,
-        [((4 * attn_rows, width), bf16)],
+        [((attn_rows, width), bf16)] * 4,
         place,
         mixed_plane,
-        grad_attn_plane,
+        *grad_attn_parts,
         scalars=1,
-    )
-    wgrad_output = lax.psum_scatter(
-        wgrad_output, "z", scatter_dimension=0, tiled=True
-    ).astype(f32)
-
-    sum_zero = jnp.sum(grad_normed * token_normed, axis=0)
-    grad_in = grad_normed * gain_rows[0] * (1.0 + scale_attn)
-    grad_tokens = (
-        grad_residual
-        + (grad_in - token_normed * jnp.mean(grad_in * token_normed, axis=-1, keepdims=True))
-        * token_scale
-    )
-
-    wide = lax.dynamic_update_slice(
-        jnp.zeros((3, width), f32),
-        jnp.stack([own_gain_sums[:, 0], own_gain_sums[:, 1], text_gain[:, 0]]),
-        (0, seq_at * cols),
-    )
-    gate_wide = lax.dynamic_update_slice(
-        jnp.zeros((128,), f32), gate_sum[:own_heads, 0], (seq_at * own_heads,)
-    )
-    sums = sum_seq(
-        jnp.concatenate([sum_zero, sum_one, sum_two, sum_three, wide.reshape(-1), gate_wide])
-    )
-    sum_zero, sum_one, sum_two, sum_three = sums[: 4 * width].reshape(4, width)
-    grad_mod_own = jnp.concatenate(
-        [
-            gain_rows[0] * sum_zero,
-            gain_rows[1] * sum_one * (1.0 - gate_attn * gate_attn),
-            gain_rows[2] * sum_two,
-            gain_rows[3] * sum_three * (1.0 - gate_ffn * gate_ffn),
-        ]
-    )
-    shared = jnp.concatenate(
-        [
-            (1.0 + scale_attn) * sum_zero,
-            gate_attn * sum_one,
-            (1.0 + scale_ffn) * sum_two,
-            gate_ffn * sum_three,
-            sums[4 * width :],
-        ]
-    )
-    gathered = gather_clip(jnp.concatenate([grad_mod_own, shared]))
-    grad_mod_row = gathered[:, : 4 * width]
-    shared = (gathered[0] + gathered[1] + gathered[2] + gathered[3])[4 * width :]
-    gain_grads = lax.dynamic_slice(
-        shared[: 7 * width].reshape(7, width), (0, owner * gain_cols), (7, gain_cols)
-    )
-    grad_gate_total = shared[7 * width : 7 * width + heads]
-    bias_grad = lax.dynamic_slice(
-        jnp.sum(grad_mod_row, axis=0), (owner * bias_len,), (bias_len,)
-    )
-    wgrad_modulation = jnp.dot(cond_own.astype(f32).T, grad_mod_row, precision=highest)
-    cond_back = jnp.dot(grad_mod_row, w_modulation.astype(f32).T, precision=highest)
-    cond_wide = lax.dynamic_update_slice(
-        jnp.zeros((4, cond_float.shape[0]), f32), cond_back, (0, owner * cond_rows)
-    )
-    cond_back = sum_seq(scatter_clip(cond_wide))
+        far=8,
+        scratch=[pltpu.VMEM((total, width), bf16), pltpu.SemaphoreType.DMA((8,))],
+    )
+    wgrad_parts = [wgrad_parts[0]] + [from_ahead(wgrad_parts[4 - k], "z", k) for k in (1, 2, 3)]
+    (wgrad_attention,) = line(attention_grad_body, [(w_attention.shape, f32)], wgrad_attention)
+    cap_pieces, wgrad_gateup = together(cap_pieces, wgrad_gateup)
+
+    wgrad_gateup = lax.all_to_all(
+        wgrad_gateup.reshape(8, block // 2, -1), plane_axes, 0, 0, tiled=True
+    )
+    wgrad_gateup, wgrad_parts = together(wgrad_gateup, wgrad_parts)
+    grad_caption, cond_back = line(
+        caption_grad_body, [((text_rows, 32 * cap_cols), f32), ((32, cap_cols), f32)], cap_pieces
+    )
+    (wgrad_output,) = line(output_sum_body, [((attn_rows, width), f32)], *wgrad_parts)
+    (wgrad_gateup,) = line(gateup_grad_body, [(w_gateup.shape, f32)], wgrad_gateup)
+    (grad_tokens,) = line(
+        final_body, [(own_shape, f32)], grad_normed, grad_residual, own_tokens, vector
+    )
+    bias_grad = lax.dynamic_slice(shared, (clip_at, seq_at * bias_len), (1, bias_len))[0]
+    gain_grads = lax.dynamic_slice(shared, (4, owner * gain_cols), (7, gain_cols))
+    grad_gate_total = shared[11, :heads]
+    cond_back = cond_back[:, :cond_rows].reshape(1, -1)
+    cond_float = condition.astype(f32)
     cond_sigmoid = jax.nn.sigmoid(cond_float)
     grad_condition = cond_back * cond_sigmoid * (1.0 + cond_float * (1.0 - cond_sigmoid))
 
@@ -1450,7 +1927,7 @@
         block_out[None],
         grad_tokens[None],
         grad_caption[None],
-        grad_condition[None],
+        grad_condition,
         wgrad_modulation,
         bias_grad,
         wgrad_attention,
@@ -1459,7 +1936,7 @@
         gain_grads,
         grad_gate_total,
         wgrad_gateup,
-        wgrad_down,
+        wgrad_down.astype(f32),
     )
 
 

time: 615 us -> 595 us (0.967)
  Pallas kernels: 63.2 us -> 132 us
  starting transfers between devices: 162 us -> 119 us
  other arithmetic: 43.7 us -> 7.05 us
  waiting for transfers between devices: 210 us -> 246 us
  matrix products: 33.5 us -> 0 us
  local copies, waits for them, and re-layouts: 62.1 us -> 44.7 us
    pallas_call x13 -> x41, Pallas kernels: 63.2 us -> 132 us  [__call__(): pl.pallas_call(run, out_shape=[jax.ShapeDtypeStruct(shape, kind) for shap...]
    ppermute x48 -> x50, waiting for transfers between devices: 79.1 us -> 117 us  [flip(): return lax.ppermute(value, axis, [(0, 1), (1, 0)])]
    dot_general x11 -> x0, matrix products: 33.5 us -> none  [the longest x1 6.46 us: local_fast(): gate_up = jnp.dot(normed_ffn_all, own_gateup, preferred_element_type=f32)]
    all_to_all x4 -> x5, waiting for transfers between devices: 3.53 us -> 30.8 us  [the longest x2 20.7 us: share(): return lax.all_to_all(copies, ('z', 'x'), 0, 0, tiled=True)]
    ppermute x48 -> x50, starting transfers between devices: 80.3 us -> 53.4 us  [flip(): return lax.ppermute(value, axis, [(0, 1), (1, 0)])]
    ppermute x12 -> x2, waiting for transfers between devices: 25.7 us -> 0.01 us  [swap_z(): return lax.ppermute(value, 'z', [(i, i ^ bit) for i in range(4)])]
    ppermute x6 -> x18, waiting for transfers between devices: 43.2 us -> 62.4 us  [from_ahead(): lax.ppermute(value, axis, [((i + step) % count, i) for i in range(count)])]
    all_gather x1, waiting for transfers between devices: 26.1 us -> 8.55 us  [local_fast(): own_down = lax.all_gather(w_down, 'z', axis=0, tiled=True)]
  transfers between devices with their start and end apart: 83 -> 86, of which waited for: 45 -> 43; matrix products, arithmetic and copies ran while one was open for 16% -> 2% of each run, Pallas kernels for 10% -> 16%
where the time goes in v3:
time: 595 us; the launch traced here: 584 us
  waiting for transfers between devices  246 us (41%)
  Pallas kernels  132 us (22%)
  starting transfers between devices  119 us (20%)
  local copies, waits for them, and re-layouts  44.7 us (8%)
  between operations  18.7 us (3%)
  blocking collectives  16.8 us (3%)
  other arithmetic  7.05 us (1%)
    pallas_call x41, Pallas kernels, __call__(): pl.pallas_call(run, out_shape=[jax.ShapeDtypeStruct(shape, kind) for shap...  132 us
    ppermute x50, waiting for transfers between devices, flip(): return lax.ppermute(value, axis, [(0, 1), (1, 0)])  117 us
    ppermute x18, waiting for transfers between devices, from_ahead(): lax.ppermute(value, axis, [((i + step) % count, i) for i in range(count)])  62.4 us
    ppermute x50, starting transfers between devices, flip(): return lax.ppermute(value, axis, [(0, 1), (1, 0)])  53.4 us
    unnamed x204, local copies, waits for them, and re-layouts  38.7 us
    all_to_all x2, waiting for transfers between devices, share(): return lax.all_to_all(copies, ('z', 'x'), 0, 0, tiled=True)  20.7 us
    all_to_all x1, blocking collectives, local_fast(): cap_pieces = lax.all_to_all(cap_pieces, all_axes, 0, 0, tiled=True)  16.8 us
    ppermute x18, starting transfers between devices, from_ahead(): lax.ppermute(value, axis, [((i + step) % count, i) for i in range(count)])  16.6 us
  transfers between devices with their start and end apart: 86, of which 43 were waited for; matrix products, arithmetic and copies ran while one was open for 2% of the time, Pallas kernels for 16%

profile of v3, /device:TPU:1, one launch (start us, length us, event | category | flops | bytes accessed | tf_op | source)
XLA Modules:
  0.0 584.1 jit_solution(167438639211569834)
XLA Ops:
  16.1 6.4 %all-to-all-start = ((bf16[8,48,640]{2,1,0:T(8,128)(2,1)}), bf16[8,48,640]{2,1,0:T(8,128)(2,1)S(1)}, u32[]{:S(2)}, u32[]{:S(2)}) async-start(bf16[8,48,640]{2,1,0:T(8,128)(2,1)} %get-tuple-element.187), calls=%async_computation | async-start | bytes 983040 | tf_op jit(solution)/shard_map/all_to_all | solution.py:1499
  25.0 7.8 %collective-permute-done.refs_4_.refs_7_ = bf16[32,6528]{1,0:T(8,128)(2,1)S(1)} collective-permute-done((bf16[32,6528]{1,0:T(8,128)(2,1)S(1)}, bf16[32,6528]{1,0:T(8,128)(2,1)S(1)}, u32[]{:S(2)}, u32[]{:S(2)}) %collective-permute-start) | collective-permute-done | bytes 417824 | tf_op jit(solution)/shard_map/ppermute | solution.py:528
  32.8 14.6 %all-to-all-done = bf16[8,48,640]{2,1,0:T(8,128)(2,1)S(1)} async-done(((bf16[8,48,640]{2,1,0:T(8,128)(2,1)}), bf16[8,48,640]{2,1,0:T(8,128)(2,1)S(1)}, u32[]{:S(2)}, u32[]{:S(2)}) %all-to-all-start) | async-done | bytes 491552 | tf_op jit(solution)/shard_map/all_to_all | solution.py:1499
  69.3 11.0 %collective-permute-done.5.refs_3_ = f32[32,640]{1,0:T(8,128)S(1)} collective-permute-done((f32[32,640]{1,0:T(8,128)S(1)}, f32[32,640]{1,0:T(8,128)S(1)}, u32[]{:S(2)}, u32[]{:S(2)}) %collective-permute-start.5) | collective-permute-done | bytes 81952 | tf_op jit(solution)/shard_map/ppermute | solution.py:533
  98.6 9.0 %shard_map.260 = (bf16[1024,1536]{1,0:T(8,128)(2,1)}, f32[640,1024]{1,0:T(8,128)}, f32[8,1024]{1,0:T(8,128)S(1)}) custom-call(s32[6]{0:T(128)S(1)} %stack.27.refs_0_, bf16[1024,1536]{1,0:T(8,128)(2,1)} %bitcast.53, bf16[384,640]{1,0:T(8,128)(2,1)S(1)} %bitcast.41, bf16[384,640]{1,0:T(8,128)(2,1)S(1)} %collective-permute-done.7.refs_3_, ...), custom_call_target="tpu_custom_call" | custom-call | tf_op jit(solution)/shard_map/pallas_call | solution.py:600
  126.0 11.2 %collective-permute-done.15.refs_3_ = f32[8,1024]{1,0:T(8,128)S(1)} collective-permute-done((f32[8,1024]{1,0:T(8,128)S(1)}, f32[8,1024]{1,0:T(8,128)S(1)}, u32[]{:S(2)}, u32[]{:S(2)}) %collective-permute-start.15) | collective-permute-done | bytes 32800 | tf_op jit(solution)/shard_map/ppermute | solution.py:533
  146.2 8.0 %shard_map.265 = (bf16[192,1024]{1,0:T(8,128)(2,1)S(1)}, bf16[192,1024]{1,0:T(8,128)(2,1)S(1)}, bf16[192,1024]{1,0:T(8,128)(2,1)S(1)}, f32[192,1024]{1,0:T(8,128...) custom-call(f32[640,1024]{1,0:T(8,128)} %get-tuple-element.219.refs_0_.refs_8_.refs_9_, ...), custom_call_target="tpu_custom_call" | custom-call | tf_op jit(solution)/shard_map/pallas_call | solution.py:600
  162.8 7.2 %collective-permute-done.20.refs_1_ = bf16[128,384]{1,0:T(8,128)(2,1)S(1)} collective-permute-done((bf16[128,384]{1,0:T(8,128)(2,1)S(1)}, bf16[128,384]{1,0:T(8,128)(2,1)S(1)}, u32[]{:S(2)}, u32[]{:S(2)}) %collective-permute-start.20) | collective-permute-done | bytes 98336 | tf_op jit(solution)/shard_map/ppermute | solution.py:533
  170.0 10.8 %collective-permute-done.21.refs_2_ = bf16[128,384]{1,0:T(8,128)(2,1)S(1)} collective-permute-done((bf16[128,384]{1,0:T(8,128)(2,1)S(1)}, bf16[128,384]{1,0:T(8,128)(2,1)S(1)}, u32[]{:S(2)}, u32[]{:S(2)}) %collective-permute-start.21) | collective-permute-done | bytes 98336 | tf_op jit(solution)/shard_map/ppermute | solution.py:533
  207.5 9.0 %all-to-all-done.3 = bf16[8,192,128]{2,1,0:T(8,128)(2,1)S(1)} async-done(((bf16[8,192,128]{2,1,0:T(8,128)(2,1)}), bf16[8,192,128]{2,1,0:T(8,128)(2,1)S(1)}, u32[]{:S(2)}, u32[]{:S(2)}) %all-to-all-start.3) | async-done | bytes 393248 | tf_op jit(solution)/shard_map/all_to_all | solution.py:1625
  224.6 8.4 %collective-permute-done.31.refs_2_ = bf16[128,1536]{1,0:T(8,128)(2,1)S(1)} collective-permute-done((bf16[128,1536]{1,0:T(8,128)(2,1)S(1)}, bf16[128,1536]{1,0:T(8,128)(2,1)S(1)}, u32[]{:S(2)}, u32[]{:S(2)}) %collective-permute-start.31) | collective-permute-done | bytes 393248 | tf_op jit(solution)/shard_map/ppermute | solution.py:528
  234.3 8.7 %collective-permute-done.32.refs_3_ = bf16[128,1536]{1,0:T(8,128)(2,1)S(1)} collective-permute-done((bf16[128,1536]{1,0:T(8,128)(2,1)S(1)}, bf16[128,1536]{1,0:T(8,128)(2,1)S(1)}, u32[]{:S(2)}, u32[]{:S(2)}) %collective-permute-start.32) | collective-permute-done | bytes 393248 | tf_op jit(solution)/shard_map/ppermute | solution.py:528
  243.8 8.6 %all-gather.7.cloned.1.call-done.refs_6_ = bf16[512,1536]{1,0:T(8,128)(2,1)} async-done(((bf16[128,1536]{1,0:T(8,128)(2,1)}), bf16[512,1536]{1,0:T(8,128)(2,1)}) %all-gather.7.cloned.1.call-update) | async-done | bytes 1572880 | tf_op jit(solution)/shard_map/all_gather | solution.py:1638
  258.5 10.4 %shard_map.271 = (bf16[512,1536]{1,0:T(8,128)(2,1)}, f32[2,512,1024]{2,1,0:T(8,128)}, bf16[2,512,512]{2,1,0:T(8,128)(2,1)}, f32[128,1536]{1,0:T(8,128)S(1)}, f32...) custom-call(bf16[128,1536]{1,0:T(8,128)(2,1)S(1)} %get-tuple-element.246.refs_0_, ...), custom_call_target="tpu_custom_call" | custom-call | tf_op jit(solution)/shard_map/pallas_call | solution.py:600
  271.3 7.9 %collective-permute-done.35.refs_2_ = bf16[128,1536]{1,0:T(8,128)(2,1)S(1)} collective-permute-done((bf16[128,1536]{1,0:T(8,128)(2,1)S(1)}, bf16[128,1536]{1,0:T(8,128)(2,1)S(1)}, u32[]{:S(2)}, u32[]{:S(2)}) %collective-permute-start.35) | collective-permute-done | bytes 393248 | tf_op jit(solution)/shard_map/ppermute | solution.py:528
  288.4 7.4 %collective-permute-done.40.refs_2_ = bf16[128,1536]{1,0:T(8,128)(2,1)S(1)} collective-permute-done((bf16[128,1536]{1,0:T(8,128)(2,1)S(1)}, bf16[128,1536]{1,0:T(8,128)(2,1)S(1)}, u32[]{:S(2)}, u32[]{:S(2)}) %collective-permute-start.40) | collective-permute-done | bytes 393248 | tf_op jit(solution)/shard_map/ppermute | solution.py:528
  296.1 8.1 %collective-permute-done.41.refs_3_ = bf16[128,1536]{1,0:T(8,128)(2,1)S(1)} collective-permute-done((bf16[128,1536]{1,0:T(8,128)(2,1)S(1)}, bf16[128,1536]{1,0:T(8,128)(2,1)S(1)}, u32[]{:S(2)}, u32[]{:S(2)}) %collective-permute-start.41) | collective-permute-done | bytes 393248 | tf_op jit(solution)/shard_map/ppermute | solution.py:528
  304.2 10.6 %shard_map.274 = (bf16[512,1536]{1,0:T(8,128)(2,1)}, bf16[2,512,1024]{2,1,0:T(8,128)(2,1)}, f32[128,1536]{1,0:T(8,128)S(1)}, f32[128,1536]{1,0:T(8,128)S(1)}, bf...) custom-call(bf16[128,1536]{1,0:T(8,128)(2,1)S(1)} %get-tuple-element.260.refs_0_, ...), custom_call_target="tpu_custom_call" | custom-call | tf_op jit(solution)/shard_map/pallas_call | solution.py:600
  314.9 9.6 %shard_map.275 = (bf16[512,1536]{1,0:T(8,128)(2,1)S(1)}, bf16[512,1536]{1,0:T(8,128)(2,1)}, bf16[4,384,1024]{2,1,0:T(8,128)(2,1)}, bf16[4,384,1024]{2,1,0:T(8,128)(2,1)}) custom-call(bf16[2,512,512]{2,1,0:T(8,128)(2,1)S(1)} %copy-done.31, bf16[512,1536]{1,0:T(8,128)(2,1)} %get-tuple-element.268.refs_1_, bf16[512,1536]{1,0:T(8,128)(2,1)} %get-tuple-element.269.refs_2_, ...), custom_call_target="tpu_custom_call" | custom-call | tf_op jit(solution)/shard_map/pallas_call | solution.py:600
  330.9 8.7 %collective-permute-done.42.refs_2_ = bf16[128,1536]{1,0:T(8,128)(2,1)S(1)} collective-permute-done((bf16[128,1536]{1,0:T(8,128)(2,1)S(1)}, bf16[128,1536]{1,0:T(8,128)(2,1)S(1)}, u32[]{:S(2)}, u32[]{:S(2)}) %collective-permute-start.42) | collective-permute-done | bytes 393248 | tf_op jit(solution)/shard_map/ppermute | solution.py:528
  341.9 6.1 %shard_map.277 = (bf16[512,1536]{1,0:T(8,128)(2,1)}, bf16[4,384,1024]{2,1,0:T(8,128)(2,1)}) custom-call(bf16[512,1536]{1,0:T(8,128)(2,1)S(1)} %copy-done.1, bf16[512,1536]{1,0:T(8,128)(2,1)} %copy-done.96, bf16[4,384,1024]{2,1,0:T(8,128)(2,1)} %get-tuple-element.276.refs_2_, bf16[4,384,1024]{2,1,0:T(8,128)(2,1)} %copy-done.95, ...), custom_call_target="tpu_custom_call" | custom-call | tf_op jit(solution)/shard_map/pallas_call | solution.py:600
  368.5 9.2 %collective-permute-done.48.refs_3_ = bf16[128,1536]{1,0:T(8,128)(2,1)} collective-permute-done((bf16[128,1536]{1,0:T(8,128)(2,1)}, bf16[128,1536]{1,0:T(8,128)(2,1)}, u32[]{:S(2)}, u32[]{:S(2)}) %collective-permute-start.48) | collective-permute-done | bytes 393248 | tf_op jit(solution)/shard_map/ppermute | solution.py:528
  377.8 11.2 %all-to-all-done.4.refs_2_ = bf16[8,192,128]{2,1,0:T(8,128)(2,1)S(1)} async-done(((bf16[8,192,128]{2,1,0:T(8,128)(2,1)}), bf16[8,192,128]{2,1,0:T(8,128)(2,1)S(1)}, u32[]{:S(2)}, u32[]{:S(2)}) %all-to-all-start.4) | async-done | bytes 393248 | tf_op jit(solution)/shard_map/all_to_all | solution.py:1728
  389.0 7.0 %all-to-all-start.5 = ((bf16[8,192,128]{2,1,0:T(8,128)(2,1)}), bf16[8,192,128]{2,1,0:T(8,128)(2,1)S(1)}, u32[]{:S(2)}, u32[]{:S(2)}) async-start(bf16[8,192,128]{2,1,0:T(8,128)(2,1)} %copy-done.55), calls=%async_computation.5 | async-start | bytes 786432 | tf_op jit(solution)/shard_map/all_to_all | solution.py:1733
  405.2 11.8 %shard_map.280 = (f32[192,1024]{1,0:T(8,128)S(1)}, f32[192,1024]{1,0:T(8,128)}, bf16[192,1024]{1,0:T(8,128)(2,1)S(1)}, f32[8,8,1024]{2,1,0:T(8,128)}, f32[256,128]{1,0:T(8,128)S(1)}) custom-call(bf16[192,1024]{1,0:T(8,128)(2,1)S(1)} %get-tuple-element.287.refs_0_, bf16[192,1024]{1,0:T(8,128)(2,1)S(1)} %get-tuple-element.226.refs_2_.refs_3_.refs_1_, ...), custom_call_target="tpu_custom_call" | custom-call | tf_op jit(solution)/shard_map/pallas_call | solution.py:600
  423.6 11.2 %all-to-all-done.6.refs_4_.refs_11_ = f32[8,8,1024]{2,1,0:T(8,128)S(1)} async-done(((f32[8,8,1024]{2,1,0:T(8,128)}), f32[8,8,1024]{2,1,0:T(8,128)S(1)}, u32[]{:S(2)}, u32[]{:S(2)}) %all-to-all-start.6) | async-done | bytes 262176 | tf_op jit(solution)/shard_map/all_to_all | solution.py:546
  441.2 13.6 %shard_map.282 = (bf16[1024,1536]{1,0:T(8,128)(2,1)}, bf16[2,384,640]{2,1,0:T(8,128)(2,1)}, bf16[2,384,640]{2,1,0:T(8,128)(2,1)}, f32[8,8,1536]{2,1,0:T(8,128)}) custom-call(s32[6]{0:T(128)S(1)} %copy-done.77, bf16[1024,1536]{1,0:T(8,128)(2,1)} %bitcast.54, bf16[384,640]{1,0:T(8,128)(2,1)S(1)} %bitcast.42, bf16[384,640]{1,0:T(8,128)(2,1)S(1)} %copy-done.9, ...), custom_call_target="tpu_custom_call" | custom-call | tf_op jit(solution)/shard_map/pallas_call | solution.py:600
  465.9 6.5 %collective-permute-done.55.refs_1_ = bf16[512,384]{1,0:T(8,128)(2,1)S(1)} collective-permute-done((bf16[512,384]{1,0:T(8,128)(2,1)S(1)}, bf16[512,384]{1,0:T(8,128)(2,1)S(1)}, u32[]{:S(2)}, u32[]{:S(2)}) %collective-permute-start.55) | collective-permute-done | bytes 393248 | tf_op jit(solution)/shard_map/ppermute | solution.py:528
  478.0 5.7 collective-permute-done.56.refs_1_
  488.6 9.5 %all-to-all-done.7.refs_0_ = f32[8,8,1536]{2,1,0:T(8,128)} async-done(((f32[8,8,1536]{2,1,0:T(8,128)}), f32[8,8,1536]{2,1,0:T(8,128)}, u32[]{:S(2)}, u32[]{:S(2)}) %all-to-all-start.7) | async-done | bytes 393248 | tf_op jit(solution)/shard_map/all_to_all | solution.py:546
  522.2 16.8 %all_to_all.55.refs_0_ = f32[32,24,128]{2,1,0:T(8,128)S(1)} all-to-all(f32[32,24,128]{2,1,0:T(8,128)S(1)} %get-tuple-element.335.refs_10_), channel_id=1, replica_groups=mesh['y'=2,'core'=2,'z'=4,'x'=2] {'y','core','z','x'}, dimensions={0} | all-to-all | bytes 786432 | tf_op jit(solution)/shard_map/all_to_all | solution.py:1891
  560.4 9.7 %collective-permute-done.68.refs_2_ = bf16[48,1536]{1,0:T(8,128)(2,1)S(1)} collective-permute-done((bf16[48,1536]{1,0:T(8,128)(2,1)}, bf16[48,1536]{1,0:T(8,128)(2,1)S(1)}, u32[]{:S(2)}, u32[]{:S(2)}) %collective-permute-start.68) | collective-permute-done | bytes 147488 | tf_op jit(solution)/shard_map/ppermute | solution.py:533
  (418 shorter events, 263.8 us)
Async XLA Ops:
  7.2 91.4 %all-gather.9.cloned.1.call-start = ((), (), s32[]{:S(2)}) async-start(), calls=%async_computation.19 | async-start | bytes 3538944 | tf_op jit(solution)/shard_map/all_gather | solution.py:1467
  16.1 31.3 %all-to-all-start = ((bf16[8,48,640]{2,1,0:T(8,128)(2,1)}), bf16[8,48,640]{2,1,0:T(8,128)(2,1)S(1)}, u32[]{:S(2)}, u32[]{:S(2)}) async-start(bf16[8,48,640]{2,1,0:T(8,128)(2,1)} %get-tuple-element.187), calls=%async_computation | async-start | bytes 983040 | tf_op jit(solution)/shard_map/all_to_all | solution.py:1499
  48.1 33.2 %collective-permute-start.7 = (bf16[384,640]{1,0:T(8,128)(2,1)S(1)}, bf16[384,640]{1,0:T(8,128)(2,1)S(1)}, u32[]{:S(2)}, u32[]{:S(2)}) collective-permute-start(bf16[384,640]{1,0:T(8,128)(2,1)S(1)} %bitcast.39), channel_id=1, source_target_pairs={{0,8},{8,0},{1,9},{9,1},{2,10},{10,2},{3,11},{11,3},{4,12},{12,4},... | collective-permute-start | bytes 1474568 | tf_op jit(solution)/shard_map/ppermute | solution.py:528
  48.1 33.3 %collective-permute-start.8 = (bf16[384,640]{1,0:T(8,128)(2,1)S(1)}, bf16[384,640]{1,0:T(8,128)(2,1)}, u32[]{:S(2)}, u32[]{:S(2)}) collective-permute-start(bf16[384,640]{1,0:T(8,128)(2,1)S(1)} %bitcast.40), channel_id=1, source_target_pairs={{0,16},{16,0},{1,17},{17,1},{2,18},{18,2},{3,19},{19,3},{4,20},{20... | collective-permute-start | bytes 1474568 | tf_op jit(solution)/shard_map/ppermute | solution.py:528
  49.3 32.0 %all-to-all-start.1 = ((bf16[32,16,128]{2,1,0:T(8,128)(2,1)}), bf16[32,16,128]{2,1,0:T(8,128)(2,1)S(1)}, u32[]{:S(2)}, u32[]{:S(2)}) async-start(bf16[32,16,128]{2,1,0:T(8,128)(2,1)} %get-tuple-element.195), calls=%async_computation.1 | async-start | bytes 262144 | tf_op jit(solution)/shard_map/all_to_all | solution.py:1506
  63.8 16.6 %collective-permute-start.5 = (f32[32,640]{1,0:T(8,128)S(1)}, f32[32,640]{1,0:T(8,128)S(1)}, u32[]{:S(2)}, u32[]{:S(2)}) collective-permute-start(f32[32,640]{1,0:T(8,128)S(1)} %add.118.refs_1_), channel_id=1, source_target_pairs={{4,0},{6,2},{0,4},{2,6},{5,1},{7,3},{1,5},{3,7},{12,8},{14,10},{8,... | collective-permute-start | bytes 245768 | tf_op jit(solution)/shard_map/ppermute | solution.py:533
  63.8 16.6 %collective-permute-start.6 = (f32[32,640]{1,0:T(8,128)S(1)}, f32[32,640]{1,0:T(8,128)S(1)}, u32[]{:S(2)}, u32[]{:S(2)}) collective-permute-start(f32[32,640]{1,0:T(8,128)S(1)} %add.118.refs_1_), channel_id=1, source_target_pairs={{6,0},{0,2},{2,4},{4,6},{7,1},{1,3},{3,5},{5,7},{14,8},{8,10},{10,... | collective-permute-start | bytes 245768 | tf_op jit(solution)/shard_map/ppermute | solution.py:533
  91.9 23.3 %collective-permute-start.17 = (bf16[2,4,128,384]{3,2,1,0:T(8,128)(2,1)}, bf16[2,4,128,384]{3,2,1,0:T(8,128)(2,1)}, u32[]{:S(2)}, u32[]{:S(2)}) collective-permute-start(bf16[2,4,128,384]{3,2,1,0:T(8,128)(2,1)} %get-tuple-element.210), channel_id=1, source_target_pairs={{0,16},{16,0},{1,17},{17,1},{2,18},{18,2},{3,19},{19,3},{4,20},{20... | collective-permute-start | bytes 2359304 | tf_op jit(solution)/shard_map/ppermute | solution.py:528
  93.2 46.0 %all-to-all-start.2 = ((bf16[8,48,1024]{2,1,0:T(8,128)(2,1)}), bf16[8,48,1024]{2,1,0:T(8,128)(2,1)}, u32[]{:S(2)}, u32[]{:S(2)}) async-start(bf16[8,48,1024]{2,1,0:T(8,128)(2,1)} %copy-done.36), calls=%async_computation.2 | async-start | bytes 1572864 | tf_op jit(solution)/shard_map/all_to_all | solution.py:1539
  97.9 118.5 %all-gather.5.cloned.1.call-start = ((), (), s32[]{:S(2)}) async-start(), calls=%async_computation.14 | async-start | bytes 3932160 | tf_op jit(solution)/shard_map/all_gather | solution.py:1568
  116.6 20.5 %collective-permute-start.18 = (bf16[4,128,384]{2,1,0:T(8,128)(2,1)S(1)}, bf16[4,128,384]{2,1,0:T(8,128)(2,1)S(1)}, u32[]{:S(2)}, u32[]{:S(2)}) collective-permute-start(bf16[4,128,384]{2,1,0:T(8,128)(2,1)S(1)} %get-tuple-element.212), channel_id=1, source_target_pairs={{0,1},{1,0},{2,3},{3,2},{4,5},{5,4},{6,7},{7,6},{8,9},{9,8},{10,11... | collective-permute-start | bytes 1179656 | tf_op jit(solution)/shard_map/ppermute | solution.py:528
  118.8 20.3 %collective-permute-start.13 = (bf16[96,1536]{1,0:T(8,128)(2,1)S(1)}, bf16[96,1536]{1,0:T(8,128)(2,1)S(1)}, u32[]{:S(2)}, u32[]{:S(2)}) collective-permute-start(bf16[96,1536]{1,0:T(8,128)(2,1)S(1)} %shard_map.261.refs_2_.refs_0_), channel_id=1, source_target_pairs={{0,4},{2,6},{4,0},{6,2},{1,5},{3,7},{5,1},{7,3},{8,12},{10,14},{12... | collective-permute-start | bytes 884744 | tf_op jit(solution)/shard_map/ppermute | solution.py:537
  160.0 35.5 %collective-permute-start.27 = (bf16[384,1536]{1,0:T(8,128)(2,1)S(1)}, bf16[384,1536]{1,0:T(8,128)(2,1)}, u32[]{:S(2)}, u32[]{:S(2)}) collective-permute-start(bf16[384,1536]{1,0:T(8,128)(2,1)S(1)} %shard_map.266.refs_4_.refs_1_), channel_id=1, source_target_pairs={{0,16},{16,0},{1,17},{17,1},{2,18},{18,2},{3,19},{19,3},{4,20},{20... | collective-permute-start | bytes 3538952 | tf_op jit(solution)/shard_map/ppermute | solution.py:528
  161.3 19.5 %collective-permute-start.21 = (bf16[128,384]{1,0:T(8,128)(2,1)S(1)}, bf16[128,384]{1,0:T(8,128)(2,1)S(1)}, u32[]{:S(2)}, u32[]{:S(2)}) collective-permute-start(bf16[128,384]{1,0:T(8,128)(2,1)S(1)} %copy-done.91), channel_id=1, source_target_pairs={{4,0},{6,2},{0,4},{2,6},{5,1},{7,3},{1,5},{3,7},{12,8},{14,10},{8,... | collective-permute-start | bytes 294920 | tf_op jit(solution)/shard_map/ppermute | solution.py:533
  161.9 18.9 %collective-permute-start.22 = (bf16[128,384]{1,0:T(8,128)(2,1)S(1)}, bf16[128,384]{1,0:T(8,128)(2,1)S(1)}, u32[]{:S(2)}, u32[]{:S(2)}) collective-permute-start(bf16[128,384]{1,0:T(8,128)(2,1)S(1)} %copy-done.89), channel_id=1, source_target_pairs={{6,0},{0,2},{2,4},{4,6},{7,1},{1,3},{3,5},{5,7},{14,8},{8,10},{10,... | collective-permute-start | bytes 294920 | tf_op jit(solution)/shard_map/ppermute | solution.py:533
  198.5 17.9 %all-to-all-start.3 = ((bf16[8,192,128]{2,1,0:T(8,128)(2,1)}), bf16[8,192,128]{2,1,0:T(8,128)(2,1)S(1)}, u32[]{:S(2)}, u32[]{:S(2)}) async-start(bf16[8,192,128]{2,1,0:T(8,128)(2,1)} %copy-done.56), calls=%async_computation.3 | async-start | bytes 786432 | tf_op jit(solution)/shard_map/all_to_all | solution.py:1625
  202.2 50.1 %all-gather.7.cloned.1.call-start = ((), (), s32[]{:S(2)}) async-start(), calls=%async_computation.15 | async-start | bytes 1966080 | tf_op jit(solution)/shard_map/all_gather | solution.py:1638
  216.4 322.6 %reduce-scatter.6.cloned.1.call-start = ((), (), s32[]{:S(2)}) async-start(), calls=%async_computation.17 | async-start | bytes 3932160 | tf_op jit(solution)/shard_map/reduce_scatter | solution.py:1715
  216.9 36.2 %collective-permute-start.33 = (bf16[1536,1024]{1,0:T(8,128)(2,1)}, bf16[1536,1024]{1,0:T(8,128)(2,1)}, u32[]{:S(2)}, u32[]{:S(2)}) collective-permute-start(bf16[1536,1024]{1,0:T(8,128)(2,1)} %bitcast.55), channel_id=1, source_target_pairs={{0,8},{8,0},{1,9},{9,1},{2,10},{10,2},{3,11},{11,3},{4,12},{12,4},... | collective-permute-start | bytes 9437192 | tf_op jit(solution)/shard_map/ppermute | solution.py:528
  348.0 196.8 %reduce-scatter.8.cloned.1.call-start = ((), (), s32[]{:S(2)}) async-start(), calls=%async_computation.18 | async-start | bytes 1966080 | tf_op jit(solution)/shard_map/reduce_scatter | solution.py:1716
  362.8 26.2 %all-to-all-start.4 = ((bf16[8,192,128]{2,1,0:T(8,128)(2,1)}), bf16[8,192,128]{2,1,0:T(8,128)(2,1)S(1)}, u32[]{:S(2)}, u32[]{:S(2)}) async-start(bf16[8,192,128]{2,1,0:T(8,128)(2,1)} %bitcast.50), calls=%async_computation.4 | async-start | bytes 786432 | tf_op jit(solution)/shard_map/all_to_all | solution.py:1728
  389.0 29.6 %all-to-all-start.5 = ((bf16[8,192,128]{2,1,0:T(8,128)(2,1)}), bf16[8,192,128]{2,1,0:T(8,128)(2,1)S(1)}, u32[]{:S(2)}, u32[]{:S(2)}) async-start(bf16[8,192,128]{2,1,0:T(8,128)(2,1)} %copy-done.55), calls=%async_computation.5 | async-start | bytes 786432 | tf_op jit(solution)/shard_map/all_to_all | solution.py:1733
  418.6 16.2 %all-to-all-start.6 = ((f32[8,8,1024]{2,1,0:T(8,128)}), f32[8,8,1024]{2,1,0:T(8,128)S(1)}, u32[]{:S(2)}, u32[]{:S(2)}) async-start(f32[8,8,1024]{2,1,0:T(8,128)} %get-tuple-element.297), calls=%async_computation.6 | async-start | bytes 524288 | tf_op jit(solution)/shard_map/all_to_all | solution.py:546
  422.2 150.9 %reduce-scatter.4.cloned.1.call-start = ((), (), s32[]{:S(2)}) async-start(), calls=%async_computation.16 | async-start | bytes 3538944 | tf_op jit(solution)/shard_map/reduce_scatter | solution.py:1836
  436.7 18.1 %collective-permute-start.51 = (bf16[128,384]{1,0:T(8,128)(2,1)S(1)}, bf16[128,384]{1,0:T(8,128)(2,1)S(1)}, u32[]{:S(2)}, u32[]{:S(2)}) collective-permute-start(bf16[128,384]{1,0:T(8,128)(2,1)S(1)} %shard_map.281.refs_19_.refs_0_), channel_id=1, source_target_pairs={{2,0},{4,2},{6,4},{0,6},{3,1},{5,3},{7,5},{1,7},{10,8},{12,10},{14... | collective-permute-start | bytes 294920 | tf_op jit(solution)/shard_map/ppermute | solution.py:533
  439.6 18.1 %collective-permute-start.52 = (bf16[128,384]{1,0:T(8,128)(2,1)S(1)}, bf16[128,384]{1,0:T(8,128)(2,1)S(1)}, u32[]{:S(2)}, u32[]{:S(2)}) collective-permute-start(bf16[128,384]{1,0:T(8,128)(2,1)S(1)} %shard_map.281.refs_19_.refs_0_), channel_id=1, source_target_pairs={{4,0},{6,2},{0,4},{2,6},{5,1},{7,3},{1,5},{3,7},{12,8},{14,10},{8,... | collective-permute-start | bytes 294920 | tf_op jit(solution)/shard_map/ppermute | solution.py:533
  439.6 18.8 %collective-permute-start.53 = (bf16[128,384]{1,0:T(8,128)(2,1)S(1)}, bf16[128,384]{1,0:T(8,128)(2,1)S(1)}, u32[]{:S(2)}, u32[]{:S(2)}) collective-permute-start(bf16[128,384]{1,0:T(8,128)(2,1)S(1)} %shard_map.281.refs_19_.refs_0_), channel_id=1, source_target_pairs={{6,0},{0,2},{2,4},{4,6},{7,1},{1,3},{3,5},{5,7},{14,8},{8,10},{10,... | collective-permute-start | bytes 294920 | tf_op jit(solution)/shard_map/ppermute | solution.py:533
  473.8 24.2 %all-to-all-start.7 = ((f32[8,8,1536]{2,1,0:T(8,128)}), f32[8,8,1536]{2,1,0:T(8,128)}, u32[]{:S(2)}, u32[]{:S(2)}) async-start(f32[8,8,1536]{2,1,0:T(8,128)} %get-tuple-element.324.refs_4_), calls=%async_computation.8 | async-start | bytes 786432 | tf_op jit(solution)/shard_map/all_to_all | solution.py:546
  483.7 24.0 %collective-permute-start.59 = (bf16[1024,384]{1,0:T(8,128)(2,1)S(1)}, bf16[1024,384]{1,0:T(8,128)(2,1)}, u32[]{:S(2)}, u32[]{:S(2)}) collective-permute-start(bf16[1024,384]{1,0:T(8,128)(2,1)S(1)} %shard_map.285.refs_2_), channel_id=1, source_target_pairs={{0,8},{8,0},{1,9},{9,1},{2,10},{10,2},{3,11},{11,3},{4,12},{12,4},... | collective-permute-start | bytes 2359304 | tf_op jit(solution)/shard_map/ppermute | solution.py:528
  486.3 21.4 %collective-permute-start.60 = (bf16[1024,384]{1,0:T(8,128)(2,1)S(1)}, bf16[1024,384]{1,0:T(8,128)(2,1)}, u32[]{:S(2)}, u32[]{:S(2)}) collective-permute-start(bf16[1024,384]{1,0:T(8,128)(2,1)S(1)} %shard_map.285.refs_2_), channel_id=1, source_target_pairs={{0,16},{16,0},{1,17},{17,1},{2,18},{18,2},{3,19},{19,3},{4,20},{20... | collective-permute-start | bytes 2359304 | tf_op jit(solution)/shard_map/ppermute | solution.py:528
  502.6 19.6 %all-to-all-start.8 = ((bf16[8,48,640]{2,1,0:T(8,128)(2,1)}), bf16[8,48,640]{2,1,0:T(8,128)(2,1)S(1)}, u32[]{:S(2)}, u32[]{:S(2)}) async-start(bf16[8,48,640]{2,1,0:T(8,128)(2,1)} %bitcast.27), calls=%async_computation.9 | async-start | bytes 983040 | tf_op jit(solution)/shard_map/all_to_all | solution.py:1854
  539.0 31.0 %all-to-all-start.10 = ((bf16[8,48,1024]{2,1,0:T(8,128)(2,1)}), bf16[8,48,1024]{2,1,0:T(8,128)(2,1)S(1)}, u32[]{:S(2)}, u32[]{:S(2)}) async-start(bf16[8,48,1024]{2,1,0:T(8,128)(2,1)} %bitcast.58), calls=%async_computation.12 | async-start | bytes 1572864 | tf_op jit(solution)/shard_map/all_to_all | solution.py:1906
  (156 other events, 1811.6 us)
Sparse Core Ops, SparseCore 0:
  10.2 80.4 all-gather.8
  139.3 74.9 all-gather.4
  216.6 35.7 all-gather.6
  348.2 66.0 reduce-scatter.5
  416.4 46.7 reduce-scatter.7
  466.7 87.2 reduce-scatter.3

commit v4 on v3

--- a/solution.py
+++ b/solution.py
@@ -1009,22 +1009,20 @@
     spread_out(parts, *refs[11:])
 
 
-def feed_weight_body(active, down_grad, normed, hidden_grad, *outs):
+def down_weight_body(active, down_grad, *outs):
+    for core in range(2):
+        outs[core][...] = dot_cols(active[core], down_grad[...]).astype(bf16)
+
+
+def gateup_weight_body(normed, hidden_grad, *outs):
     width = normed.shape[1]
     block = width // 4
     own = block // 4
     for core in range(2):
-        down_out, gateup_out = outs[core], outs[2 + core]
-        down_out[...] = dot_cols(active[core], down_grad[...]).astype(bf16)
         for c in range(4):
             part = dot_cols(normed[:, c * block : (c + 1) * block], hidden_grad[core]).astype(bf16)
             for z in range(4):
-                gateup_out[z, c * own : (c + 1) * own] = part[z * own : (z + 1) * own]
-
-
-def add_two_body(a, b, c, d, first_out, second_out):
-    first_out[...] = (a[...].astype(f32) + b[...].astype(f32)).astype(bf16)
-    second_out[...] = (c[...].astype(f32) + d[...].astype(f32)).astype(bf16)
+                outs[core][z, c * own : (c + 1) * own] = part[z * own : (z + 1) * own]
 
 
 def residual_back_body(
@@ -1123,14 +1121,34 @@
     )
 
 
-def text_proj_back_body(key, value, text, stats, means, grad_out):
+def text_proj_back_body(key, value, text, stats, means, w0, w1, w2, w3, *outs):
     cols = key.shape[0]
     width = cols * 8
     text_scale = rms_scale(stats[2:3, : text.shape[1]] / width)
     normed = text[:cols] * text_scale
     mean = eight_sum(means)[2:3, : text.shape[1]] / width
     before = (key[...] - normed * mean) * text_scale
-    grad_out[...] = jnp.concatenate([before, value[...]], axis=0).T.astype(bf16)
+    grad = jnp.concatenate([before, value[...]], axis=0).T.astype(bf16)
+    own, wide = w0.shape[0], grad.shape[1]
+    rows = grad.shape[0] * wide // width
+    for k, piece in enumerate((w0, w1, w2, w3)):
+        outs[k][:own] = piece[...]
+        for q in range(width // wide):
+            outs[k][own : own + rows, q * wide : (q + 1) * wide] = grad[
+                q * rows : (q + 1) * rows
+            ]
+
+
+def text_stack_body(a, b, c, d, out):
+    wide = out.shape[1]
+    total = out.shape[0] // 4
+    count = a.shape[1] // wide
+    rows = total // count
+    for k, piece in enumerate((a, b, c, d)):
+        for q in range(count):
+            out[k * total + q * rows : k * total + (q + 1) * rows] = piece[
+                piece.shape[0] - rows :, q * wide : (q + 1) * wide
+            ]
 
 
 def caption_back_body(place, cap, *refs):
@@ -1421,7 +1439,7 @@
 
 
 def output_sum_body(a, b, c, d, out):
-    out[...] = four_sum([v[...].astype(f32) for v in (a, b, c, d)])
+    out[...] = four_sum([v[: out.shape[0]].astype(f32) for v in (a, b, c, d)])
 
 
 def local_fast(
@@ -1536,6 +1554,7 @@
         scalars=1,
     )
     out_near = swap_z(own_out, 1)
+    own_down = lax.all_gather(w_down, "z", axis=0, tiled=True)
     ffn_piece = lax.all_to_all(ffn_piece, plane_axes, 0, 0, tiled=True)
     block = 2 * ffn_piece.shape[1]
     cap_keep, cap_send = line(
@@ -1564,8 +1583,9 @@
     text_parts = line(
         add_four_body, [(four_text[1:], bf16)] * 4, cap_keep, cap_send, after=tuple(squares[1:])
     )
-    out_far, squares, text_parts, ffn_piece = together(out_far, squares, text_parts, ffn_piece)
-    own_gateup = lax.all_gather(ffn_piece.reshape(4, block, -1), "z", axis=0)
+    out_far, squares, text_parts, ffn_piece, own_down = together(
+        out_far, squares, text_parts, ffn_piece, own_down
+    )
 
     text_parts = [text_parts[0]] + [from_ahead(text_parts[4 - k], "z", k) for k in (1, 2, 3)]
     (out_z,) = line(stack_body, [((4 * attn_rows, width), bf16)], out_pair, out_far)
@@ -1594,7 +1614,9 @@
         cosine,
         sine,
     )
-    self_out, out_x = together(self_out, out_x)
+    self_out, out_x, text_parts, ffn_piece = together(self_out, out_x, text_parts, ffn_piece)
+    own_gateup = lax.all_gather(ffn_piece.reshape(4, block, -1), "z", axis=0)
+    own_gateup = jnp.transpose(own_gateup, (1, 0, 2, 3)).reshape(width, -1)
     (out_0,) = line(stack_body, [((8 * attn_rows, width), bf16)], out_z, out_x)
     out_2 = flip(out_0, "y")
 
@@ -1634,10 +1656,7 @@
         out_3,
         scalars=1,
     )
-    own_gateup, mixed_own, w_down, full_out = together(own_gateup, mixed_own, w_down, full_out)
-    own_down = lax.all_gather(w_down, "z", axis=0, tiled=True)
-    own_gateup = jnp.transpose(own_gateup, (1, 0, 2, 3)).reshape(width, -1)
-    gateups = (own_gateup, flip(own_gateup, "core"))
+    mixed_own, full_out = together(mixed_own, full_out)
     own_shape = (rows, width)
     attn_proj, residual, normed_ffn, mixed_plane = line(
         output_body,
@@ -1656,7 +1675,9 @@
     chip_shape = (4 * rows, width)
     on_way = [(own_shape, f32), (own_shape, f32), (own_shape, bf16), (own_shape, bf16)]
     normed_parts = gather_chips(normed_ffn)
-    own_down = together(own_down, normed_parts[1], normed_parts[3])[0]
+    own_gateup = together(own_gateup, normed_parts[1], normed_parts[2])[0]
+    gateups = (own_gateup, flip(own_gateup, "core"))
+    own_down = together(own_down, normed_ffn)[0]
     downs = (own_down, flip(own_down, "core"))
     normed_ffn_all, gate_up, activated, *parts = line(
         feed_body,
@@ -1690,30 +1711,25 @@
     ffn_grads = []
 
     def feed_weights():
-        ffn_grads.extend(
-            line(
-                feed_weight_body,
-                [((hidden, width), bf16)] * 2 + [((4, 4 * block, 2 * hidden), bf16)] * 2,
-                activated,
-                grad_down_all,
-                normed_ffn_all,
-                grad_gate_up,
-            )
-        )
+        down_own, down_other = line(
+            down_weight_body, [((hidden, width), bf16)] * 2, activated, grad_down_all
+        )
+        gateup_own, gateup_other = line(
+            gateup_weight_body,
+            [((4, 4 * block, 2 * hidden), bf16)] * 2,
+            normed_ffn_all,
+            grad_gate_up,
+        )
+        (down_sum,) = line(
+            add_body, [((hidden, width), bf16)], down_own, flip(down_other, "core")
+        )
+        ffn_grads.extend([down_sum, gateup_own, flip(gateup_other, "core")])
 
     ffn_parts = scatter_chips(line, *parts, feed_weights)
-    down_got, gateup_got = flip(ffn_grads[1], "core"), flip(ffn_grads[3], "core")
-
-    wgrad_down, wgrad_gateup = line(
-        add_two_body,
-        [((hidden, width), bf16), ((4, 4 * block, 2 * hidden), bf16)],
-        ffn_grads[0],
-        down_got,
-        ffn_grads[2],
-        gateup_got,
-    )
-    wgrad_gateup = lax.psum_scatter(wgrad_gateup, "z", scatter_dimension=0, tiled=False)
-    wgrad_down = lax.psum_scatter(wgrad_down, "z", scatter_dimension=0, tiled=True)
+    wgrad_down = lax.psum_scatter(ffn_grads[0], "z", scatter_dimension=0, tiled=True)
+    (wgrad_gateup,) = line(
+        add_body, [((4, 4 * block, 2 * hidden), bf16)], ffn_grads[1], ffn_grads[2]
+    )
 
     grad_residual, grad_attn, grad_mixed, residual_sums = line(
         residual_back_body,
@@ -1725,6 +1741,8 @@
         vector,
         full_out,
     )
+    grad_mixed, wgrad_down, wgrad_gateup = together(grad_mixed, wgrad_down, wgrad_gateup)
+    wgrad_gateup = lax.psum_scatter(wgrad_gateup, "z", scatter_dimension=0, tiled=False)
     grad_pieces = lax.all_to_all(grad_mixed.reshape(8, cols, rows), seq_axes, 0, 0, tiled=True)
     grad_by_x, grad_by_y = flip(grad_attn, "x"), flip(grad_attn, "y")
     grad_pieces, grad_by_x, grad_by_y, mixed_plane = together(
@@ -1787,20 +1805,39 @@
         cosine,
         sine,
     )
-    means, mixed_plane = together(means, mixed_plane)
+    means, mixed_plane, grad_attn, grad_by_x, grad_by_y, grad_far = together(
+        means, mixed_plane, grad_attn, grad_by_x, grad_by_y, grad_far
+    )
     means = share(means)
-    (grad_text_proj,) = line(
+    grad_attn_parts = [grad_attn, grad_by_x, grad_by_y, grad_far]
+    grad_attn_parts = grad_attn_parts + [flip(piece, "core") for piece in grad_attn_parts]
+    wgrad_parts = line(
+        output_grad_body,
+        [((attn_rows, width), bf16)] * 4,
+        place,
+        mixed_plane,
+        *grad_attn_parts,
+        scalars=1,
+        far=8,
+        scratch=[pltpu.VMEM((total, width), bf16), pltpu.SemaphoreType.DMA((8,))],
+    )
+    pack = (attn_rows + text_total * 2 * cols // width, width)
+    packs = line(
         text_proj_back_body,
-        [((text_total, 2 * cols), bf16)],
+        [(pack, bf16)] * 4,
         text_key_in,
         text_value_grad,
         text_proj,
         squares,
         means,
-    )
-    means, grad_text_proj, grad_far = together(means, grad_text_proj, grad_far)
-
-    text_parts = all_ahead(grad_text_proj)
+        *wgrad_parts,
+    )
+    means, packs, wgrad_gateup = together(means, packs, wgrad_gateup)
+
+    packs = [packs[0]] + [from_ahead(packs[4 - k], "z", k) for k in (1, 2, 3)]
+    wgrad_gateup = lax.all_to_all(
+        wgrad_gateup.reshape(8, block // 2, -1), plane_axes, 0, 0, tiled=True
+    )
     quarter = width // 4
     grad_normed, near_part, far_part, sums = line(
         project_back_body,
@@ -1831,10 +1868,12 @@
             pltpu.VMEM((8, width), f32),
         ],
     )
-    grad_normed, far_part, sums, text_parts = together(grad_normed, far_part, sums, text_parts)
+    grad_normed, far_part, sums, packs, wgrad_gateup = together(
+        grad_normed, far_part, sums, packs, wgrad_gateup
+    )
 
     grad_normed = lax.psum_scatter(grad_normed, seq_axes, scatter_dimension=0, tiled=True)
-    (text_z,) = line(stack_body, [((4 * text_total, 2 * cols), bf16)], *text_parts)
+    (text_z,) = line(text_stack_body, [((4 * text_total, 2 * cols), bf16)], *packs)
     text_x = flip(text_z, "x")
     far_part = flip(far_part, "core")
     wide = (quarter, wide_cols)
@@ -1844,6 +1883,7 @@
     far_part = flip(far_part, "y")
     sums = share(sums)
     (text_seq,) = line(stack_body, [((8 * text_total, 2 * cols), bf16)], text_z, text_x)
+    (wgrad_gateup,) = line(gateup_grad_body, [(w_gateup.shape, f32)], wgrad_gateup)
     far_part, text_seq = together(far_part, text_seq)
 
     text_y, text_core = flip(text_seq, "y"), flip(text_seq, "core")
@@ -1854,12 +1894,8 @@
     wgrad_attention = lax.all_to_all(
         wgrad_attention.reshape(8, attn_rows, wide_cols), seq_axes, 0, 0, tiled=True
     )
-    shared_y, shared_core, text_core, text_y, grad_attn, grad_by_x, grad_by_y, grad_far = together(
-        shared_y, shared_core, text_core, text_y, grad_attn, grad_by_x, grad_by_y, grad_far
-    )
-
-    grad_attn_parts = [grad_attn, grad_by_x, grad_by_y, grad_far]
-    grad_attn_parts = grad_attn_parts + [flip(piece, "core") for piece in grad_attn_parts]
+    shared_y, shared_core, text_core, text_y = together(shared_y, shared_core, text_core, text_y)
+
     wgrad_modulation, shared, cond_back = line(
         modulation_weight_body,
         [(w_modulation.shape, f32), ((16, width), f32), ((4, 8, cap_cols), f32)],
@@ -1889,29 +1925,12 @@
     cap_pieces, wgrad_attention = together(cap_pieces, wgrad_attention)
 
     cap_pieces = lax.all_to_all(cap_pieces, all_axes, 0, 0, tiled=True)
-    wgrad_parts = line(
-        output_grad_body,
-        [((attn_rows, width), bf16)] * 4,
-        place,
-        mixed_plane,
-        *grad_attn_parts,
-        scalars=1,
-        far=8,
-        scratch=[pltpu.VMEM((total, width), bf16), pltpu.SemaphoreType.DMA((8,))],
-    )
-    wgrad_parts = [wgrad_parts[0]] + [from_ahead(wgrad_parts[4 - k], "z", k) for k in (1, 2, 3)]
     (wgrad_attention,) = line(attention_grad_body, [(w_attention.shape, f32)], wgrad_attention)
-    cap_pieces, wgrad_gateup = together(cap_pieces, wgrad_gateup)
-
-    wgrad_gateup = lax.all_to_all(
-        wgrad_gateup.reshape(8, block // 2, -1), plane_axes, 0, 0, tiled=True
-    )
-    wgrad_gateup, wgrad_parts = together(wgrad_gateup, wgrad_parts)
+    (wgrad_output,) = line(output_sum_body, [((attn_rows, width), f32)], *packs)
+
     grad_caption, cond_back = line(
         caption_grad_body, [((text_rows, 32 * cap_cols), f32), ((32, cap_cols), f32)], cap_pieces
     )
-    (wgrad_output,) = line(output_sum_body, [((attn_rows, width), f32)], *wgrad_parts)
-    (wgrad_gateup,) = line(gateup_grad_body, [(w_gateup.shape, f32)], wgrad_gateup)
     (grad_tokens,) = line(
         final_body, [(own_shape, f32)], grad_normed, grad_residual, own_tokens, vector
     )

time: 595 us -> 584 us (0.982)
  waiting for transfers between devices: 246 us -> 202 us
  local copies, waits for them, and re-layouts: 44.7 us -> 79.5 us
  blocking collectives: 16.8 us -> 0 us
  Pallas kernels: 132 us -> 140 us
  starting transfers between devices: 119 us -> 126 us
    unnamed x204 -> x302, local copies, waits for them, and re-layouts: 38.7 us -> 73.5 us
    ppermute x18 -> x15, waiting for transfers between devices: 62.4 us -> 32.7 us  [from_ahead(): lax.ppermute(value, axis, [((i + step) % count, i) for i in range(count)])]
    all_to_all x1 -> x0, blocking collectives: 16.8 us -> none  [local_fast(): cap_pieces = lax.all_to_all(cap_pieces, all_axes, 0, 0, tiled=True)]
    all_to_all x0 -> x1, waiting for transfers between devices: none -> 12 us  [local_fast(): cap_pieces = lax.all_to_all(cap_pieces, all_axes, 0, 0, tiled=True)]
    all_to_all x1, waiting for transfers between devices: 11.2 us -> 0.01 us  [local_fast(): lax.all_to_all(grad_mixed.reshape(8, cols, rows), seq_axes, 0, 0, tiled=T...]
    ppermute x50, waiting for transfers between devices: 117 us -> 107 us  [flip(): return lax.ppermute(value, axis, [(0, 1), (1, 0)])]
    all_to_all x2, waiting for transfers between devices: 20.7 us -> 10.5 us  [share(): return lax.all_to_all(copies, ('z', 'x'), 0, 0, tiled=True)]
    all_gather x1, waiting for transfers between devices: 8.55 us -> 0.01 us  [local_fast(): own_down = lax.all_gather(w_down, 'z', axis=0, tiled=True)]
  transfers between devices with their start and end apart: 86 -> 84, of which waited for: 43 -> 43; matrix products, arithmetic and copies ran while one was open for 2% -> 2% of each run, Pallas kernels for 16% -> 19%
where the time goes in v4:
time: 584 us; the launch traced here: 573 us
  waiting for transfers between devices  202 us (35%)
  Pallas kernels  140 us (24%)
  starting transfers between devices  126 us (22%)
  local copies, waits for them, and re-layouts  79.5 us (14%)
  between operations  18.8 us (3%)
  other arithmetic  6.04 us (1%)
    pallas_call x43, Pallas kernels, __call__(): pl.pallas_call(run, out_shape=[jax.ShapeDtypeStruct(shape, kind) for shap...  140 us
    ppermute x50, waiting for transfers between devices, flip(): return lax.ppermute(value, axis, [(0, 1), (1, 0)])  107 us
    unnamed x302, local copies, waits for them, and re-layouts  73.5 us
    ppermute x50, starting transfers between devices, flip(): return lax.ppermute(value, axis, [(0, 1), (1, 0)])  54.9 us
    ppermute x15, waiting for transfers between devices, from_ahead(): lax.ppermute(value, axis, [((i + step) % count, i) for i in range(count)])  32.7 us
    all_to_all x1, waiting for transfers between devices, local_fast(): lax.all_to_all(mixed_pieces, seq_axes, 0, 0, tiled=True)  16.5 us
    all_to_all x1, waiting for transfers between devices, local_fast(): lax.all_to_all(attn_piece, seq_axes, 0, 0, tiled=True)  13.8 us
    ppermute x15, starting transfers between devices, from_ahead(): lax.ppermute(value, axis, [((i + step) % count, i) for i in range(count)])  13.3 us
  transfers between devices with their start and end apart: 84, of which 43 were waited for; matrix products, arithmetic and copies ran while one was open for 2% of the time, Pallas kernels for 19%

profile of v4, /device:TPU:1, one launch (start us, length us, event | category | flops | bytes accessed | tf_op | source)
XLA Modules:
  0.0 572.7 jit_solution(11062361029112775630)
XLA Ops:
  16.0 6.4 %all-to-all-start = ((bf16[8,48,640]{2,1,0:T(8,128)(2,1)}), bf16[8,48,640]{2,1,0:T(8,128)(2,1)S(1)}, u32[]{:S(2)}, u32[]{:S(2)}) async-start(bf16[8,48,640]{2,1,0:T(8,128)(2,1)} %get-tuple-element.194), calls=%async_computation | async-start | bytes 983040 | tf_op jit(solution)/shard_map/all_to_all | solution.py:1517
  25.0 7.8 %collective-permute-done.refs_4_.refs_7_ = bf16[32,6528]{1,0:T(8,128)(2,1)S(1)} collective-permute-done((bf16[32,6528]{1,0:T(8,128)(2,1)S(1)}, bf16[32,6528]{1,0:T(8,128)(2,1)S(1)}, u32[]{:S(2)}, u32[]{:S(2)}) %collective-permute-start) | collective-permute-done | bytes 417824 | tf_op jit(solution)/shard_map/ppermute | solution.py:528
  33.6 13.8 %all-to-all-done = bf16[8,48,640]{2,1,0:T(8,128)(2,1)S(1)} async-done(((bf16[8,48,640]{2,1,0:T(8,128)(2,1)}), bf16[8,48,640]{2,1,0:T(8,128)(2,1)S(1)}, u32[]{:S(2)}, u32[]{:S(2)}) %all-to-all-start) | async-done | bytes 491552 | tf_op jit(solution)/shard_map/all_to_all | solution.py:1517
  56.5 5.3 collective-permute-done.3
  69.3 11.1 %collective-permute-done.5.refs_3_ = f32[32,640]{1,0:T(8,128)S(1)} collective-permute-done((f32[32,640]{1,0:T(8,128)S(1)}, f32[32,640]{1,0:T(8,128)S(1)}, u32[]{:S(2)}, u32[]{:S(2)}) %collective-permute-start.5) | collective-permute-done | bytes 81952 | tf_op jit(solution)/shard_map/ppermute | solution.py:533
  98.3 4.7 all-to-all-start.2
  103.2 8.8 %shard_map.260 = (bf16[1024,1536]{1,0:T(8,128)(2,1)}, f32[640,1024]{1,0:T(8,128)}, f32[8,1024]{1,0:T(8,128)S(1)}) custom-call(s32[6]{0:T(128)S(1)} %stack.27.refs_0_, bf16[1024,1536]{1,0:T(8,128)(2,1)} %bitcast.52, bf16[384,640]{1,0:T(8,128)(2,1)S(1)} %bitcast.41, bf16[384,640]{1,0:T(8,128)(2,1)S(1)} %copy-done.12, bf16[384,640]{1,0:T(8,128)(2,1)S(1)} %copy-done.15, ...), custom_call_target="tpu_custom_call" | custom-call | tf_op jit(solution)/shard_map/pallas_call | solution.py:600
  134.3 10.1 %collective-permute-done.15.refs_3_ = f32[8,1024]{1,0:T(8,128)S(1)} collective-permute-done((f32[8,1024]{1,0:T(8,128)S(1)}, f32[8,1024]{1,0:T(8,128)S(1)}, u32[]{:S(2)}, u32[]{:S(2)}) %collective-permute-start.15) | collective-permute-done | bytes 32800 | tf_op jit(solution)/shard_map/ppermute | solution.py:533
  151.1 7.9 %shard_map.265 = (bf16[192,1024]{1,0:T(8,128)(2,1)S(1)}, bf16[192,1024]{1,0:T(8,128)(2,1)S(1)}, bf16[192,1024]{1,0:T(8,128)(2,1)S(1)}, f32[192,1024]{1,0:T(8,128...) custom-call(f32[640,1024]{1,0:T(8,128)} %get-tuple-element.214.refs_0_.refs_8_.refs_9_, f32[8,1024]{1,0:T(8,128)S(1)} %copy-done.83, ...), custom_call_target="tpu_custom_call" | custom-call | tf_op jit(solution)/shard_map/pallas_call | solution.py:600
  187.0 6.4 %collective-permute-done.27.refs_3_ = bf16[384,1536]{1,0:T(8,128)(2,1)} collective-permute-done((bf16[384,1536]{1,0:T(8,128)(2,1)S(1)}, bf16[384,1536]{1,0:T(8,128)(2,1)}, u32[]{:S(2)}, u32[]{:S(2)}) %collective-permute-start.27) | collective-permute-done | bytes 1179680 | tf_op jit(solution)/shard_map/ppermute | solution.py:528
  205.8 16.5 %all-to-all-done.3 = bf16[8,192,128]{2,1,0:T(8,128)(2,1)S(1)} async-done(((bf16[8,192,128]{2,1,0:T(8,128)(2,1)}), bf16[8,192,128]{2,1,0:T(8,128)(2,1)S(1)}, u32[]{:S(2)}, u32[]{:S(2)}) %all-to-all-start.3) | async-done | bytes 393248 | tf_op jit(solution)/shard_map/all_to_all | solution.py:1647
  229.1 6.6 %collective-permute-done.30.refs_1_ = bf16[128,1536]{1,0:T(8,128)(2,1)S(1)} collective-permute-done((bf16[128,1536]{1,0:T(8,128)(2,1)S(1)}, bf16[128,1536]{1,0:T(8,128)(2,1)S(1)}, u32[]{:S(2)}, u32[]{:S(2)}) %collective-permute-start.30) | collective-permute-done | bytes 393248 | tf_op jit(solution)/shard_map/ppermute | solution.py:528
  240.4 9.5 %collective-permute-done.32.refs_3_ = bf16[128,1536]{1,0:T(8,128)(2,1)S(1)} collective-permute-done((bf16[128,1536]{1,0:T(8,128)(2,1)}, bf16[128,1536]{1,0:T(8,128)(2,1)S(1)}, u32[]{:S(2)}, u32[]{:S(2)}) %collective-permute-start.32) | collective-permute-done | bytes 393248 | tf_op jit(solution)/shard_map/ppermute | solution.py:528
  252.1 10.6 %shard_map.271 = (bf16[512,1536]{1,0:T(8,128)(2,1)}, f32[2,512,1024]{2,1,0:T(8,128)}, bf16[2,512,512]{2,1,0:T(8,128)(2,1)}, f32[128,1536]{1,0:T(8,128)S(1)}, f32...) custom-call(bf16[128,1536]{1,0:T(8,128)(2,1)S(1)} %get-tuple-element.257.refs_0_, ...), custom_call_target="tpu_custom_call" | custom-call | tf_op jit(solution)/shard_map/pallas_call | solution.py:600
  264.7 7.2 %collective-permute-done.35.refs_2_ = bf16[128,1536]{1,0:T(8,128)(2,1)S(1)} collective-permute-done((bf16[128,1536]{1,0:T(8,128)(2,1)S(1)}, bf16[128,1536]{1,0:T(8,128)(2,1)S(1)}, u32[]{:S(2)}, u32[]{:S(2)}) %collective-permute-start.35) | collective-permute-done | bytes 393248 | tf_op jit(solution)/shard_map/ppermute | solution.py:528
  280.9 6.0 %collective-permute-done.40.refs_2_ = bf16[128,1536]{1,0:T(8,128)(2,1)S(1)} collective-permute-done((bf16[128,1536]{1,0:T(8,128)(2,1)S(1)}, bf16[128,1536]{1,0:T(8,128)(2,1)S(1)}, u32[]{:S(2)}, u32[]{:S(2)}) %collective-permute-start.40) | collective-permute-done | bytes 393248 | tf_op jit(solution)/shard_map/ppermute | solution.py:528
  287.5 9.8 %collective-permute-done.41.refs_3_ = bf16[128,1536]{1,0:T(8,128)(2,1)S(1)} collective-permute-done((bf16[128,1536]{1,0:T(8,128)(2,1)S(1)}, bf16[128,1536]{1,0:T(8,128)(2,1)S(1)}, u32[]{:S(2)}, u32[]{:S(2)}) %collective-permute-start.41) | collective-permute-done | bytes 393248 | tf_op jit(solution)/shard_map/ppermute | solution.py:528
  297.2 10.8 %shard_map.274 = (bf16[512,1536]{1,0:T(8,128)(2,1)}, bf16[2,512,1024]{2,1,0:T(8,128)(2,1)}, f32[128,1536]{1,0:T(8,128)S(1)}, f32[128,1536]{1,0:T(8,128)S(1)}, bf...) custom-call(bf16[128,1536]{1,0:T(8,128)(2,1)S(1)} %get-tuple-element.272.refs_0_, ...), custom_call_target="tpu_custom_call" | custom-call | tf_op jit(solution)/shard_map/pallas_call | solution.py:600
  317.7 7.2 %shard_map.276 = (bf16[4,384,1024]{2,1,0:T(8,128)(2,1)}, bf16[4,384,1024]{2,1,0:T(8,128)(2,1)}) custom-call(bf16[512,1536]{1,0:T(8,128)(2,1)S(1)} %copy-done.30, bf16[2,512,1024]{2,1,0:T(8,128)(2,1)} %get-tuple-element.284.refs_1_, bf16[512,1536]{1,0:T(8,128)(2,1)S(1)} %get-tuple-element.281.refs_2_.refs_0_), custom_call_target="tpu_custom_call" | custom-call | tf_op jit(solution)/shard_map/pallas_call | solution.py:600
  331.0 8.7 %collective-permute-done.42.refs_2_ = bf16[128,1536]{1,0:T(8,128)(2,1)S(1)} collective-permute-done((bf16[128,1536]{1,0:T(8,128)(2,1)}, bf16[128,1536]{1,0:T(8,128)(2,1)S(1)}, u32[]{:S(2)}, u32[]{:S(2)}) %collective-permute-start.42) | collective-permute-done | bytes 393248 | tf_op jit(solution)/shard_map/ppermute | solution.py:528
  344.8 5.2 shard_map.279.refs_8_
  354.4 5.6 shard_map.280
  369.2 10.9 %collective-permute-done.48.refs_3_ = bf16[128,1536]{1,0:T(8,128)(2,1)} collective-permute-done((bf16[128,1536]{1,0:T(8,128)(2,1)}, bf16[128,1536]{1,0:T(8,128)(2,1)}, u32[]{:S(2)}, u32[]{:S(2)}) %collective-permute-start.48) | collective-permute-done | bytes 393248 | tf_op jit(solution)/shard_map/ppermute | solution.py:528
  381.4 12.9 %all-to-all-start.5 = ((bf16[8,192,128]{2,1,0:T(8,128)(2,1)}), bf16[8,192,128]{2,1,0:T(8,128)(2,1)S(1)}, u32[]{:S(2)}, u32[]{:S(2)}) async-start(bf16[8,192,128]{2,1,0:T(8,128)(2,1)} %copy-done.77), calls=%async_computation.6 | async-start | bytes 786432 | tf_op jit(solution)/shard_map/all_to_all | solution.py:1751
  403.7 11.6 %shard_map.282 = (f32[192,1024]{1,0:T(8,128)S(1)}, f32[192,1024]{1,0:T(8,128)}, bf16[192,1024]{1,0:T(8,128)(2,1)S(1)}, f32[8,8,1024]{2,1,0:T(8,128)S(1)}, f32[256,128]{1,0:T(8,128)S(1)}) custom-call(bf16[192,1024]{1,0:T(8,128)(2,1)S(1)} %get-tuple-element.299.refs_0_, bf16[192,1024]{1,0:T(8,128)(2,1)S(1)} %get-tuple-element.233.refs_2_.refs_3_.refs_1_, ...), custom_call_target="tpu_custom_call" | custom-call | tf_op jit(solution)/shard_map/pallas_call | solution.py:600
  452.8 13.4 %shard_map.285 = (bf16[1024,1536]{1,0:T(8,128)(2,1)}, bf16[2,384,640]{2,1,0:T(8,128)(2,1)}, bf16[2,384,640]{2,1,0:T(8,128)(2,1)}, f32[8,8,1536]{2,1,0:T(8,128)}) custom-call(s32[6]{0:T(128)S(1)} %copy-done.126, bf16[1024,1536]{1,0:T(8,128)(2,1)} %bitcast.53, bf16[384,640]{1,0:T(8,128)(2,1)S(1)} %bitcast.42, bf16[384,640]{1,0:T(8,128)(2,1)S(1)} %copy-done.13, ...), custom_call_target="tpu_custom_call" | custom-call | tf_op jit(solution)/shard_map/pallas_call | solution.py:600
  473.6 7.8 %collective-permute-done.59.refs_1_ = bf16[512,384]{1,0:T(8,128)(2,1)S(1)} collective-permute-done((bf16[512,384]{1,0:T(8,128)(2,1)S(1)}, bf16[512,384]{1,0:T(8,128)(2,1)S(1)}, u32[]{:S(2)}, u32[]{:S(2)}) %collective-permute-start.59) | collective-permute-done | bytes 393248 | tf_op jit(solution)/shard_map/ppermute | solution.py:528
  489.8 5.6 collective-permute-start.63
  501.3 6.9 %all-to-all-done.8.refs_0_ = f32[8,8,1536]{2,1,0:T(8,128)} async-done(((f32[8,8,1536]{2,1,0:T(8,128)}), f32[8,8,1536]{2,1,0:T(8,128)}, u32[]{:S(2)}, u32[]{:S(2)}) %all-to-all-start.8) | async-done | bytes 393248 | tf_op jit(solution)/shard_map/all_to_all | solution.py:546
  526.0 5.6 shard_map.293
  531.6 5.8 %all-to-all-start.10 = ((f32[32,24,128]{2,1,0:T(8,128)}), f32[32,24,128]{2,1,0:T(8,128)S(1)}, u32[]{:S(2)}, u32[]{:S(2)}) async-start(f32[32,24,128]{2,1,0:T(8,128)} %get-tuple-element.365.refs_1_), calls=%async_computation.13 | async-start | bytes 786432 | tf_op jit(solution)/shard_map/all_to_all | solution.py:1927
  545.3 12.0 %all-to-all-done.10.refs_0_ = f32[32,24,128]{2,1,0:T(8,128)S(1)} async-done(((f32[32,24,128]{2,1,0:T(8,128)}), f32[32,24,128]{2,1,0:T(8,128)S(1)}, u32[]{:S(2)}, u32[]{:S(2)}) %all-to-all-start.10) | async-done | bytes 393248 | tf_op jit(solution)/shard_map/all_to_all | solution.py:1927
  (513 shorter events, 275.5 us)
Async XLA Ops:
  7.2 96.0 %all-gather.9.cloned.1.call-start = ((), (), s32[]{:S(2)}) async-start(), calls=%async_computation.19 | async-start | bytes 3538944 | tf_op jit(solution)/shard_map/all_gather | solution.py:1485
  16.0 31.3 %all-to-all-start = ((bf16[8,48,640]{2,1,0:T(8,128)(2,1)}), bf16[8,48,640]{2,1,0:T(8,128)(2,1)S(1)}, u32[]{:S(2)}, u32[]{:S(2)}) async-start(bf16[8,48,640]{2,1,0:T(8,128)(2,1)} %get-tuple-element.194), calls=%async_computation | async-start | bytes 983040 | tf_op jit(solution)/shard_map/all_to_all | solution.py:1517
  48.1 33.9 %collective-permute-start.7 = (bf16[384,640]{1,0:T(8,128)(2,1)S(1)}, bf16[384,640]{1,0:T(8,128)(2,1)S(1)}, u32[]{:S(2)}, u32[]{:S(2)}) collective-permute-start(bf16[384,640]{1,0:T(8,128)(2,1)S(1)} %bitcast.39), channel_id=1, source_target_pairs={{0,8},{8,0},{1,9},{9,1},{2,10},{10,2},{3,11},{11,3},{4,12},{12,4},... | collective-permute-start | bytes 1474568 | tf_op jit(solution)/shard_map/ppermute | solution.py:528
  48.1 34.7 %collective-permute-start.8 = (bf16[384,640]{1,0:T(8,128)(2,1)S(1)}, bf16[384,640]{1,0:T(8,128)(2,1)S(1)}, u32[]{:S(2)}, u32[]{:S(2)}) collective-permute-start(bf16[384,640]{1,0:T(8,128)(2,1)S(1)} %bitcast.40), channel_id=1, source_target_pairs={{0,16},{16,0},{1,17},{17,1},{2,18},{18,2},{3,19},{19,3},{4,20},{20... | collective-permute-start | bytes 1474568 | tf_op jit(solution)/shard_map/ppermute | solution.py:528
  49.3 32.0 %all-to-all-start.1 = ((bf16[32,16,128]{2,1,0:T(8,128)(2,1)}), bf16[32,16,128]{2,1,0:T(8,128)(2,1)S(1)}, u32[]{:S(2)}, u32[]{:S(2)}) async-start(bf16[32,16,128]{2,1,0:T(8,128)(2,1)} %copy-done.114), calls=%async_computation.1 | async-start | bytes 262144 | tf_op jit(solution)/shard_map/all_to_all | solution.py:1524
  52.4 94.6 %all-gather.5.cloned.1.call-start = ((), (), s32[]{:S(2)}) async-start(), calls=%async_computation.14 | async-start | bytes 1966080 | tf_op jit(solution)/shard_map/all_gather | solution.py:1557
  97.1 23.3 %collective-permute-start.17 = (bf16[2,4,128,384]{3,2,1,0:T(8,128)(2,1)}, bf16[2,4,128,384]{3,2,1,0:T(8,128)(2,1)}, u32[]{:S(2)}, u32[]{:S(2)}) collective-permute-start(bf16[2,4,128,384]{3,2,1,0:T(8,128)(2,1)} %get-tuple-element.218), channel_id=1, source_target_pairs={{0,16},{16,0},{1,17},{17,1},{2,18},{18,2},{3,19},{19,3},{4,20},{20... | collective-permute-start | bytes 2359304 | tf_op jit(solution)/shard_map/ppermute | solution.py:528
  98.3 48.7 %all-to-all-start.2 = ((bf16[8,48,1024]{2,1,0:T(8,128)(2,1)}), bf16[8,48,1024]{2,1,0:T(8,128)(2,1)}, u32[]{:S(2)}, u32[]{:S(2)}) async-start(bf16[8,48,1024]{2,1,0:T(8,128)(2,1)} %copy-done.53), calls=%async_computation.2 | async-start | bytes 1572864 | tf_op jit(solution)/shard_map/all_to_all | solution.py:1558
  103.0 135.5 %all-gather.7.cloned.1.call-start = ((), (), s32[]{:S(2)}) async-start(), calls=%async_computation.15 | async-start | bytes 3932160 | tf_op jit(solution)/shard_map/all_gather | solution.py:1618
  121.7 22.7 %collective-permute-start.18 = (bf16[4,128,384]{2,1,0:T(8,128)(2,1)S(1)}, bf16[4,128,384]{2,1,0:T(8,128)(2,1)S(1)}, u32[]{:S(2)}, u32[]{:S(2)}) collective-permute-start(bf16[4,128,384]{2,1,0:T(8,128)(2,1)S(1)} %get-tuple-element.220), channel_id=1, source_target_pairs={{0,1},{1,0},{2,3},{3,2},{4,5},{5,4},{6,7},{7,6},{8,9},{9,8},{10,11... | collective-permute-start | bytes 1179656 | tf_op jit(solution)/shard_map/ppermute | solution.py:528
  123.6 23.4 %collective-permute-start.13 = (bf16[96,1536]{1,0:T(8,128)(2,1)S(1)}, bf16[96,1536]{1,0:T(8,128)(2,1)S(1)}, u32[]{:S(2)}, u32[]{:S(2)}) collective-permute-start(bf16[96,1536]{1,0:T(8,128)(2,1)S(1)} %shard_map.261.refs_2_.refs_0_), channel_id=1, source_target_pairs={{0,4},{2,6},{4,0},{6,2},{1,5},{3,7},{5,1},{7,3},{8,12},{10,14},{12... | collective-permute-start | bytes 884744 | tf_op jit(solution)/shard_map/ppermute | solution.py:537
  127.9 16.5 %collective-permute-start.15 = (f32[8,1024]{1,0:T(8,128)S(1)}, f32[8,1024]{1,0:T(8,128)S(1)}, u32[]{:S(2)}, u32[]{:S(2)}) collective-permute-start(f32[8,1024]{1,0:T(8,128)S(1)} %add.120.refs_2_.refs_1_), channel_id=1, source_target_pairs={{4,0},{6,2},{0,4},{2,6},{5,1},{7,3},{1,5},{3,7},{12,8},{14,10},{8,... | collective-permute-start | bytes 98312 | tf_op jit(solution)/shard_map/ppermute | solution.py:533
  147.1 17.5 %collective-permute-start.19 = (bf16[192,1536]{1,0:T(8,128)(2,1)S(1)}, bf16[192,1536]{1,0:T(8,128)(2,1)S(1)}, u32[]{:S(2)}, u32[]{:S(2)}) collective-permute-start(bf16[192,1536]{1,0:T(8,128)(2,1)S(1)} %shard_map.264.refs_8_.refs_0_), channel_id=1, source_target_pairs={{0,1},{1,0},{2,3},{3,2},{4,5},{5,4},{6,7},{7,6},{8,9},{9,8},{10,11... | collective-permute-start | bytes 1769480 | tf_op jit(solution)/shard_map/ppermute | solution.py:528
  167.4 26.1 %collective-permute-start.27 = (bf16[384,1536]{1,0:T(8,128)(2,1)S(1)}, bf16[384,1536]{1,0:T(8,128)(2,1)}, u32[]{:S(2)}, u32[]{:S(2)}) collective-permute-start(bf16[384,1536]{1,0:T(8,128)(2,1)S(1)} %shard_map.266.refs_4_.refs_1_), channel_id=1, source_target_pairs={{0,16},{16,0},{1,17},{17,1},{2,18},{18,2},{3,19},{19,3},{4,20},{20... | collective-permute-start | bytes 3538952 | tf_op jit(solution)/shard_map/ppermute | solution.py:528
  195.9 26.3 %all-to-all-start.3 = ((bf16[8,192,128]{2,1,0:T(8,128)(2,1)}), bf16[8,192,128]{2,1,0:T(8,128)(2,1)S(1)}, u32[]{:S(2)}, u32[]{:S(2)}) async-start(bf16[8,192,128]{2,1,0:T(8,128)(2,1)} %get-tuple-element.251), calls=%async_computation.3 | async-start | bytes 786432 | tf_op jit(solution)/shard_map/all_to_all | solution.py:1647
  199.8 163.1 %reduce-scatter.4.cloned.1.call-start = ((), (), s32[]{:S(2)}) async-start(), calls=%async_computation.16 | async-start | bytes 1966080 | tf_op jit(solution)/shard_map/reduce_scatter | solution.py:1729
  325.0 19.9 %collective-permute-start.47 = (bf16[4,384,1024]{2,1,0:T(8,128)(2,1)}, bf16[4,384,1024]{2,1,0:T(8,128)(2,1)}, u32[]{:S(2)}, u32[]{:S(2)}) collective-permute-start(bf16[4,384,1024]{2,1,0:T(8,128)(2,1)} %get-tuple-element.289), channel_id=1, source_target_pairs={{0,8},{8,0},{1,9},{9,1},{2,10},{10,2},{3,11},{11,3},{4,12},{12,4},... | collective-permute-start | bytes 9437192 | tf_op jit(solution)/shard_map/ppermute | solution.py:528
  329.1 111.8 %reduce-scatter.6.cloned.1.call-start = ((), (), s32[]{:S(2)}) async-start(), calls=%async_computation.17 | async-start | bytes 3932160 | tf_op jit(solution)/shard_map/reduce_scatter | solution.py:1745
  362.9 17.2 %all-to-all-start.4 = ((bf16[8,192,128]{2,1,0:T(8,128)(2,1)}), bf16[8,192,128]{2,1,0:T(8,128)(2,1)S(1)}, u32[]{:S(2)}, u32[]{:S(2)}) async-start(bf16[8,192,128]{2,1,0:T(8,128)(2,1)} %bitcast.25), calls=%async_computation.5 | async-start | bytes 786432 | tf_op jit(solution)/shard_map/all_to_all | solution.py:1746
  380.1 37.5 %collective-permute-start.50 = (bf16[128,1536]{1,0:T(8,128)(2,1)}, bf16[128,1536]{1,0:T(8,128)(2,1)}, u32[]{:S(2)}, u32[]{:S(2)}) collective-permute-start(bf16[128,1536]{1,0:T(8,128)(2,1)} %collective-permute-done.49.refs_4_), channel_id=1, source_target_pairs={{0,1},{1,0},{2,3},{3,2},{4,5},{5,4},{6,7},{7,6},{8,9},{9,8},{10,11... | collective-permute-start | bytes 1179656 | tf_op jit(solution)/shard_map/ppermute | solution.py:528
  381.4 36.2 %all-to-all-start.5 = ((bf16[8,192,128]{2,1,0:T(8,128)(2,1)}), bf16[8,192,128]{2,1,0:T(8,128)(2,1)S(1)}, u32[]{:S(2)}, u32[]{:S(2)}) async-start(bf16[8,192,128]{2,1,0:T(8,128)(2,1)} %copy-done.77), calls=%async_computation.6 | async-start | bytes 786432 | tf_op jit(solution)/shard_map/all_to_all | solution.py:1751
  417.6 17.4 %all-to-all-start.6 = ((f32[8,8,1024]{2,1,0:T(8,128)}), f32[8,8,1024]{2,1,0:T(8,128)S(1)}, u32[]{:S(2)}, u32[]{:S(2)}) async-start(f32[8,8,1024]{2,1,0:T(8,128)} %copy-done.84), calls=%async_computation.7 | async-start | bytes 524288 | tf_op jit(solution)/shard_map/all_to_all | solution.py:546
  440.9 28.3 %all-to-all-start.7 = ((bf16[8,48,1024]{2,1,0:T(8,128)(2,1)}), bf16[8,48,1024]{2,1,0:T(8,128)(2,1)S(1)}, u32[]{:S(2)}, u32[]{:S(2)}) async-start(bf16[8,48,1024]{2,1,0:T(8,128)(2,1)} %bitcast.57), calls=%async_computation.9 | async-start | bytes 1572864 | tf_op jit(solution)/shard_map/all_to_all | solution.py:1838
  444.9 118.2 %reduce-scatter.8.cloned.1.call-start = ((), (), s32[]{:S(2)}) async-start(), calls=%async_computation.18 | async-start | bytes 3538944 | tf_op jit(solution)/shard_map/reduce_scatter | solution.py:1875
  444.9 21.3 %collective-permute-start.55 = (bf16[80,1536]{1,0:T(8,128)(2,1)}, bf16[80,1536]{1,0:T(8,128)(2,1)S(1)}, u32[]{:S(2)}, u32[]{:S(2)}) collective-permute-start(bf16[80,1536]{1,0:T(8,128)(2,1)} %copy-done.141), channel_id=1, source_target_pairs={{2,0},{4,2},{6,4},{0,6},{3,1},{5,3},{7,5},{1,7},{10,8},{12,10},{14... | collective-permute-start | bytes 737288 | tf_op jit(solution)/shard_map/ppermute | solution.py:533
  446.1 21.7 %collective-permute-start.56 = (bf16[80,1536]{1,0:T(8,128)(2,1)}, bf16[80,1536]{1,0:T(8,128)(2,1)S(1)}, u32[]{:S(2)}, u32[]{:S(2)}) collective-permute-start(bf16[80,1536]{1,0:T(8,128)(2,1)} %copy-done.140), channel_id=1, source_target_pairs={{4,0},{6,2},{0,4},{2,6},{5,1},{7,3},{1,5},{3,7},{12,8},{14,10},{8,... | collective-permute-start | bytes 737288 | tf_op jit(solution)/shard_map/ppermute | solution.py:533
  446.1 22.4 %collective-permute-start.57 = (bf16[80,1536]{1,0:T(8,128)(2,1)}, bf16[80,1536]{1,0:T(8,128)(2,1)S(1)}, u32[]{:S(2)}, u32[]{:S(2)}) collective-permute-start(bf16[80,1536]{1,0:T(8,128)(2,1)} %copy-done.139), channel_id=1, source_target_pairs={{6,0},{0,2},{2,4},{4,6},{7,1},{1,3},{3,5},{5,7},{14,8},{8,10},{10,... | collective-permute-start | bytes 737288 | tf_op jit(solution)/shard_map/ppermute | solution.py:533
  482.6 25.6 %all-to-all-start.8 = ((f32[8,8,1536]{2,1,0:T(8,128)}), f32[8,8,1536]{2,1,0:T(8,128)}, u32[]{:S(2)}, u32[]{:S(2)}) async-start(f32[8,8,1536]{2,1,0:T(8,128)} %get-tuple-element.355.refs_4_), calls=%async_computation.11 | async-start | bytes 786432 | tf_op jit(solution)/shard_map/all_to_all | solution.py:546
  489.8 27.4 %collective-permute-start.63 = (bf16[1024,384]{1,0:T(8,128)(2,1)S(1)}, bf16[1024,384]{1,0:T(8,128)(2,1)}, u32[]{:S(2)}, u32[]{:S(2)}) collective-permute-start(bf16[1024,384]{1,0:T(8,128)(2,1)S(1)} %shard_map.288.refs_1_.refs_2_), channel_id=1, source_target_pairs={{0,8},{8,0},{1,9},{9,1},{2,10},{10,2},{3,11},{11,3},{4,12},{12,4},... | collective-permute-start | bytes 2359304 | tf_op jit(solution)/shard_map/ppermute | solution.py:528
  495.3 21.9 %collective-permute-start.64 = (bf16[1024,384]{1,0:T(8,128)(2,1)S(1)}, bf16[1024,384]{1,0:T(8,128)(2,1)}, u32[]{:S(2)}, u32[]{:S(2)}) collective-permute-start(bf16[1024,384]{1,0:T(8,128)(2,1)S(1)} %shard_map.288.refs_1_.refs_2_), channel_id=1, source_target_pairs={{0,16},{16,0},{1,17},{17,1},{2,18},{18,2},{3,19},{19,3},{4,20},{20... | collective-permute-start | bytes 2359304 | tf_op jit(solution)/shard_map/ppermute | solution.py:528
  513.3 18.3 %all-to-all-start.9 = ((bf16[8,48,640]{2,1,0:T(8,128)(2,1)}), bf16[8,48,640]{2,1,0:T(8,128)(2,1)S(1)}, u32[]{:S(2)}, u32[]{:S(2)}) async-start(bf16[8,48,640]{2,1,0:T(8,128)(2,1)} %bitcast.28), calls=%async_computation.12 | async-start | bytes 983040 | tf_op jit(solution)/shard_map/all_to_all | solution.py:1894
  531.6 25.8 %all-to-all-start.10 = ((f32[32,24,128]{2,1,0:T(8,128)}), f32[32,24,128]{2,1,0:T(8,128)S(1)}, u32[]{:S(2)}, u32[]{:S(2)}) async-start(f32[32,24,128]{2,1,0:T(8,128)} %get-tuple-element.365.refs_1_), calls=%async_computation.13 | async-start | bytes 786432 | tf_op jit(solution)/shard_map/all_to_all | solution.py:1927
  (203 other events, 1584.1 us)
Sparse Core Ops, SparseCore 0:
  10.2 80.4 all-gather.8
  92.2 39.1 all-gather.4
  165.5 72.9 all-gather.6
  329.2 33.5 reduce-scatter.3
  365.0 64.8 reduce-scatter.5
  469.3 93.7 reduce-scatter.7

commit v5 on v4

--- a/solution.py
+++ b/solution.py
@@ -948,7 +948,8 @@
     rows, width = own.shape
     by_x, by_y = flip(to_x, "x"), flip(to_y, "y")
     if between is not None:
-        between()
+        by_x, by_y, *grads = together(by_x, by_y, *between())
+        between.grads = grads
     own, to_y, to_x = line(
         scatter_two_body,
         [((rows, width), f32), ((rows // 2, width), bf16), ((rows // 2, width), bf16)],
@@ -1708,28 +1709,24 @@
         *downs,
         gate_up,
     )
-    ffn_grads = []
 
     def feed_weights():
-        down_own, down_other = line(
+        return line(
             down_weight_body, [((hidden, width), bf16)] * 2, activated, grad_down_all
-        )
-        gateup_own, gateup_other = line(
+        ) + line(
             gateup_weight_body,
             [((4, 4 * block, 2 * hidden), bf16)] * 2,
             normed_ffn_all,
             grad_gate_up,
         )
-        (down_sum,) = line(
-            add_body, [((hidden, width), bf16)], down_own, flip(down_other, "core")
-        )
-        ffn_grads.extend([down_sum, gateup_own, flip(gateup_other, "core")])
 
     ffn_parts = scatter_chips(line, *parts, feed_weights)
-    wgrad_down = lax.psum_scatter(ffn_grads[0], "z", scatter_dimension=0, tiled=True)
-    (wgrad_gateup,) = line(
-        add_body, [((4, 4 * block, 2 * hidden), bf16)], ffn_grads[1], ffn_grads[2]
-    )
+    down_own, down_other, gateup_own, gateup_other = feed_weights.grads
+    (wgrad_down,) = line(
+        add_body, [((hidden, width), bf16)], down_own, flip(down_other, "core")
+    )
+    wgrad_down = lax.psum_scatter(wgrad_down, "z", scatter_dimension=0, tiled=True)
+    gateup_got = flip(gateup_other, "core")
 
     grad_residual, grad_attn, grad_mixed, residual_sums = line(
         residual_back_body,
@@ -1741,13 +1738,15 @@
         vector,
         full_out,
     )
-    grad_mixed, wgrad_down, wgrad_gateup = together(grad_mixed, wgrad_down, wgrad_gateup)
-    wgrad_gateup = lax.psum_scatter(wgrad_gateup, "z", scatter_dimension=0, tiled=False)
     grad_pieces = lax.all_to_all(grad_mixed.reshape(8, cols, rows), seq_axes, 0, 0, tiled=True)
     grad_by_x, grad_by_y = flip(grad_attn, "x"), flip(grad_attn, "y")
-    grad_pieces, grad_by_x, grad_by_y, mixed_plane = together(
-        grad_pieces, grad_by_x, grad_by_y, mixed_plane
-    )
+    (wgrad_gateup,) = line(
+        add_body, [((4, 4 * block, 2 * hidden), bf16)], gateup_own, gateup_got
+    )
+    grad_pieces, grad_by_x, grad_by_y, mixed_plane, wgrad_down, wgrad_gateup = together(
+        grad_pieces, grad_by_x, grad_by_y, mixed_plane, wgrad_down, wgrad_gateup
+    )
+    wgrad_gateup = lax.psum_scatter(wgrad_gateup, "z", scatter_dimension=0, tiled=False)
     mixed_plane = lax.all_to_all(mixed_plane, plane_axes, 0, 0, tiled=True)
     grad_far = flip(grad_by_y, "x")
 

time: 584 us -> 589 us (level)
  waiting for transfers between devices: 202 us -> 218 us
  local copies, waits for them, and re-layouts: 79.5 us -> 73.1 us
    reduce_scatter x1, waiting for transfers between devices: 0.01 us -> 15.6 us  [local_fast(): lax.psum_scatter(wgrad_gateup, 'z', scatter_dimension=0, tiled=False)]
    all_to_all x1, waiting for transfers between devices: 0.01 us -> 8.64 us  [local_fast(): lax.all_to_all(grad_mixed.reshape(8, cols, rows), seq_axes, 0, 0, tiled=T...]
    all_to_all x1, starting transfers between devices: 12.9 us -> 4.54 us  [local_fast(): mixed_plane = lax.all_to_all(mixed_plane, plane_axes, 0, 0, tiled=True)]
    ppermute x50, waiting for transfers between devices: 107 us -> 99.7 us  [flip(): return lax.ppermute(value, axis, [(0, 1), (1, 0)])]
    unnamed x302 -> x288, local copies, waits for them, and re-layouts: 73.5 us -> 67.1 us
  transfers between devices with their start and end apart: 84 -> 84, of which waited for: 43 -> 43; matrix products, arithmetic and copies ran while one was open for 2% -> 2% of each run, Pallas kernels for 19% -> 20%
where the time goes in v5:
time: 589 us; the launch traced here: 577 us
  waiting for transfers between devices  218 us (37%)
  Pallas kernels  140 us (24%)
  starting transfers between devices  121 us (21%)
  local copies, waits for them, and re-layouts  73.1 us (12%)
  between operations  18.8 us (3%)
  other arithmetic  6.04 us (1%)
    pallas_call x43, Pallas kernels, __call__(): pl.pallas_call(run, out_shape=[jax.ShapeDtypeStruct(shape, kind) for shap...  140 us
    ppermute x50, waiting for transfers between devices, flip(): return lax.ppermute(value, axis, [(0, 1), (1, 0)])  99.7 us
    unnamed x288, local copies, waits for them, and re-layouts  67.1 us
    ppermute x50, starting transfers between devices, flip(): return lax.ppermute(value, axis, [(0, 1), (1, 0)])  55.3 us
    ppermute x15, waiting for transfers between devices, from_ahead(): lax.ppermute(value, axis, [((i + step) % count, i) for i in range(count)])  33.5 us
    all_to_all x1, waiting for transfers between devices, local_fast(): lax.all_to_all(mixed_pieces, seq_axes, 0, 0, tiled=True)  16.4 us
    reduce_scatter x1, waiting for transfers between devices, local_fast(): lax.psum_scatter(wgrad_gateup, 'z', scatter_dimension=0, tiled=False)  15.6 us
    ppermute x15, starting transfers between devices, from_ahead(): lax.ppermute(value, axis, [((i + step) % count, i) for i in range(count)])  15.2 us
  transfers between devices with their start and end apart: 84, of which 43 were waited for; matrix products, arithmetic and copies ran while one was open for 2% of the time, Pallas kernels for 20%

profile of v5, /device:TPU:1, one launch (start us, length us, event | category | flops | bytes accessed | tf_op | source)
XLA Modules:
  0.0 577.1 jit_solution(14257079582618387589)
XLA Ops:
  16.0 6.4 %all-to-all-start = ((bf16[8,48,640]{2,1,0:T(8,128)(2,1)}), bf16[8,48,640]{2,1,0:T(8,128)(2,1)S(1)}, u32[]{:S(2)}, u32[]{:S(2)}) async-start(bf16[8,48,640]{2,1,0:T(8,128)(2,1)} %get-tuple-element.199), calls=%async_computation | async-start | bytes 983040 | tf_op jit(solution)/shard_map/all_to_all | solution.py:1518
  25.0 7.8 %collective-permute-done.refs_4_.refs_7_ = bf16[32,6528]{1,0:T(8,128)(2,1)S(1)} collective-permute-done((bf16[32,6528]{1,0:T(8,128)(2,1)S(1)}, bf16[32,6528]{1,0:T(8,128)(2,1)S(1)}, u32[]{:S(2)}, u32[]{:S(2)}) %collective-permute-start) | collective-permute-done | bytes 417824 | tf_op jit(solution)/shard_map/ppermute | solution.py:528
  33.6 13.8 %all-to-all-done = bf16[8,48,640]{2,1,0:T(8,128)(2,1)S(1)} async-done(((bf16[8,48,640]{2,1,0:T(8,128)(2,1)}), bf16[8,48,640]{2,1,0:T(8,128)(2,1)S(1)}, u32[]{:S(2)}, u32[]{:S(2)}) %all-to-all-start) | async-done | bytes 491552 | tf_op jit(solution)/shard_map/all_to_all | solution.py:1518
  56.5 5.3 collective-permute-done.3
  69.3 11.1 %collective-permute-done.5.refs_3_ = f32[32,640]{1,0:T(8,128)S(1)} collective-permute-done((f32[32,640]{1,0:T(8,128)S(1)}, f32[32,640]{1,0:T(8,128)S(1)}, u32[]{:S(2)}, u32[]{:S(2)}) %collective-permute-start.5) | collective-permute-done | bytes 81952 | tf_op jit(solution)/shard_map/ppermute | solution.py:533
  103.2 8.8 %shard_map.260 = (bf16[1024,1536]{1,0:T(8,128)(2,1)}, f32[640,1024]{1,0:T(8,128)}, f32[8,1024]{1,0:T(8,128)S(1)}) custom-call(s32[6]{0:T(128)S(1)} %stack.27.refs_0_, bf16[1024,1536]{1,0:T(8,128)(2,1)} %bitcast.52, bf16[384,640]{1,0:T(8,128)(2,1)S(1)} %bitcast.41, bf16[384,640]{1,0:T(8,128)(2,1)S(1)} %copy-done.10, bf16[384,640]{1,0:T(8,128)(2,1)S(1)} %copy-done.13, ...), custom_call_target="tpu_custom_call" | custom-call | tf_op jit(solution)/shard_map/pallas_call | solution.py:600
  134.3 10.0 %collective-permute-done.15.refs_3_ = f32[8,1024]{1,0:T(8,128)S(1)} collective-permute-done((f32[8,1024]{1,0:T(8,128)S(1)}, f32[8,1024]{1,0:T(8,128)S(1)}, u32[]{:S(2)}, u32[]{:S(2)}) %collective-permute-start.15) | collective-permute-done | bytes 32800 | tf_op jit(solution)/shard_map/ppermute | solution.py:533
  151.1 7.9 %shard_map.265 = (bf16[192,1024]{1,0:T(8,128)(2,1)S(1)}, bf16[192,1024]{1,0:T(8,128)(2,1)S(1)}, bf16[192,1024]{1,0:T(8,128)(2,1)S(1)}, f32[192,1024]{1,0:T(8,128...) custom-call(f32[640,1024]{1,0:T(8,128)} %get-tuple-element.219.refs_0_.refs_8_.refs_9_, f32[8,1024]{1,0:T(8,128)S(1)} %copy-done.80, ...), custom_call_target="tpu_custom_call" | custom-call | tf_op jit(solution)/shard_map/pallas_call | solution.py:600
  187.2 6.2 %collective-permute-done.27.refs_3_ = bf16[384,1536]{1,0:T(8,128)(2,1)} collective-permute-done((bf16[384,1536]{1,0:T(8,128)(2,1)S(1)}, bf16[384,1536]{1,0:T(8,128)(2,1)}, u32[]{:S(2)}, u32[]{:S(2)}) %collective-permute-start.27) | collective-permute-done | bytes 1179680 | tf_op jit(solution)/shard_map/ppermute | solution.py:528
  205.8 16.4 %all-to-all-done.3 = bf16[8,192,128]{2,1,0:T(8,128)(2,1)S(1)} async-done(((bf16[8,192,128]{2,1,0:T(8,128)(2,1)}), bf16[8,192,128]{2,1,0:T(8,128)(2,1)S(1)}, u32[]{:S(2)}, u32[]{:S(2)}) %all-to-all-start.3) | async-done | bytes 393248 | tf_op jit(solution)/shard_map/all_to_all | solution.py:1648
  229.8 6.4 %collective-permute-done.30.refs_1_ = bf16[128,1536]{1,0:T(8,128)(2,1)S(1)} collective-permute-done((bf16[128,1536]{1,0:T(8,128)(2,1)S(1)}, bf16[128,1536]{1,0:T(8,128)(2,1)S(1)}, u32[]{:S(2)}, u32[]{:S(2)}) %collective-permute-start.30) | collective-permute-done | bytes 393248 | tf_op jit(solution)/shard_map/ppermute | solution.py:528
  240.5 10.2 %collective-permute-done.32.refs_3_ = bf16[128,1536]{1,0:T(8,128)(2,1)S(1)} collective-permute-done((bf16[128,1536]{1,0:T(8,128)(2,1)}, bf16[128,1536]{1,0:T(8,128)(2,1)S(1)}, u32[]{:S(2)}, u32[]{:S(2)}) %collective-permute-start.32) | collective-permute-done | bytes 393248 | tf_op jit(solution)/shard_map/ppermute | solution.py:528
  252.9 10.6 %shard_map.271 = (bf16[512,1536]{1,0:T(8,128)(2,1)}, f32[2,512,1024]{2,1,0:T(8,128)}, bf16[2,512,512]{2,1,0:T(8,128)(2,1)}, f32[128,1536]{1,0:T(8,128)S(1)}, f32...) custom-call(bf16[128,1536]{1,0:T(8,128)(2,1)S(1)} %get-tuple-element.262.refs_0_, ...), custom_call_target="tpu_custom_call" | custom-call | tf_op jit(solution)/shard_map/pallas_call | solution.py:600
  264.9 7.8 %collective-permute-done.35.refs_2_ = bf16[128,1536]{1,0:T(8,128)(2,1)S(1)} collective-permute-done((bf16[128,1536]{1,0:T(8,128)(2,1)S(1)}, bf16[128,1536]{1,0:T(8,128)(2,1)S(1)}, u32[]{:S(2)}, u32[]{:S(2)}) %collective-permute-start.35) | collective-permute-done | bytes 393248 | tf_op jit(solution)/shard_map/ppermute | solution.py:528
  281.6 5.8 %collective-permute-done.40.refs_2_ = bf16[128,1536]{1,0:T(8,128)(2,1)S(1)} collective-permute-done((bf16[128,1536]{1,0:T(8,128)(2,1)S(1)}, bf16[128,1536]{1,0:T(8,128)(2,1)S(1)}, u32[]{:S(2)}, u32[]{:S(2)}) %collective-permute-start.40) | collective-permute-done | bytes 393248 | tf_op jit(solution)/shard_map/ppermute | solution.py:528
  288.3 8.9 %collective-permute-done.41.refs_3_ = bf16[128,1536]{1,0:T(8,128)(2,1)S(1)} collective-permute-done((bf16[128,1536]{1,0:T(8,128)(2,1)S(1)}, bf16[128,1536]{1,0:T(8,128)(2,1)S(1)}, u32[]{:S(2)}, u32[]{:S(2)}) %collective-permute-start.41) | collective-permute-done | bytes 393248 | tf_op jit(solution)/shard_map/ppermute | solution.py:528
  297.2 10.6 %shard_map.274 = (bf16[512,1536]{1,0:T(8,128)(2,1)}, bf16[2,512,1024]{2,1,0:T(8,128)(2,1)}, f32[128,1536]{1,0:T(8,128)S(1)}, f32[128,1536]{1,0:T(8,128)S(1)}, bf...) custom-call(bf16[128,1536]{1,0:T(8,128)(2,1)S(1)} %get-tuple-element.277.refs_0_, ...), custom_call_target="tpu_custom_call" | custom-call | tf_op jit(solution)/shard_map/pallas_call | solution.py:600
  314.7 7.4 %shard_map.276 = (bf16[4,384,1024]{2,1,0:T(8,128)(2,1)}, bf16[4,384,1024]{2,1,0:T(8,128)(2,1)}) custom-call(bf16[512,1536]{1,0:T(8,128)(2,1)S(1)} %copy-done.28, bf16[2,512,1024]{2,1,0:T(8,128)(2,1)} %get-tuple-element.289.refs_1_, bf16[512,1536]{1,0:T(8,128)(2,1)S(1)} %get-tuple-element.297.refs_2_.refs_0_), custom_call_target="tpu_custom_call" | custom-call | tf_op jit(solution)/shard_map/pallas_call | solution.py:600
  337.3 5.8 collective-permute-done.44.refs_1_
  344.2 5.6 shard_map.279
  358.1 5.2 shard_map.280.refs_10_
  367.1 8.6 %all-to-all-done.4.refs_2_ = bf16[8,192,128]{2,1,0:T(8,128)(2,1)S(1)} async-done(((bf16[8,192,128]{2,1,0:T(8,128)(2,1)}), bf16[8,192,128]{2,1,0:T(8,128)(2,1)S(1)}, u32[]{:S(2)}, u32[]{:S(2)}) %all-to-all-start.4) | async-done | bytes 393248 | tf_op jit(solution)/shard_map/all_to_all | solution.py:1741
  389.1 11.9 %shard_map.282 = (f32[192,1024]{1,0:T(8,128)S(1)}, f32[192,1024]{1,0:T(8,128)}, bf16[192,1024]{1,0:T(8,128)(2,1)S(1)}, f32[8,8,1024]{2,1,0:T(8,128)}, f32[256,128]{1,0:T(8,128)S(1)}) custom-call(bf16[192,1024]{1,0:T(8,128)(2,1)S(1)} %get-tuple-element.309.refs_0_, bf16[192,1024]{1,0:T(8,128)(2,1)S(1)} %get-tuple-element.238.refs_2_.refs_3_.refs_1_, ...), custom_call_target="tpu_custom_call" | custom-call | tf_op jit(solution)/shard_map/pallas_call | solution.py:600
  425.6 15.6 %reduce-scatter.6.cloned.1.call-done = bf16[1,384,1024]{2,1,0:T(8,128)(2,1)} async-done(((bf16[4,384,1024]{2,1,0:T(8,128)(2,1)}), bf16[1,384,1024]{2,1,0:T(8,128)(2,1)}) %reduce-scatter.6.cloned.1.call-update) | async-done | bytes 786448 | tf_op jit(solution)/shard_map/reduce_scatter | solution.py:1749
  455.6 13.4 %shard_map.285 = (bf16[1024,1536]{1,0:T(8,128)(2,1)}, bf16[2,384,640]{2,1,0:T(8,128)(2,1)}, bf16[2,384,640]{2,1,0:T(8,128)(2,1)}, f32[8,8,1536]{2,1,0:T(8,128)}) custom-call(s32[6]{0:T(128)S(1)} %copy-done.118, bf16[1024,1536]{1,0:T(8,128)(2,1)} %bitcast.53, bf16[384,640]{1,0:T(8,128)(2,1)S(1)} %bitcast.42, bf16[384,640]{1,0:T(8,128)(2,1)S(1)} %copy-done.11, ...), custom_call_target="tpu_custom_call" | custom-call | tf_op jit(solution)/shard_map/pallas_call | solution.py:600
  476.9 8.2 %collective-permute-done.59.refs_1_ = bf16[512,384]{1,0:T(8,128)(2,1)S(1)} collective-permute-done((bf16[512,384]{1,0:T(8,128)(2,1)S(1)}, bf16[512,384]{1,0:T(8,128)(2,1)S(1)}, u32[]{:S(2)}, u32[]{:S(2)}) %collective-permute-start.59) | collective-permute-done | bytes 393248 | tf_op jit(solution)/shard_map/ppermute | solution.py:528
  493.7 5.3 collective-permute-start.63
  504.6 7.2 %all-to-all-done.8.refs_0_ = f32[8,8,1536]{2,1,0:T(8,128)} async-done(((f32[8,8,1536]{2,1,0:T(8,128)}), f32[8,8,1536]{2,1,0:T(8,128)}, u32[]{:S(2)}, u32[]{:S(2)}) %all-to-all-start.8) | async-done | bytes 393248 | tf_op jit(solution)/shard_map/all_to_all | solution.py:546
  512.9 4.9 collective-permute-start.62
  530.3 5.6 shard_map.293
  535.9 5.8 %all-to-all-start.10 = ((f32[32,24,128]{2,1,0:T(8,128)}), f32[32,24,128]{2,1,0:T(8,128)S(1)}, u32[]{:S(2)}, u32[]{:S(2)}) async-start(f32[32,24,128]{2,1,0:T(8,128)} %get-tuple-element.375.refs_1_), calls=%async_computation.13 | async-start | bytes 786432 | tf_op jit(solution)/shard_map/all_to_all | solution.py:1926
  549.8 12.5 %all-to-all-done.10.refs_0_ = f32[32,24,128]{2,1,0:T(8,128)S(1)} async-done(((f32[32,24,128]{2,1,0:T(8,128)}), f32[32,24,128]{2,1,0:T(8,128)S(1)}, u32[]{:S(2)}, u32[]{:S(2)}) %all-to-all-start.10) | async-done | bytes 393248 | tf_op jit(solution)/shard_map/all_to_all | solution.py:1926
  (499 shorter events, 280.9 us)
Async XLA Ops:
  7.2 96.0 %all-gather.9.cloned.1.call-start = ((), (), s32[]{:S(2)}) async-start(), calls=%async_computation.19 | async-start | bytes 3538944 | tf_op jit(solution)/shard_map/all_gather | solution.py:1486
  16.0 31.3 %all-to-all-start = ((bf16[8,48,640]{2,1,0:T(8,128)(2,1)}), bf16[8,48,640]{2,1,0:T(8,128)(2,1)S(1)}, u32[]{:S(2)}, u32[]{:S(2)}) async-start(bf16[8,48,640]{2,1,0:T(8,128)(2,1)} %get-tuple-element.199), calls=%async_computation | async-start | bytes 983040 | tf_op jit(solution)/shard_map/all_to_all | solution.py:1518
  48.1 33.9 %collective-permute-start.7 = (bf16[384,640]{1,0:T(8,128)(2,1)S(1)}, bf16[384,640]{1,0:T(8,128)(2,1)S(1)}, u32[]{:S(2)}, u32[]{:S(2)}) collective-permute-start(bf16[384,640]{1,0:T(8,128)(2,1)S(1)} %bitcast.39), channel_id=1, source_target_pairs={{0,8},{8,0},{1,9},{9,1},{2,10},{10,2},{3,11},{11,3},{4,12},{12,4},... | collective-permute-start | bytes 1474568 | tf_op jit(solution)/shard_map/ppermute | solution.py:528
  48.1 34.7 %collective-permute-start.8 = (bf16[384,640]{1,0:T(8,128)(2,1)S(1)}, bf16[384,640]{1,0:T(8,128)(2,1)S(1)}, u32[]{:S(2)}, u32[]{:S(2)}) collective-permute-start(bf16[384,640]{1,0:T(8,128)(2,1)S(1)} %bitcast.40), channel_id=1, source_target_pairs={{0,16},{16,0},{1,17},{17,1},{2,18},{18,2},{3,19},{19,3},{4,20},{20... | collective-permute-start | bytes 1474568 | tf_op jit(solution)/shard_map/ppermute | solution.py:528
  49.3 32.0 %all-to-all-start.1 = ((bf16[32,16,128]{2,1,0:T(8,128)(2,1)}), bf16[32,16,128]{2,1,0:T(8,128)(2,1)S(1)}, u32[]{:S(2)}, u32[]{:S(2)}) async-start(bf16[32,16,128]{2,1,0:T(8,128)(2,1)} %copy-done.106), calls=%async_computation.1 | async-start | bytes 262144 | tf_op jit(solution)/shard_map/all_to_all | solution.py:1525
  52.4 94.5 %all-gather.5.cloned.1.call-start = ((), (), s32[]{:S(2)}) async-start(), calls=%async_computation.14 | async-start | bytes 1966080 | tf_op jit(solution)/shard_map/all_gather | solution.py:1558
  97.1 23.3 %collective-permute-start.17 = (bf16[2,4,128,384]{3,2,1,0:T(8,128)(2,1)}, bf16[2,4,128,384]{3,2,1,0:T(8,128)(2,1)}, u32[]{:S(2)}, u32[]{:S(2)}) collective-permute-start(bf16[2,4,128,384]{3,2,1,0:T(8,128)(2,1)} %get-tuple-element.223), channel_id=1, source_target_pairs={{0,16},{16,0},{1,17},{17,1},{2,18},{18,2},{3,19},{19,3},{4,20},{20... | collective-permute-start | bytes 2359304 | tf_op jit(solution)/shard_map/ppermute | solution.py:528
  98.3 48.6 %all-to-all-start.2 = ((bf16[8,48,1024]{2,1,0:T(8,128)(2,1)}), bf16[8,48,1024]{2,1,0:T(8,128)(2,1)}, u32[]{:S(2)}, u32[]{:S(2)}) async-start(bf16[8,48,1024]{2,1,0:T(8,128)(2,1)} %copy-done.53), calls=%async_computation.2 | async-start | bytes 1572864 | tf_op jit(solution)/shard_map/all_to_all | solution.py:1559
  103.1 135.6 %all-gather.7.cloned.1.call-start = ((), (), s32[]{:S(2)}) async-start(), calls=%async_computation.15 | async-start | bytes 3932160 | tf_op jit(solution)/shard_map/all_gather | solution.py:1619
  121.7 22.6 %collective-permute-start.18 = (bf16[4,128,384]{2,1,0:T(8,128)(2,1)S(1)}, bf16[4,128,384]{2,1,0:T(8,128)(2,1)S(1)}, u32[]{:S(2)}, u32[]{:S(2)}) collective-permute-start(bf16[4,128,384]{2,1,0:T(8,128)(2,1)S(1)} %get-tuple-element.225), channel_id=1, source_target_pairs={{0,1},{1,0},{2,3},{3,2},{4,5},{5,4},{6,7},{7,6},{8,9},{9,8},{10,11... | collective-permute-start | bytes 1179656 | tf_op jit(solution)/shard_map/ppermute | solution.py:528
  123.6 23.3 %collective-permute-start.13 = (bf16[96,1536]{1,0:T(8,128)(2,1)S(1)}, bf16[96,1536]{1,0:T(8,128)(2,1)S(1)}, u32[]{:S(2)}, u32[]{:S(2)}) collective-permute-start(bf16[96,1536]{1,0:T(8,128)(2,1)S(1)} %shard_map.261.refs_2_.refs_0_), channel_id=1, source_target_pairs={{0,4},{2,6},{4,0},{6,2},{1,5},{3,7},{5,1},{7,3},{8,12},{10,14},{12... | collective-permute-start | bytes 884744 | tf_op jit(solution)/shard_map/ppermute | solution.py:537
  128.4 16.0 %collective-permute-start.15 = (f32[8,1024]{1,0:T(8,128)S(1)}, f32[8,1024]{1,0:T(8,128)S(1)}, u32[]{:S(2)}, u32[]{:S(2)}) collective-permute-start(f32[8,1024]{1,0:T(8,128)S(1)} %add.120.refs_2_.refs_1_), channel_id=1, source_target_pairs={{4,0},{6,2},{0,4},{2,6},{5,1},{7,3},{1,5},{3,7},{12,8},{14,10},{8,... | collective-permute-start | bytes 98312 | tf_op jit(solution)/shard_map/ppermute | solution.py:533
  147.0 17.6 %collective-permute-start.19 = (bf16[192,1536]{1,0:T(8,128)(2,1)S(1)}, bf16[192,1536]{1,0:T(8,128)(2,1)S(1)}, u32[]{:S(2)}, u32[]{:S(2)}) collective-permute-start(bf16[192,1536]{1,0:T(8,128)(2,1)S(1)} %shard_map.264.refs_8_.refs_0_), channel_id=1, source_target_pairs={{0,1},{1,0},{2,3},{3,2},{4,5},{5,4},{6,7},{7,6},{8,9},{9,8},{10,11... | collective-permute-start | bytes 1769480 | tf_op jit(solution)/shard_map/ppermute | solution.py:528
  167.4 26.0 %collective-permute-start.27 = (bf16[384,1536]{1,0:T(8,128)(2,1)S(1)}, bf16[384,1536]{1,0:T(8,128)(2,1)}, u32[]{:S(2)}, u32[]{:S(2)}) collective-permute-start(bf16[384,1536]{1,0:T(8,128)(2,1)S(1)} %shard_map.266.refs_4_.refs_1_), channel_id=1, source_target_pairs={{0,16},{16,0},{1,17},{17,1},{2,18},{18,2},{3,19},{19,3},{4,20},{20... | collective-permute-start | bytes 3538952 | tf_op jit(solution)/shard_map/ppermute | solution.py:528
  196.0 26.2 %all-to-all-start.3 = ((bf16[8,192,128]{2,1,0:T(8,128)(2,1)}), bf16[8,192,128]{2,1,0:T(8,128)(2,1)S(1)}, u32[]{:S(2)}, u32[]{:S(2)}) async-start(bf16[8,192,128]{2,1,0:T(8,128)(2,1)} %get-tuple-element.256), calls=%async_computation.3 | async-start | bytes 786432 | tf_op jit(solution)/shard_map/all_to_all | solution.py:1648
  199.8 175.9 %reduce-scatter.4.cloned.1.call-start = ((), (), s32[]{:S(2)}) async-start(), calls=%async_computation.16 | async-start | bytes 1966080 | tf_op jit(solution)/shard_map/reduce_scatter | solution.py:1728
  326.7 30.7 %collective-permute-start.49 = (bf16[4,384,1024]{2,1,0:T(8,128)(2,1)}, bf16[4,384,1024]{2,1,0:T(8,128)(2,1)}, u32[]{:S(2)}, u32[]{:S(2)}) collective-permute-start(bf16[4,384,1024]{2,1,0:T(8,128)(2,1)} %get-tuple-element.303), channel_id=1, source_target_pairs={{0,8},{8,0},{1,9},{9,1},{2,10},{10,2},{3,11},{11,3},{4,12},{12,4},... | collective-permute-start | bytes 9437192 | tf_op jit(solution)/shard_map/ppermute | solution.py:528
  351.4 24.4 %all-to-all-start.4 = ((bf16[8,192,128]{2,1,0:T(8,128)(2,1)}), bf16[8,192,128]{2,1,0:T(8,128)(2,1)S(1)}, u32[]{:S(2)}, u32[]{:S(2)}) async-start(bf16[8,192,128]{2,1,0:T(8,128)(2,1)} %bitcast.25), calls=%async_computation.4 | async-start | bytes 786432 | tf_op jit(solution)/shard_map/all_to_all | solution.py:1741
  354.8 86.4 %reduce-scatter.6.cloned.1.call-start = ((), (), s32[]{:S(2)}) async-start(), calls=%async_computation.17 | async-start | bytes 3932160 | tf_op jit(solution)/shard_map/reduce_scatter | solution.py:1749
  375.8 26.9 %collective-permute-start.50 = (bf16[128,1536]{1,0:T(8,128)(2,1)}, bf16[128,1536]{1,0:T(8,128)(2,1)}, u32[]{:S(2)}, u32[]{:S(2)}) collective-permute-start(bf16[128,1536]{1,0:T(8,128)(2,1)} %collective-permute-done.48.refs_4_), channel_id=1, source_target_pairs={{0,1},{1,0},{2,3},{3,2},{4,5},{5,4},{6,7},{7,6},{8,9},{9,8},{10,11... | collective-permute-start | bytes 1179656 | tf_op jit(solution)/shard_map/ppermute | solution.py:528
  377.1 25.6 %all-to-all-start.5 = ((bf16[8,192,128]{2,1,0:T(8,128)(2,1)}), bf16[8,192,128]{2,1,0:T(8,128)(2,1)S(1)}, u32[]{:S(2)}, u32[]{:S(2)}) async-start(bf16[8,192,128]{2,1,0:T(8,128)(2,1)} %get-tuple-element.318), calls=%async_computation.6 | async-start | bytes 786432 | tf_op jit(solution)/shard_map/all_to_all | solution.py:1750
  402.7 18.8 %all-to-all-start.6 = ((f32[8,8,1024]{2,1,0:T(8,128)}), f32[8,8,1024]{2,1,0:T(8,128)S(1)}, u32[]{:S(2)}, u32[]{:S(2)}) async-start(f32[8,8,1024]{2,1,0:T(8,128)} %get-tuple-element.321), calls=%async_computation.7 | async-start | bytes 524288 | tf_op jit(solution)/shard_map/all_to_all | solution.py:546
  441.2 31.3 %all-to-all-start.7 = ((bf16[8,48,1024]{2,1,0:T(8,128)(2,1)}), bf16[8,48,1024]{2,1,0:T(8,128)(2,1)S(1)}, u32[]{:S(2)}, u32[]{:S(2)}) async-start(bf16[8,48,1024]{2,1,0:T(8,128)(2,1)} %bitcast.57), calls=%async_computation.9 | async-start | bytes 1572864 | tf_op jit(solution)/shard_map/all_to_all | solution.py:1837
  445.7 121.8 %reduce-scatter.8.cloned.1.call-start = ((), (), s32[]{:S(2)}) async-start(), calls=%async_computation.18 | async-start | bytes 3538944 | tf_op jit(solution)/shard_map/reduce_scatter | solution.py:1874
  445.7 23.2 %collective-permute-start.55 = (bf16[80,1536]{1,0:T(8,128)(2,1)}, bf16[80,1536]{1,0:T(8,128)(2,1)S(1)}, u32[]{:S(2)}, u32[]{:S(2)}) collective-permute-start(bf16[80,1536]{1,0:T(8,128)(2,1)} %copy-done.131), channel_id=1, source_target_pairs={{2,0},{4,2},{6,4},{0,6},{3,1},{5,3},{7,5},{1,7},{10,8},{12,10},{14... | collective-permute-start | bytes 737288 | tf_op jit(solution)/shard_map/ppermute | solution.py:533
  447.9 23.2 %collective-permute-start.56 = (bf16[80,1536]{1,0:T(8,128)(2,1)}, bf16[80,1536]{1,0:T(8,128)(2,1)S(1)}, u32[]{:S(2)}, u32[]{:S(2)}) collective-permute-start(bf16[80,1536]{1,0:T(8,128)(2,1)} %copy-done.130), channel_id=1, source_target_pairs={{4,0},{6,2},{0,4},{2,6},{5,1},{7,3},{1,5},{3,7},{12,8},{14,10},{8,... | collective-permute-start | bytes 737288 | tf_op jit(solution)/shard_map/ppermute | solution.py:533
  449.1 22.7 %collective-permute-start.57 = (bf16[80,1536]{1,0:T(8,128)(2,1)}, bf16[80,1536]{1,0:T(8,128)(2,1)S(1)}, u32[]{:S(2)}, u32[]{:S(2)}) collective-permute-start(bf16[80,1536]{1,0:T(8,128)(2,1)} %copy-done.129), channel_id=1, source_target_pairs={{6,0},{0,2},{2,4},{4,6},{7,1},{1,3},{3,5},{5,7},{14,8},{8,10},{10,... | collective-permute-start | bytes 737288 | tf_op jit(solution)/shard_map/ppermute | solution.py:533
  485.9 25.8 %all-to-all-start.8 = ((f32[8,8,1536]{2,1,0:T(8,128)}), f32[8,8,1536]{2,1,0:T(8,128)}, u32[]{:S(2)}, u32[]{:S(2)}) async-start(f32[8,8,1536]{2,1,0:T(8,128)} %get-tuple-element.365.refs_4_), calls=%async_computation.11 | async-start | bytes 786432 | tf_op jit(solution)/shard_map/all_to_all | solution.py:546
  493.7 28.0 %collective-permute-start.63 = (bf16[1024,384]{1,0:T(8,128)(2,1)S(1)}, bf16[1024,384]{1,0:T(8,128)(2,1)}, u32[]{:S(2)}, u32[]{:S(2)}) collective-permute-start(bf16[1024,384]{1,0:T(8,128)(2,1)S(1)} %shard_map.288.refs_1_.refs_2_), channel_id=1, source_target_pairs={{0,8},{8,0},{1,9},{9,1},{2,10},{10,2},{3,11},{11,3},{4,12},{12,4},... | collective-permute-start | bytes 2359304 | tf_op jit(solution)/shard_map/ppermute | solution.py:528
  499.1 22.7 %collective-permute-start.64 = (bf16[1024,384]{1,0:T(8,128)(2,1)S(1)}, bf16[1024,384]{1,0:T(8,128)(2,1)}, u32[]{:S(2)}, u32[]{:S(2)}) collective-permute-start(bf16[1024,384]{1,0:T(8,128)(2,1)S(1)} %shard_map.288.refs_1_.refs_2_), channel_id=1, source_target_pairs={{0,16},{16,0},{1,17},{17,1},{2,18},{18,2},{3,19},{19,3},{4,20},{20... | collective-permute-start | bytes 2359304 | tf_op jit(solution)/shard_map/ppermute | solution.py:528
  517.8 18.1 %all-to-all-start.9 = ((bf16[8,48,640]{2,1,0:T(8,128)(2,1)}), bf16[8,48,640]{2,1,0:T(8,128)(2,1)S(1)}, u32[]{:S(2)}, u32[]{:S(2)}) async-start(bf16[8,48,640]{2,1,0:T(8,128)(2,1)} %bitcast.28), calls=%async_computation.12 | async-start | bytes 983040 | tf_op jit(solution)/shard_map/all_to_all | solution.py:1893
  535.9 26.3 %all-to-all-start.10 = ((f32[32,24,128]{2,1,0:T(8,128)}), f32[32,24,128]{2,1,0:T(8,128)S(1)}, u32[]{:S(2)}, u32[]{:S(2)}) async-start(f32[32,24,128]{2,1,0:T(8,128)} %get-tuple-element.375.refs_1_), calls=%async_computation.13 | async-start | bytes 786432 | tf_op jit(solution)/shard_map/all_to_all | solution.py:1926
  (196 other events, 1858.7 us)
Sparse Core Ops, SparseCore 0:
  10.2 80.4 all-gather.8
  92.2 39.3 all-gather.4
  165.6 73.0 all-gather.6
  336.0 38.5 reduce-scatter.3
  376.8 64.4 reduce-scatter.5
  472.7 94.7 reduce-scatter.7
